TPU v7x, 32 devices: a whole 2x2x4 slice. The times are simulated.
32 devices in a mesh: dp: 4 (over y, core), expert: 8 (over z, x).
Axes of the slice: x: 2, y: 2, z: 4, core: 2. Of those that a mesh axis runs over, the one named last changes fastest.
Arguments:
- tokens: bfloat16 [64, 1024, 384], P(('dp', 'expert')), may hold values from -12 to 12
- image_ids: int32 [64, 1024], P(('dp', 'expert')), may hold values from 0 to 5, never falling along the last dimension, each value on 1 to 576 neighbouring positions
- slot_image: int32 [64, 16], P(('dp', 'expert')), may hold values from 0 to 5, as said below
- ln1_gain: float32 [384], replicated, may hold values from 0.5 to 1.5
- ln1_bias: float32 [384], replicated, may hold values from -4 to 4
- qkv_weight: bfloat16 [384, 1152], replicated, may hold values from -0.3125 to 0.3125
- query_bias: float32 [384], replicated, may hold values from -4 to 4
- value_bias: float32 [384], replicated, may hold values from -4 to 4
- out_weight: bfloat16 [384, 384], replicated, may hold values from -0.875 to 0.875
- out_bias: float32 [384], replicated, may hold values from -4 to 4
- ln2_gain: float32 [384], replicated, may hold values from 0.5 to 1.5
- ln2_bias: float32 [384], replicated, may hold values from -0.3125 to 0.3125
- slot_params: bfloat16 [384, 16], P(None, 'expert'), may hold values from -0.15625 to 0.15625
- up_weight: bfloat16 [16, 1536, 384], P('expert', 'dp'), may hold values from -3 to 3
- up_bias: bfloat16 [16, 1536], P('expert', 'dp'), may hold values from -1.5 to 1.5
- down_weight: bfloat16 [16, 1536, 384], P('expert', 'dp'), may hold values from -0.625 to 0.625
- down_bias: float32 [16, 384], P('expert'), may hold values from -6 to 6
- cotangent: bfloat16 [64, 1024, 384], P(('dp', 'expert')), may hold values from -6 to 6
Outputs:
- output: bfloat16 [64, 1024, 384], P(('dp', 'expert'))
- input_grad: bfloat16 [64, 1024, 384], P(('dp', 'expert'))
- ln1_gain_grad: float32 [384], replicated
- ln1_bias_grad: float32 [384], replicated
- qkv_weight_grad: float32 [384, 1152], replicated
- query_bias_grad: float32 [384], replicated
- value_bias_grad: float32 [384], replicated
- out_weight_grad: float32 [384, 384], replicated
- out_bias_grad: float32 [384], replicated
- ln2_gain_grad: float32 [384], replicated
- ln2_bias_grad: float32 [384], replicated
- slot_params_grad: float32 [384, 16], P(None, 'expert')
- up_weight_grad: float32 [16, 1536, 384], P('expert', 'dp')
- up_bias_grad: float32 [16, 1536], P('expert', 'dp')
- down_weight_grad: float32 [16, 1536, 384], P('expert', 'dp')
- down_bias_grad: float32 [16, 384], P('expert')
- stream_rms: float32 [3], replicated
Inputs may be any that keep to these rules, and one draw needn't show every extreme that they name: `image_ids`: within each row the image numbers never fall and every number 0 to 5 occurs; the largest image of a row has 576 patches. `slot_image`: every image number of a row is named by at least one slot of that row.
All inputs are finite; a program needn't handle non-finite values.
Results may differ from a plain program's by a relative error of at most 0.024.
Values may be sent and summed in bfloat16 or wider, within the bound.
No kernel may reach another device: no remote copies, remote signals or barrier semaphores. Data moves between devices by JAX's collectives and lax.ppermute only.
A program may use at most 192 MiB of HBM per device.

v0:
```python
import jax
import jax.numpy as jnp
from jax import lax
from jax.sharding import PartitionSpec as P

HEADS = 6


epsilon = 1e-06
masked_out = -1e30


def norm_fwd(values, gain, shift):
    centre = values - jnp.mean(values, axis=-1, keepdims=True)
    recip = lax.rsqrt(jnp.mean(centre * centre, axis=-1, keepdims=True) + epsilon)
    normed = centre * recip
    return (normed * gain + shift, normed, recip)


def norm_back(grad_out, normed, recip, gain):
    gain_grad = jnp.sum(grad_out * normed, axis=0)
    shift_grad = jnp.sum(grad_out, axis=0)
    scaled = grad_out * gain
    inner = (
        scaled
        - jnp.mean(scaled, axis=-1, keepdims=True)
        - normed * jnp.mean(scaled * normed, axis=-1, keepdims=True)
    )
    return (recip * inner, gain_grad, shift_grad)


def soft_select(scores, allowed, axis):
    scores = jnp.where(allowed, scores, masked_out)
    row_top = jnp.max(scores, axis=axis, keepdims=True)
    exp_scores = jnp.where(allowed, jnp.exp(scores - row_top), 0.0)
    return exp_scores / jnp.sum(exp_scores, axis=axis, keepdims=True)


def gelu_parts(pre_act):
    normal_cdf = 0.5 * (1.0 + lax.erf(pre_act * 0.7071067811865476))
    density = jnp.exp(-0.5 * pre_act * pre_act) * 0.3989422804014327
    return (pre_act * normal_cdf, normal_cdf + pre_act * density)


def local(
    tokens,
    image_ids,
    slot_image,
    ln1_gain,
    ln1_bias,
    qkv_weight,
    query_bias,
    value_bias,
    out_weight,
    out_bias,
    ln2_gain,
    ln2_bias,
    slot_params,
    up_weight,
    up_bias,
    down_weight,
    down_bias,
    cotangent,
):
    seq_dev, seq_len, model_width = tokens.shape
    head_count = HEADS
    head_dim = model_width // head_count
    score_scale = head_dim ** (-0.5)
    block_rows = min(512, seq_len)
    per_seq = seq_len // block_rows
    n_blocks = seq_dev * per_seq
    flat_rows = seq_dev * seq_len
    bf16 = jnp.bfloat16
    f32 = jnp.float32
    stream = tokens.reshape(flat_rows, model_width).astype(f32)
    normed_one, hat_one, recip_one = norm_fwd(stream, ln1_gain, ln1_bias)
    low_one = normed_one.astype(bf16)
    projected = jnp.dot(low_one, qkv_weight, preferred_element_type=f32)
    query_low = (projected[:, :model_width] + query_bias).astype(bf16)
    key_low = projected[:, model_width : 2 * model_width].astype(bf16)
    value_low = (projected[:, 2 * model_width :] + value_bias).astype(bf16)
    query_blocks = query_low.reshape(n_blocks, block_rows, head_count, head_dim)
    key_seq = key_low.reshape(seq_dev, seq_len, head_count, head_dim)
    value_seq = value_low.reshape(seq_dev, seq_len, head_count, head_dim)
    id_blocks = image_ids.reshape(n_blocks, block_rows)
    owner_list = jnp.arange(n_blocks, dtype=jnp.int32) // per_seq

    def block_scores(query_part, id_part, owner_index):
        key_part = lax.dynamic_index_in_dim(key_seq, owner_index, 0, keepdims=False)
        value_part = lax.dynamic_index_in_dim(value_seq, owner_index, 0, keepdims=False)
        id_keys = lax.dynamic_index_in_dim(image_ids, owner_index, 0, keepdims=False)
        raw_scores = (
            jnp.einsum("qhd,khd->hqk", query_part, key_part, preferred_element_type=f32)
            * score_scale
        )
        allowed = (id_part[:, None] == id_keys[None, :])[None]
        return (jnp.where(allowed, raw_scores, masked_out), allowed, key_part, value_part)

    def attend_block(inputs):
        query_part, id_part, owner_index = inputs
        scores, allowed, key_part, value_part = block_scores(query_part, id_part, owner_index)
        row_top = jnp.max(scores, axis=-1, keepdims=True)
        exp_scores = jnp.where(allowed, jnp.exp(scores - row_top), 0.0)
        total = jnp.sum(exp_scores, axis=-1, keepdims=True)
        attn_low = (exp_scores / total).astype(bf16)
        mixed_part = jnp.einsum("hqk,khd->qhd", attn_low, value_part, preferred_element_type=f32)
        return (mixed_part, row_top + jnp.log(total))

    mixed_heads, log_totals = lax.map(attend_block, (query_blocks, id_blocks, owner_list))
    mixed_low = mixed_heads.reshape(flat_rows, model_width).astype(bf16)
    branch = jnp.dot(mixed_low, out_weight, preferred_element_type=f32) + out_bias
    residual = stream + branch
    normed_two, hat_two, recip_two = norm_fwd(residual, ln2_gain, ln2_bias)
    low_two = normed_two.astype(bf16)
    low_two_seq = low_two.reshape(seq_dev, seq_len, model_width)
    phi_all = lax.all_gather(slot_params, "expert", axis=1, tiled=True)
    slot_count = phi_all.shape[1]
    logits = jnp.dot(low_two, phi_all, preferred_element_type=f32).reshape(
        seq_dev, seq_len, slot_count
    )
    allowed_slots = image_ids[:, :, None] == slot_image[:, None, :]
    dispatch = soft_select(logits, allowed_slots, 1)
    combine = soft_select(logits, allowed_slots, 2)
    dispatch_low = dispatch.astype(bf16)
    combine_low = combine.astype(bf16)
    slot_in = jnp.einsum(
        "stk,std->skd", dispatch_low, low_two_seq, preferred_element_type=f32
    ).astype(bf16)
    arrived = lax.all_to_all(slot_in, "expert", split_axis=1, concat_axis=0, tiled=True)
    expert_rows = lax.all_gather(arrived, "dp", axis=0, tiled=True)
    pre_act = (
        jnp.einsum("sed,ehd->seh", expert_rows, up_weight, preferred_element_type=f32)
        + up_bias[None]
    )
    hidden_f, slope = gelu_parts(pre_act)
    hidden_low = hidden_f.astype(bf16)
    partial_out = jnp.einsum("seh,ehd->sed", hidden_low, down_weight, preferred_element_type=f32)
    expert_out = (
        lax.psum_scatter(
            partial_out.astype(jnp.bfloat16), "dp", scatter_dimension=0, tiled=True
        ).astype(jnp.float32)
        + down_bias[None]
    )
    out_low = expert_out.astype(bf16)
    returned = lax.all_to_all(out_low, "expert", split_axis=0, concat_axis=1, tiled=True)
    moe_out = jnp.einsum("stk,skd->std", combine_low, returned, preferred_element_type=f32).reshape(
        flat_rows, model_width
    )
    result = (residual + moe_out).astype(bf16).reshape(seq_dev, seq_len, model_width)
    squares = jnp.stack(
        [jnp.sum(stream * stream), jnp.sum(branch * branch), jnp.sum(moe_out * moe_out)]
    )
    out_grad = jnp.einsum(
        "stk,std->skd", combine_low, cotangent, preferred_element_type=f32
    ).astype(bf16)
    combine_grad = jnp.einsum("std,skd->stk", cotangent, returned, preferred_element_type=f32)
    logit_grad = combine * (combine_grad - jnp.sum(combine * combine_grad, axis=2, keepdims=True))
    came_back = lax.all_to_all(out_grad, "expert", split_axis=1, concat_axis=0, tiled=True)
    grad_rows = lax.all_gather(came_back, "dp", axis=0, tiled=True)
    down_bias_grad = jnp.sum(grad_rows.astype(f32), axis=0)
    hidden_grad = jnp.einsum("sed,ehd->seh", grad_rows, down_weight, preferred_element_type=f32)
    pre_grad = (hidden_grad * slope).astype(bf16)
    down_weight_grad = jnp.einsum("seh,sed->ehd", hidden_low, grad_rows, preferred_element_type=f32)
    up_weight_grad = jnp.einsum("seh,sed->ehd", pre_grad, expert_rows, preferred_element_type=f32)
    up_bias_grad = jnp.sum(pre_grad.astype(f32), axis=0)
    slot_partial = jnp.einsum("seh,ehd->sed", pre_grad, up_weight, preferred_element_type=f32)
    slot_grad = (
        lax.psum_scatter(slot_partial.astype(jnp.bfloat16), "dp", scatter_dimension=0, tiled=True)
        .astype(jnp.float32)
        .astype(bf16)
    )
    slot_back = lax.all_to_all(slot_grad, "expert", split_axis=0, concat_axis=1, tiled=True)
    dispatch_grad = jnp.einsum("std,skd->stk", low_two_seq, slot_back, preferred_element_type=f32)
    logit_grad = logit_grad + dispatch * (
        dispatch_grad - jnp.sum(dispatch * dispatch_grad, axis=1, keepdims=True)
    )
    logit_low = logit_grad.astype(bf16).reshape(flat_rows, slot_count)
    normed_two_grad = jnp.einsum(
        "stk,skd->std", dispatch_low, slot_back, preferred_element_type=f32
    ).reshape(flat_rows, model_width)
    normed_two_grad = normed_two_grad + lax.dot_general(
        logit_low, phi_all, (((1,), (1,)), ((), ())), preferred_element_type=f32
    )
    phi_grad = lax.dot_general(
        low_two, logit_low, (((0,), (0,)), ((), ())), preferred_element_type=f32
    )
    resid_part, ln2_gain_grad, ln2_bias_grad = norm_back(
        normed_two_grad, hat_two, recip_two, ln2_gain
    )
    residual_grad = cotangent.reshape(flat_rows, model_width).astype(f32) + resid_part
    branch_low = residual_grad.astype(bf16)
    out_bias_grad = jnp.sum(branch_low.astype(f32), axis=0)
    out_weight_grad = lax.dot_general(
        mixed_low, branch_low, (((0,), (0,)), ((), ())), preferred_element_type=f32
    )
    mixed_grad = lax.dot_general(
        branch_low, out_weight, (((1,), (1,)), ((), ())), preferred_element_type=f32
    ).astype(bf16)
    grad_blocks = mixed_grad.reshape(n_blocks, block_rows, head_count, head_dim)

    def attend_back(carry, inputs):
        key_acc, value_acc = carry
        query_part, id_part, owner_index, grad_part, log_part = inputs
        scores, allowed, key_part, value_part = block_scores(query_part, id_part, owner_index)
        attn_full = jnp.where(allowed, jnp.exp(scores - log_part), 0.0)
        prob_grad = jnp.einsum("qhd,khd->hqk", grad_part, value_part, preferred_element_type=f32)
        row_dot = jnp.sum(attn_full * prob_grad, axis=-1, keepdims=True)
        score_low = (attn_full * (prob_grad - row_dot) * score_scale).astype(bf16)
        query_grad = jnp.einsum("hqk,khd->qhd", score_low, key_part, preferred_element_type=f32)
        key_add = jnp.einsum("hqk,qhd->khd", score_low, query_part, preferred_element_type=f32)
        value_add = jnp.einsum(
            "hqk,qhd->khd", attn_full.astype(bf16), grad_part, preferred_element_type=f32
        )
        key_now = lax.dynamic_index_in_dim(key_acc, owner_index, 0, keepdims=False)
        value_now = lax.dynamic_index_in_dim(value_acc, owner_index, 0, keepdims=False)
        key_acc = lax.dynamic_update_index_in_dim(key_acc, key_now + key_add, owner_index, 0)
        value_acc = lax.dynamic_update_index_in_dim(
            value_acc, value_now + value_add, owner_index, 0
        )
        return ((key_acc, value_acc), query_grad)

    zero_heads = jnp.zeros((seq_dev, seq_len, head_count, head_dim), f32)
    (key_total, value_total), query_grads = lax.scan(
        attend_back,
        (zero_heads, zero_heads),
        (query_blocks, id_blocks, owner_list, grad_blocks, log_totals),
    )
    query_grad_low = query_grads.reshape(flat_rows, model_width).astype(bf16)
    key_grad_low = key_total.reshape(flat_rows, model_width).astype(bf16)
    value_grad_low = value_total.reshape(flat_rows, model_width).astype(bf16)
    query_bias_grad = jnp.sum(query_grad_low.astype(f32), axis=0)
    value_bias_grad = jnp.sum(value_grad_low.astype(f32), axis=0)
    qkv_grad = jnp.concatenate([query_grad_low, key_grad_low, value_grad_low], axis=1)
    qkv_weight_grad = lax.dot_general(
        low_one, qkv_grad, (((0,), (0,)), ((), ())), preferred_element_type=f32
    )
    normed_one_grad = lax.dot_general(
        qkv_grad, qkv_weight, (((1,), (1,)), ((), ())), preferred_element_type=f32
    )
    input_part, ln1_gain_grad, ln1_bias_grad = norm_back(
        normed_one_grad, hat_one, recip_one, ln1_gain
    )
    input_grad = (residual_grad + input_part).astype(bf16).reshape(seq_dev, seq_len, model_width)
    (
        ln1_gain_grad,
        ln1_bias_grad,
        qkv_weight_grad,
        query_bias_grad,
        value_bias_grad,
        out_weight_grad,
        out_bias_grad,
        ln2_gain_grad,
        ln2_bias_grad,
        phi_grad,
        squares,
    ) = lax.psum(
        (
            ln1_gain_grad,
            ln1_bias_grad,
            qkv_weight_grad,
            query_bias_grad,
            value_bias_grad,
            out_weight_grad,
            out_bias_grad,
            ln2_gain_grad,
            ln2_bias_grad,
            phi_grad,
            squares,
        ),
        ("dp", "expert"),
    )
    own_slots = slot_params.shape[1]
    column_start = lax.axis_index("expert") * own_slots
    slot_params_grad = lax.dynamic_slice_in_dim(phi_grad, column_start, own_slots, 1)
    total_count = lax.axis_size("dp") * lax.axis_size("expert") * flat_rows * model_width
    stream_rms = jnp.sqrt(squares / total_count)
    return (
        result,
        input_grad,
        ln1_gain_grad,
        ln1_bias_grad,
        qkv_weight_grad,
        query_bias_grad,
        value_bias_grad,
        out_weight_grad,
        out_bias_grad,
        ln2_gain_grad,
        ln2_bias_grad,
        slot_params_grad,
        up_weight_grad,
        up_bias_grad,
        down_weight_grad,
        down_bias_grad,
        stream_rms,
    )


def solution(mesh):
    return jax.shard_map(
        local,
        mesh=mesh,
        in_specs=(
            P(("dp", "expert"), None, None),
            P(("dp", "expert"), None),
            P(("dp", "expert"), None),
            P(),
            P(),
            P(),
            P(),
            P(),
            P(),
            P(),
            P(),
            P(),
            P(None, "expert"),
            P("expert", "dp", None),
            P("expert", "dp"),
            P("expert", "dp", None),
            P("expert", None),
            P(("dp", "expert"), None, None),
        ),
        out_specs=(
            P(("dp", "expert"), None, None),
            P(("dp", "expert"), None, None),
            P(),
            P(),
            P(),
            P(),
            P(),
            P(),
            P(),
            P(),
            P(),
            P(None, "expert"),
            P("expert", "dp", None),
            P("expert", "dp"),
            P("expert", "dp", None),
            P("expert", None),
            P(),
        ),
        check_vma=False,
    )
```

profile of v0, /device:TPU:0, one launch (start us, length us, event | category | flops | bytes accessed | tf_op | source)
XLA Modules:
  0.0 734.3 jit_solution(1446103441335150052)
XLA Ops:
  15.2 27.7 %all-gather = bf16[8,2,384]{2,1,0:T(2,128)(2,1)S(1)} all-gather(bf16[1,2,384]{2,1,0:T(2,128)(2,1)S(1)} %bitcast.358), channel_id=1, replica_groups=mesh['dp'=4,'expert'=8] {'expert'}, dimensions={0}, use_global_device_ids=true | all-gather | bytes 13824 | tf_op jit(solution)/shard_map/all_gather | solution.py:116
  81.2 66.3 %while.26 = (s32[]{:T(128)}, bf16[4,512,6,64]{1,3,2,0:T(8,128)(2,1)}, f32[4,6,512,1]{2,1,3,0:T(8,128)}, s32[4]{0:T(128)S(1)}, bf16[2,1024,6,64]{1,3,2,0:T(8,128)...) while((s32[]{:T(128)}, ...), condition=%wide.region_5.6_spmd, body=%wide.region_2.5_spmd.sunk | while | flops 849867776 | bytes 61602076 | solution.py:109
  88.0 4.4 fusion.189
  104.5 4.4 fusion.189
  163.6 4.7 all-to-all-done.2
  172.2 5.3 all_gather.11
  178.3 5.3 all_gather.10
  194.7 16.2 %reduce-scatter.3.cloned.1.call-done = bf16[16,2,384]{2,0,1:T(8,128)(2,1)} async-done(((bf16[64,2,384]{2,0,1:T(8,128)(2,1)}), bf16[16,2,384]{2,0,1:T(8,128)(2,1)}) %reduce-scatter.3.cloned.1.call-update) | async-done | bytes 24592 | tf_op jit(solution)/shard_map/reduce_scatter | solution.py:139
  212.3 5.5 all-to-all-start.1
  218.4 14.5 %reduce-scatter.5.cloned.1.call-done = bf16[16,2,384]{2,0,1:T(8,128)(2,1)} async-done(((bf16[64,2,384]{2,0,1:T(8,128)(2,1)}), bf16[16,2,384]{2,0,1:T(8,128)(2,1)}) %reduce-scatter.5.cloned.1.call-update) | async-done | bytes 24592 | tf_op jit(solution)/shard_map/reduce_scatter | solution.py:168
  234.3 5.5 all-to-all-start.3
  251.2 4.6 multiply_reduce_fusion.3
  276.5 245.1 %while.27 = (s32[]{:T(128)}, f32[2,1024,6,64]{1,3,2,0:T(8,128)}, f32[2,1024,6,64]{1,3,2,0:T(8,128)}, bf16[4,512,6,64]{1,3,2,0:T(8,128)(2,1)}, s32[4]{0:T(128)S(1...) while((s32[]{:T(128)}, f32[2,1024,6,64]{1,3,2,0:T(8,128)}, ...), condition=%wide.region_20.21_spmd, body=%wide.region_18.20_spmd.sunk | while | flops 2061770752 | bytes 251193776 | solution.py:223
  282.7 4.9 exponential_select_fusion.3
  294.1 6.3 fusion.201
  300.4 18.0 %fusion.202 = bf16[4,512,6,64]{1,3,2,0:T(8,128)(2,1)} fusion(bf16[4,512,6,64]{1,3,2,0:T(8,128)(2,1)} %get-tuple-element.479, s32[]{:T(128)S(6)} %copy.169, f32[6,512,1024]{2,1,0:T(8,128)} %copy-done.1, f32[6,512,1024]{2,1,0:T(8,128)} %fusion.201, bf16[2,1024,6,64]{1,3,2,0:T(8,128)(2,1)} %get-tuple-element.499, s32[]{:T(128)S(6)} %select_n.176), kind=kOutput, calls=%fused_computation.38.clone.1 | convolution fusion | flops 418385920 | bytes 51904520 | tf_op jit(solution)/shard_map/while/body/eval_jaxpr/hqk,khd->qhd/dot_general | solution.py:209
  318.4 19.5 %bitcast_dynamic-update-slice_fusion.7 = f32[2,1024,6,64]{1,3,2,0:T(8,128)} fusion(f32[2,1024,6,64]{1,3,2,0:T(8,128)} %get-tuple-element.477, s32[]{:T(128)S(6)} %select_n.176, f32[1,1024,6,64]{1,3,2,0:T(8,128)S(1)} %get-tuple-element.423, f32[6,512,1024]{2,1,0:T(8,128)} %copy-done.1, f32[6,512,1024]{2,1,0:T(8,128)} %fusion.201, ...), kind=kOutput, calls=%fused_computation.35.clone.1 | convolution fusion | flops 418779136 | bytes 53870600 | tf_op jit(solution)/shard_map/while/body/eval_jaxpr/hqk,qhd->khd/dot_general | solution.py:210
  343.9 4.9 exponential_select_fusion.3
  355.3 6.3 fusion.201
  361.6 18.0 %fusion.202 = bf16[4,512,6,64]{1,3,2,0:T(8,128)(2,1)} fusion(bf16[4,512,6,64]{1,3,2,0:T(8,128)(2,1)} %get-tuple-element.479, s32[]{:T(128)S(6)} %copy.169, f32[6,512,1024]{2,1,0:T(8,128)} %copy-done.1, f32[6,512,1024]{2,1,0:T(8,128)} %fusion.201, bf16[2,1024,6,64]{1,3,2,0:T(8,128)(2,1)} %get-tuple-element.499, s32[]{:T(128)S(6)} %select_n.176), kind=kOutput, calls=%fused_computation.38.clone.1 | convolution fusion | flops 418385920 | bytes 51904520 | tf_op jit(solution)/shard_map/while/body/eval_jaxpr/hqk,khd->qhd/dot_general | solution.py:209
  379.6 19.6 %bitcast_dynamic-update-slice_fusion.7 = f32[2,1024,6,64]{1,3,2,0:T(8,128)} fusion(f32[2,1024,6,64]{1,3,2,0:T(8,128)} %get-tuple-element.477, s32[]{:T(128)S(6)} %select_n.176, f32[1,1024,6,64]{1,3,2,0:T(8,128)S(1)} %get-tuple-element.423, f32[6,512,1024]{2,1,0:T(8,128)} %copy-done.1, f32[6,512,1024]{2,1,0:T(8,128)} %fusion.201, ...), kind=kOutput, calls=%fused_computation.35.clone.1 | convolution fusion | flops 418779136 | bytes 53870600 | tf_op jit(solution)/shard_map/while/body/eval_jaxpr/hqk,qhd->khd/dot_general | solution.py:210
  405.1 4.9 exponential_select_fusion.3
  416.5 6.3 fusion.201
  422.8 18.0 %fusion.202 = bf16[4,512,6,64]{1,3,2,0:T(8,128)(2,1)} fusion(bf16[4,512,6,64]{1,3,2,0:T(8,128)(2,1)} %get-tuple-element.479, s32[]{:T(128)S(6)} %copy.169, f32[6,512,1024]{2,1,0:T(8,128)} %copy-done.1, f32[6,512,1024]{2,1,0:T(8,128)} %fusion.201, bf16[2,1024,6,64]{1,3,2,0:T(8,128)(2,1)} %get-tuple-element.499, s32[]{:T(128)S(6)} %select_n.176), kind=kOutput, calls=%fused_computation.38.clone.1 | convolution fusion | flops 418385920 | bytes 51904520 | tf_op jit(solution)/shard_map/while/body/eval_jaxpr/hqk,khd->qhd/dot_general | solution.py:209
  440.7 19.6 %bitcast_dynamic-update-slice_fusion.7 = f32[2,1024,6,64]{1,3,2,0:T(8,128)} fusion(f32[2,1024,6,64]{1,3,2,0:T(8,128)} %get-tuple-element.477, s32[]{:T(128)S(6)} %select_n.176, f32[1,1024,6,64]{1,3,2,0:T(8,128)S(1)} %get-tuple-element.423, f32[6,512,1024]{2,1,0:T(8,128)} %copy-done.1, f32[6,512,1024]{2,1,0:T(8,128)} %fusion.201, ...), kind=kOutput, calls=%fused_computation.35.clone.1 | convolution fusion | flops 418779136 | bytes 53870600 | tf_op jit(solution)/shard_map/while/body/eval_jaxpr/hqk,qhd->khd/dot_general | solution.py:210
  466.3 4.9 exponential_select_fusion.3
  477.7 6.3 fusion.201
  484.0 18.0 %fusion.202 = bf16[4,512,6,64]{1,3,2,0:T(8,128)(2,1)} fusion(bf16[4,512,6,64]{1,3,2,0:T(8,128)(2,1)} %get-tuple-element.479, s32[]{:T(128)S(6)} %copy.169, f32[6,512,1024]{2,1,0:T(8,128)} %copy-done.1, f32[6,512,1024]{2,1,0:T(8,128)} %fusion.201, bf16[2,1024,6,64]{1,3,2,0:T(8,128)(2,1)} %get-tuple-element.499, s32[]{:T(128)S(6)} %select_n.176), kind=kOutput, calls=%fused_computation.38.clone.1 | convolution fusion | flops 418385920 | bytes 51904520 | tf_op jit(solution)/shard_map/while/body/eval_jaxpr/hqk,khd->qhd/dot_general | solution.py:209
  501.9 19.5 %bitcast_dynamic-update-slice_fusion.7 = f32[2,1024,6,64]{1,3,2,0:T(8,128)} fusion(f32[2,1024,6,64]{1,3,2,0:T(8,128)} %get-tuple-element.477, s32[]{:T(128)S(6)} %select_n.176, f32[1,1024,6,64]{1,3,2,0:T(8,128)S(1)} %get-tuple-element.423, f32[6,512,1024]{2,1,0:T(8,128)} %copy-done.1, f32[6,512,1024]{2,1,0:T(8,128)} %fusion.201, ...), kind=kOutput, calls=%fused_computation.35.clone.1 | convolution fusion | flops 418779136 | bytes 53870600 | tf_op jit(solution)/shard_map/while/body/eval_jaxpr/hqk,qhd->khd/dot_general | solution.py:210
  538.4 8.6 %fusion.84 = (f32[384]{0:T(512)S(1)}, f32[2048]{0:T(1024)S(1)}, f32[2048]{0:T(1024)S(1)}, f32[384]{0:T(512)S(1)}, f32[2048,384]{1,0:T(8,128)}) fusion(bf16[2,1024,384]{2,1,0:T(8,128)(2,1)S(1)} %copy-done.10, f32[2048]{0:T(1024)S(1)} %copy-done.36, f32[2048]{0:T(1024)S(1)} %copy-done.38, f32[384]{0:T(512)S(1)} %copy-done.44, ...), kind=kOutput, calls=%fused_computation.101 | convolution fusion | flops 1819798784 | bytes 10359296 | tf_op jit(solution)/shard_map/dot_general | solution.py:237
  549.1 39.2 %all-reduce = (f32[384]{0:T(512)}, f32[384]{0:T(512)}, f32[384]{0:T(512)}, f32[384]{0:T(512)}, f32[384]{0:T(512)}, /*index=5*/f32[384]{0:T(512)}, f32[384]{0:T(512)}, f32[384,16]{0,1:T(8,128)S(1)}, f32[3]{0:T(128)S(1)}) all-reduce(f32[384]{0:T(512)S(1)} %get-tuple-element.199, ...), channel_id=1, replica_groups=mesh['dp'=4,'expert'=8] {'dp','expert'}, use_global_device_ids=true, to_apply=%region_24.25 | all-reduce | flops 8835 | bytes 70680 | tf_op jit(solution)/shard_map/psum | solution.py:256
  593.8 129.9 %all-reduce.4.cloned.1.call-done = (f32[384,1152]{1,0:T(8,128)}, f32[384,384]{1,0:T(8,128)}) async-done(((f32[384,1152]{1,0:T(8,128)}, f32[384,384]{1,0:T(8,128)}), (f32[384,1152]{1,0:T(8,128)}, f32[384,384]{1,0:T(8,128)})) %all-reduce.4.cloned.1.call-update) | async-done | bytes 2359312 | tf_op jit(solution)/shard_map/psum | solution.py:256
  (340 shorter events, 231.7 us)
Async XLA Ops:
  7.2 38.0 %copy-start = (bf16[384,1152]{1,0:T(8,128)(2,1)S(1)}, bf16[384,1152]{1,0:T(8,128)(2,1)}, u32[]{:S(2)}) copy-start(bf16[384,1152]{1,0:T(8,128)(2,1)} %param.27) | copy-start | bytes 2654212
  7.2 37.2 %copy-start.9 = (bf16[2,1024,384]{2,1,0:T(8,128)(2,1)S(1)}, bf16[2,1024,384]{2,1,0:T(8,128)(2,1)}, u32[]{:S(2)}) copy-start(bf16[2,1024,384]{2,1,0:T(8,128)(2,1)} %param.22) | copy-start | bytes 4718596
  7.2 8.0 %copy-start.52 = (bf16[384,2]{0,1:T(2,128)(2,1)S(1)}, bf16[384,2]{0,1:T(2,128)(2,1)}, u32[]{:S(2)}) copy-start(bf16[384,2]{0,1:T(2,128)(2,1)} %param.34) | copy-start | bytes 4612
  7.2 37.1 %copy-start.43 = (f32[384]{0:T(512)S(1)}, f32[384]{0:T(512)}, u32[]{:S(2)}) copy-start(f32[384]{0:T(512)} %param.25) | copy-start | bytes 4612
  7.2 37.1 %copy-start.48 = (f32[384]{0:T(512)S(1)}, f32[384]{0:T(512)}, u32[]{:S(2)}) copy-start(f32[384]{0:T(512)} %param.26) | copy-start | bytes 4612
  154.5 17.6 %copy-start.53 = (bf16[2,384]{1,0:T(2,128)(2,1)S(1)}, bf16[2,384]{1,0:T(2,128)(2,1)}, u32[]{:S(2)}) copy-start(bf16[2,384]{1,0:T(2,128)(2,1)} %param.36) | copy-start | bytes 4612
  154.6 29.6 %copy-start.24 = (bf16[2,384,384]{2,1,0:T(8,128)(2,1)S(1)}, bf16[2,384,384]{2,1,0:T(8,128)(2,1)}, u32[]{:S(2)}) copy-start(bf16[2,384,384]{2,1,0:T(8,128)(2,1)} %param.35) | copy-start | bytes 1769476
  157.7 10.6 %all-to-all-start.2 = ((bf16[2,16,384]{2,0,1:T(2,128)(2,1)}), bf16[2,16,384]{2,0,1:T(2,128)(2,1)S(1)}, u32[]{:S(2)}, u32[]{:S(2)}) async-start(bf16[2,16,384]{2,0,1:T(2,128)(2,1)} %copy.83), calls=%async_computation.3 | async-start | bytes 49152 | tf_op jit(solution)/shard_map/all_to_all | solution.py:158
  168.3 9.9 %all-to-all-start = ((bf16[2,16,384]{2,0,1:T(2,128)(2,1)}), bf16[2,16,384]{2,0,1:T(2,128)(2,1)S(1)}, u32[]{:S(2)}, u32[]{:S(2)}) async-start(bf16[2,16,384]{2,0,1:T(2,128)(2,1)} %copy.79), calls=%async_computation | async-start | bytes 49152 | tf_op jit(solution)/shard_map/all_to_all | solution.py:129
  171.7 39.2 %reduce-scatter.3.cloned.1.call-start = ((), (), s32[]{:S(2)}) async-start(), calls=%async_computation.6 | async-start | bytes 122880 | tf_op jit(solution)/shard_map/reduce_scatter | solution.py:139
  184.3 26.6 %copy-start.47 = (f32[2,384]{1,0:T(2,128)S(1)}, f32[2,384]{1,0:T(2,128)}, u32[]{:S(2)}) copy-start(f32[2,384]{1,0:T(2,128)} %param.38) | copy-start | bytes 9220
  190.6 42.3 %reduce-scatter.5.cloned.1.call-start = ((), (), s32[]{:S(2)}) async-start(), calls=%async_computation.7 | async-start | bytes 122880 | tf_op jit(solution)/shard_map/reduce_scatter | solution.py:168
  212.3 22.0 %all-to-all-start.1 = ((bf16[16,2,384]{2,1,0:T(2,128)(2,1)}), bf16[16,2,384]{2,1,0:T(2,128)(2,1)S(1)}, u32[]{:S(2)}, u32[]{:S(2)}) async-start(bf16[16,2,384]{2,1,0:T(2,128)(2,1)} %copy.81), calls=%async_computation.2 | async-start | bytes 49152 | tf_op jit(solution)/shard_map/all_to_all | solution.py:145
  234.3 12.1 %all-to-all-start.3 = ((bf16[16,2,384]{2,1,0:T(2,128)(2,1)}), bf16[16,2,384]{2,1,0:T(2,128)(2,1)S(1)}, u32[]{:S(2)}, u32[]{:S(2)}) async-start(bf16[16,2,384]{2,1,0:T(2,128)(2,1)} %copy.85), calls=%async_computation.5 | async-start | bytes 49152 | tf_op jit(solution)/shard_map/all_to_all | solution.py:172
  239.8 483.9 %all-reduce.4.cloned.1.call-start = ((), (), s32[]{:S(2)}) async-start(), calls=%async_computation.8 | async-start | bytes 4718592 | tf_op jit(solution)/shard_map/psum | solution.py:256
  243.1 6.3 copy-start.32
  251.2 5.2 copy-start.17
  282.7 5.0 copy-start.2
  282.7 5.0 copy-start.14
  287.7 6.4 copy-start.12
  343.9 4.9 copy-start.2
  343.9 5.0 copy-start.14
  348.9 6.4 copy-start.12
  405.1 5.0 copy-start.14
  410.1 6.4 copy-start.12
  466.3 5.0 copy-start.2
  466.3 5.0 copy-start.14
  471.3 6.4 copy-start.12
  538.3 10.8 %copy-start.34 = (f32[384,16]{0,1:T(8,128)S(1)}, f32[384,16]{0,1:T(8,128)}, u32[]{:S(2)}) copy-start(f32[384,16]{0,1:T(8,128)} %fusion.134) | copy-start | bytes 73732
  538.3 10.8 %copy-start.42 = (f32[384]{0:T(512)S(1)}, f32[384]{0:T(512)}, u32[]{:S(2)}) copy-start(f32[384]{0:T(512)} %get-tuple-element.260) | copy-start | bytes 4612
  538.3 10.8 %copy-start.45 = (f32[384]{0:T(512)S(1)}, f32[384]{0:T(512)}, u32[]{:S(2)}) copy-start(f32[384]{0:T(512)} %get-tuple-element.197) | copy-start | bytes 4612
  538.3 10.8 %copy-start.46 = (f32[384]{0:T(512)S(1)}, f32[384]{0:T(512)}, u32[]{:S(2)}) copy-start(f32[384]{0:T(512)} %get-tuple-element.203) | copy-start | bytes 4612
  (59 other events, 169.3 us)
Sparse Core Ops, SparseCore 0:
  190.7 20.1 reduce-scatter.2
  213.3 19.5 reduce-scatter.4
  589.0 134.6 all-reduce.3
where the time goes:
time: 743 us; the launch traced here: 734 us
  matrix products  279 us (38%)
  waiting for transfers between devices  169 us (23%)
  local copies, waits for them, and re-layouts  111 us (15%)
  blocking collectives  77.5 us (10%)
  other arithmetic  48.1 us (6%)
  starting transfers between devices  18.9 us (3%)
  loops' own time  16.8 us (2%)
  between operations  14.9 us (2%)
    psum x1, waiting for transfers between devices, local(): lax.psum((ln1_gain_grad, ln1_bias_grad, qkv_weight_grad, query_bias_grad,...  130 us
    dot_general x4, matrix products, attend_back(): jnp.einsum('hqk,qhd->khd', score_low, query_part, preferred_element_type=...  78.2 us
    dot_general x4, matrix products, attend_back(): jnp.einsum('hqk,khd->qhd', score_low, key_part, preferred_element_type=f32)  71.9 us
    psum x1, blocking collectives, local(): lax.psum((ln1_gain_grad, ln1_bias_grad, qkv_weight_grad, query_bias_grad,...  39.2 us
    dot_general x8, matrix products, block_scores(): jnp.einsum('qhd,khd->hqk', query_part, key_part, preferred_element_type=f32)  34.3 us
    all_gather x1, blocking collectives, local(): phi_all = lax.all_gather(slot_params, 'expert', axis=1, tiled=True)  27.7 us
    dot_general x4, matrix products, attend_back(): jnp.einsum('qhd,khd->hqk', grad_part, value_part, preferred_element_type=...  25.2 us
    while x72, local copies, waits for them, and re-layouts  22.9 us
  transfers between devices with their start and end apart: 7, of which 6 were waited for; matrix products, arithmetic and copies ran while one was open for 2% of the time, Pallas kernels for 0%

commit v1 on v0

v1 whole, which is shorter than its diff:
```python
import functools

import jax
import jax.numpy as jnp
from jax import lax
from jax.experimental import pallas as pl
from jax.experimental.pallas import tpu as pltpu
from jax.sharding import PartitionSpec as P

HEADS = 6
IMAGES = 6
EPSILON = 1e-06
MASKED = -1e30
LANES = 128
TILE = 256
CHUNK = 256
VMEM_BYTES = 60 * 1024 * 1024

bf16 = jnp.bfloat16
f32 = jnp.float32

NN = (((1,), (0,)), ((), ()))
NT = (((1,), (1,)), ((), ()))
TN = (((0,), (0,)), ((), ()))


def dot(left, right, dims=NN):
    return lax.dot_general(left, right, dims, preferred_element_type=f32)


def lane_ids(rows):
    return lax.broadcasted_iota(jnp.int32, (rows, LANES), 1)


def norm_parts(values):
    width = values.shape[-1]
    centre = values - jnp.sum(values, axis=-1, keepdims=True) * (1.0 / width)
    power = jnp.sum(centre * centre, axis=-1, keepdims=True) * (1.0 / width)
    recip = lax.rsqrt(power + EPSILON)
    return centre * recip, recip


def norm_back(grad, hat, recip, gain):
    width = grad.shape[-1]
    scaled = grad * gain
    first = jnp.sum(scaled, axis=-1, keepdims=True) * (1.0 / width)
    second = jnp.sum(scaled * hat, axis=-1, keepdims=True) * (1.0 / width)
    return recip * (scaled - first - hat * second)


def image_columns(id_row):
    return jnp.transpose(jnp.broadcast_to(id_row.astype(f32), (LANES, id_row.shape[1])))


def image_starts(id_row):
    as_float = id_row.astype(f32)
    return [
        jnp.sum(jnp.where(as_float < float(v), 1.0, 0.0)).astype(jnp.int32)
        for v in range(1, IMAGES)
    ]


def key_window(starts, tile, seq_len):
    first, last = tile * TILE, tile * TILE + TILE - 1
    low, high = 0, seq_len
    for s in starts:
        low = jnp.maximum(low, jnp.where(s <= first, s, 0))
        high = jnp.minimum(high, jnp.where(s > last, s, seq_len))
    low = lax.div(low, LANES) * LANES
    count = lax.div(high - low + (TILE - 1), TILE)
    low = jnp.minimum(low, seq_len - count * TILE)
    return low, count


def query_marks(columns, lanes):
    return jnp.where(columns == (lanes - 24).astype(f32), 1.0, 0.0)


def key_marks(columns, lanes):
    other = jnp.where(columns == (lanes - 24).astype(f32), 0.0, MASKED)
    inside = jnp.logical_and(lanes >= 24, lanes < 24 + IMAGES)
    return jnp.where(inside, other, jnp.where(lanes < 24, 1.0, 0.0))


def three_parts(values, lanes):
    values = jnp.where(lanes < 8, values, 0.0)
    top = values.astype(bf16).astype(f32)
    rest = values - top
    mid = rest.astype(bf16).astype(f32)
    low = (rest - mid).astype(bf16).astype(f32)
    return top + pltpu.roll(mid, 8, 1) + pltpu.roll(low, 16, 1)


def own_lanes(values, lanes, head):
    keep = jnp.logical_or(lanes >= 24, lax.rem(lanes, 8) == head)
    return jnp.where(keep, values, 0.0)


def attend_kernel(
    tokens_ref, ids_ref, vecs_ref, qkv_w_ref, out_w_ref,
    low_one_ref, qkv_ref, mixed_ref, mixed_rest_ref, lse_ref, residual_ref, low_two_ref, sums_ref,
    q_scr, k_scr, v_scr, s_scr, top_scr, acc_scr,
):
    row = pl.program_id(0)
    seq_len, width = tokens_ref.shape[1:]
    pairs = width // LANES
    scale = (width // HEADS) ** -0.5
    id_row = ids_ref[pl.ds(row, 1), :]
    starts = image_starts(id_row)
    columns_all = image_columns(id_row)
    lanes_all = lane_ids(seq_len)
    marks_q = query_marks(columns_all, lanes_all).astype(bf16)
    marks_k = key_marks(columns_all, lanes_all).astype(bf16)
    for h in range(HEADS):
        q_scr[h, :, LANES:] = marks_q
    for p in range(pairs):
        k_scr[p, :, LANES:] = marks_k
    lanes = lane_ids(CHUNK)
    left = lanes < LANES // 2

    def project(c, total):
        part = pl.ds(pl.multiple_of(c * CHUNK, CHUNK), CHUNK)
        stream = tokens_ref[0, part, :].astype(f32)
        hat, _ = norm_parts(stream)
        low_one = (hat * vecs_ref[0:1, :] + vecs_ref[1:2, :]).astype(bf16)
        low_one_ref[0, part, :] = low_one
        projected = dot(low_one, qkv_w_ref[...])
        query = (projected[:, :width] + vecs_ref[2:3, :]).astype(bf16)
        key = projected[:, width : 2 * width].astype(bf16)
        value = (projected[:, 2 * width :] + vecs_ref[3:4, :]).astype(bf16)
        qkv_ref[0, part, :width] = query
        qkv_ref[0, part, width : 2 * width] = key
        qkv_ref[0, part, 2 * width :] = value
        for p in range(pairs):
            cut = slice(p * LANES, (p + 1) * LANES)
            scaled = query[:, cut].astype(f32) * scale
            v_pair = value[:, cut].astype(f32)
            k_scr[p, part, :LANES] = key[:, cut]
            q_scr[2 * p, part, :LANES] = jnp.where(left, scaled, 0.0).astype(bf16)
            q_scr[2 * p + 1, part, :LANES] = jnp.where(left, 0.0, scaled).astype(bf16)
            v_scr[2 * p, part, :] = jnp.where(left, v_pair, 1.0).astype(bf16)
            v_scr[2 * p + 1, part, :] = jnp.where(left, 1.0, v_pair).astype(bf16)
        return total + jnp.sum(stream * stream, axis=0, keepdims=True)

    stream_sq = lax.fori_loop(0, seq_len // CHUNK, project, jnp.zeros((1, width), f32))

    def query_tile(i, total):
        at = pl.ds(pl.multiple_of(i * TILE, TILE), TILE)
        begin, count = key_window(starts, i, seq_len)
        top_scr[...] = jnp.full_like(top_scr, -3e38)
        acc_scr[...] = jnp.zeros_like(acc_scr)

        def scores(j, carry):
            keys = pl.ds(pl.multiple_of(begin + j * TILE, LANES), TILE)
            for h in range(HEADS):
                s = dot(q_scr[h, at, :], k_scr[h // 2, keys, :], NT)
                s_scr[j, h] = s
                best = s[:, :LANES]
                for o in range(LANES, TILE, LANES):
                    best = jnp.maximum(best, s[:, o : o + LANES])
                top_scr[h] = jnp.maximum(top_scr[h], best)
            return carry

        lax.fori_loop(0, count, scores, 0)
        for h in range(HEADS):
            top_scr[h] = jnp.broadcast_to(
                jnp.max(top_scr[h], axis=-1, keepdims=True), top_scr.shape[1:]
            )

        def weigh(j, carry):
            keys = pl.ds(pl.multiple_of(begin + j * TILE, LANES), TILE)
            for h in range(HEADS):
                top = jnp.concatenate([top_scr[h]] * (TILE // LANES), axis=1)
                probs = jnp.exp(s_scr[j, h] - top).astype(bf16)
                acc_scr[h] += dot(probs, v_scr[h, keys, :])
            return carry

        lax.fori_loop(0, count, weigh, 0)
        tile_lanes = lane_ids(TILE)
        tile_left = tile_lanes < LANES // 2
        lse = jnp.zeros((TILE, LANES), f32)
        mixed_pairs = []
        for p in range(pairs):
            even, odd = acc_scr[2 * p], acc_scr[2 * p + 1]
            swapped = jnp.where(tile_left, odd, even)
            sums = pltpu.roll(swapped, LANES // 2, 1)
            mixed_pairs.append(jnp.where(tile_left, even, odd) / sums)
            lse = jnp.where(tile_lanes == 2 * p, top_scr[2 * p] + jnp.log(sums), lse)
            lse = jnp.where(tile_lanes == 2 * p + 1, top_scr[2 * p + 1] + jnp.log(swapped), lse)
        lse_ref[0, at, :] = lse
        mixed = jnp.concatenate(mixed_pairs, axis=1)
        mixed_low = mixed.astype(bf16)
        mixed_ref[0, at, :] = mixed_low
        mixed_rest_ref[0, at, :] = (mixed - mixed_low.astype(f32)).astype(bf16)
        branch = dot(mixed_low, out_w_ref[...]) + vecs_ref[4:5, :]
        residual = tokens_ref[0, at, :].astype(f32) + branch
        residual_ref[0, at, :] = residual
        hat, _ = norm_parts(residual)
        low_two_ref[0, at, :] = (hat * vecs_ref[5:6, :] + vecs_ref[6:7, :]).astype(bf16)
        return total + jnp.sum(branch * branch, axis=0, keepdims=True)

    branch_sq = lax.fori_loop(0, seq_len // TILE, query_tile, jnp.zeros((1, width), f32))
    sums_ref[0] = jnp.concatenate(
        [stream_sq, branch_sq, jnp.zeros((6, width), f32)], axis=0
    )


def attend(tokens, image_ids, vecs, qkv_weight, out_weight):
    rows, seq_len, width = tokens.shape
    pairs = width // LANES
    per_row = lambda lanes: pl.BlockSpec((1, seq_len, lanes), lambda r: (r, 0, 0))
    whole = lambda *shape: pl.BlockSpec(shape, lambda r: (0,) * len(shape))
    shape = lambda lanes, kind: jax.ShapeDtypeStruct((rows, seq_len, lanes), kind)
    return pl.pallas_call(
        attend_kernel,
        grid=(rows,),
        in_specs=[
            per_row(width), whole(rows, seq_len), whole(8, width),
            whole(width, 3 * width), whole(width, width),
        ],
        out_specs=[
            per_row(width), per_row(3 * width), per_row(width), per_row(width), per_row(LANES),
            per_row(width), per_row(width), pl.BlockSpec((1, 8, width), lambda r: (r, 0, 0)),
        ],
        out_shape=[
            shape(width, bf16), shape(3 * width, bf16), shape(width, bf16), shape(width, bf16),
            shape(LANES, f32), shape(width, f32), shape(width, bf16),
            jax.ShapeDtypeStruct((rows, 8, width), f32),
        ],
        scratch_shapes=[
            pltpu.VMEM((HEADS, seq_len, 2 * LANES), bf16),
            pltpu.VMEM((pairs, seq_len, 2 * LANES), bf16),
            pltpu.VMEM((HEADS, seq_len, LANES), bf16),
            pltpu.VMEM((seq_len // TILE, HEADS, TILE, TILE), f32),
            pltpu.VMEM((HEADS, TILE, LANES), f32),
            pltpu.VMEM((HEADS, TILE, LANES), f32),
        ],
        cost_estimate=pl.CostEstimate(
            flops=20 * 10**9, bytes_accessed=20 * 10**6, transcendentals=10**7
        ),
        compiler_params=pltpu.CompilerParams(vmem_limit_bytes=VMEM_BYTES),
        name="attend",
    )(tokens, image_ids, vecs, qkv_weight, out_weight)


def route_kernel(
    low_two_ref, cot_ref, ids_ref, slot_ref, phi_ref, dispatch_ref, combine_ref, slots_ref
):
    row = pl.program_id(0)
    slot_count = slots_ref.shape[2]
    columns = image_columns(ids_ref[pl.ds(row, 1), :])
    allowed = columns == slot_ref[pl.ds(row, 1), :].astype(f32)
    low_two = low_two_ref[0]
    logits = jnp.where(allowed, dot(low_two, phi_ref[...], NT), MASKED)

    def select(axis):
        top = jnp.max(logits, axis=axis, keepdims=True)
        weights = jnp.where(allowed, jnp.exp(logits - top), 0.0)
        total = jnp.sum(weights, axis=axis, keepdims=True)
        return weights / jnp.where(total == 0.0, 1.0, total)

    dispatch = select(0)
    combine = select(1)
    dispatch_ref[0] = dispatch
    combine_ref[0] = combine
    slot_in = dot(dispatch.astype(bf16), low_two, TN)
    out_grad = dot(combine.astype(bf16), cot_ref[0], TN)
    slots_ref[0, 0] = slot_in[:slot_count].astype(bf16)
    slots_ref[0, 1] = out_grad[:slot_count].astype(bf16)


def route(low_two, cotangent, image_ids, slot_rows, phi, slot_count):
    rows, seq_len, width = low_two.shape
    lanes = phi.shape[0]
    per_row = lambda n: pl.BlockSpec((1, seq_len, n), lambda r: (r, 0, 0))
    whole = lambda *shape: pl.BlockSpec(shape, lambda r: (0,) * len(shape))
    return pl.pallas_call(
        route_kernel,
        grid=(rows,),
        in_specs=[
            per_row(width), per_row(width), whole(rows, seq_len), whole(rows, lanes),
            whole(lanes, width),
        ],
        out_specs=[
            per_row(lanes), per_row(lanes),
            pl.BlockSpec((1, 2, slot_count, width), lambda r: (r, 0, 0, 0)),
        ],
        out_shape=[
            jax.ShapeDtypeStruct((rows, seq_len, lanes), f32),
            jax.ShapeDtypeStruct((rows, seq_len, lanes), f32),
            jax.ShapeDtypeStruct((rows, 2, slot_count, width), bf16),
        ],
        compiler_params=pltpu.CompilerParams(vmem_limit_bytes=VMEM_BYTES),
        name="route",
    )(low_two, cotangent, image_ids, slot_rows, phi)


def expert_kernel(
    rows_ref, up_ref, up_bias_ref, down_ref, down_bias_ref, parts_ref, hidden_ref, pre_grad_ref
):
    for e in range(rows_ref.shape[0]):
        slot_in, out_grad = rows_ref[e, 0], rows_ref[e, 1]
        up, down = up_ref[e], down_ref[e]
        pre_act = dot(slot_in, up, NT) + up_bias_ref[e : e + 1, :].astype(f32)
        cdf = 0.5 * (1.0 + lax.erf(pre_act * 0.7071067811865476))
        density = jnp.exp(-0.5 * pre_act * pre_act) * 0.3989422804014327
        hidden = (pre_act * cdf).astype(bf16)
        pre_grad = (dot(out_grad, down, NT) * (cdf + pre_act * density)).astype(bf16)
        hidden_ref[e] = hidden
        pre_grad_ref[e] = pre_grad
        parts_ref[e, 0] = (dot(hidden, down) + down_bias_ref[e : e + 1, :]).astype(bf16)
        parts_ref[e, 1] = dot(pre_grad, up).astype(bf16)


def expert_grad_kernel(
    rows_ref, hidden_ref, pre_grad_ref, up_grad_ref, up_bias_grad_ref, down_grad_ref,
    down_bias_grad_ref,
):
    for e in range(rows_ref.shape[0]):
        slot_in, out_grad = rows_ref[e, 0], rows_ref[e, 1]
        pre_grad = pre_grad_ref[e]
        down_grad_ref[e] = dot(hidden_ref[e], out_grad, TN)
        up_grad_ref[e] = dot(pre_grad, slot_in, TN)
        up_bias_grad_ref[e : e + 1, :] = jnp.sum(pre_grad.astype(f32), axis=0, keepdims=True)
        down_bias_grad_ref[e : e + 1, :] = jnp.sum(out_grad.astype(f32), axis=0, keepdims=True)


def experts(rows, up_weight, up_bias, down_weight, down_bias_part):
    own, _, count, width = rows.shape
    hidden = up_weight.shape[1]
    low = lambda *shape: jax.ShapeDtypeStruct(shape, bf16)
    return pl.pallas_call(
        expert_kernel,
        out_shape=[low(*rows.shape), low(own, count, hidden), low(own, count, hidden)],
        compiler_params=pltpu.CompilerParams(vmem_limit_bytes=VMEM_BYTES),
        name="experts",
    )(rows, up_weight, up_bias, down_weight, down_bias_part)


def expert_grads(rows, hidden, pre_grad):
    own, _, count, width = rows.shape
    units = hidden.shape[-1]
    full = lambda *shape: jax.ShapeDtypeStruct(shape, f32)
    return pl.pallas_call(
        expert_grad_kernel,
        out_shape=[
            full(own, units, width), full(own, units), full(own, units, width), full(own, width),
        ],
        cost_estimate=pl.CostEstimate(
            flops=4 * own * count * units * width, bytes_accessed=4 * 10**6, transcendentals=0
        ),
        compiler_params=pltpu.CompilerParams(vmem_limit_bytes=VMEM_BYTES),
        name="expert_grads",
    )(rows, hidden, pre_grad)


def back_kernel(
    residual_ref, low_two_ref, dispatch_ref, combine_ref, cot_ref, back_ref, mixed_ref,
    mixed_rest_ref, qkv_ref, lse_ref, low_one_ref, ids_ref, vecs_ref, phi_ref, out_w_ref,
    output_ref, resid_grad_ref, qkv_grad_ref, weight_grad_ref, phi_grad_ref, rows_ref,
    cg_scr, dg_scr, logit_scr, branch_scr, mixed_grad_scr, d_scr, q_scr, k_scr, o_scr, v_scr,
    dq_scr, dk_scr, dv_scr, grad_scr,
):
    row = pl.program_id(0)
    seq_len, width = residual_ref.shape[1:]
    pairs = width // LANES
    scale = (width // HEADS) ** -0.5
    slot_count = back_ref.shape[3]
    lanes_all = lane_ids(seq_len)

    @pl.when(row == 0)
    def _():
        grad_scr[...] = jnp.zeros_like(grad_scr)
        phi_grad_ref[...] = jnp.zeros_like(phi_grad_ref)
        rows_ref[...] = jnp.zeros_like(rows_ref)

    slot_lanes = phi_ref.shape[0]

    def padded(kind):
        total = jnp.sum(back_ref[0, :, kind].astype(f32), axis=0)
        if slot_lanes > slot_count:
            total = jnp.concatenate(
                [total, jnp.zeros((slot_lanes - slot_count, width), f32)], axis=0
            )
        return total.astype(bf16)

    expert_out = padded(0)
    slot_grad = padded(1)

    def spread(c, total):
        part = pl.ds(pl.multiple_of(c * CHUNK, CHUNK), CHUNK)
        moe_out = dot(combine_ref[0, part, :].astype(bf16), expert_out)
        output_ref[0, part, :] = (residual_ref[0, part, :] + moe_out).astype(bf16)
        cg_scr[part, :] = dot(cot_ref[0, part, :], expert_out, NT)
        dg_scr[part, :] = dot(low_two_ref[0, part, :], slot_grad, NT)
        return total + jnp.sum(moe_out * moe_out, axis=0, keepdims=True)

    moe_sq = lax.fori_loop(0, seq_len // CHUNK, spread, jnp.zeros((1, width), f32))
    combine, dispatch = combine_ref[0], dispatch_ref[0]
    combine_grad, dispatch_grad = cg_scr[...], dg_scr[...]
    logit_grad = combine * (
        combine_grad - jnp.sum(combine * combine_grad, axis=1, keepdims=True)
    ) + dispatch * (dispatch_grad - jnp.sum(dispatch * dispatch_grad, axis=0, keepdims=True))
    logit_scr[...] = logit_grad.astype(bf16)
    phi_grad_ref[...] += dot(logit_scr[...], low_two_ref[0], TN)

    head_of = lax.broadcasted_iota(jnp.int32, (width, LANES), 0) // (width // HEADS)
    picker = jnp.where(
        head_of == lax.broadcasted_iota(jnp.int32, (width, LANES), 1), 1.0, 0.0
    ).astype(bf16)

    def through_norm(c, totals):
        part = pl.ds(pl.multiple_of(c * CHUNK, CHUNK), CHUNK)
        grad = dot(dispatch_ref[0, part, :].astype(bf16), slot_grad)
        grad += dot(logit_scr[part, :], phi_ref[...])
        hat, recip = norm_parts(residual_ref[0, part, :])
        resid = cot_ref[0, part, :].astype(f32) + norm_back(grad, hat, recip, vecs_ref[5:6, :])
        resid_grad_ref[0, part, :] = resid
        branch_low = resid.astype(bf16)
        branch_scr[part, :] = branch_low
        mixed_grad = dot(branch_low, out_w_ref[...], NT).astype(bf16)
        mixed_grad_scr[part, :] = mixed_grad
        wide = mixed_grad.astype(f32)
        d_total = jnp.zeros((CHUNK, LANES), f32)
        for mixed_part in (mixed_ref, mixed_rest_ref):
            product = mixed_part[0, part, :].astype(f32) * wide
            top = product.astype(bf16)
            d_total += dot(top, picker)
            d_total += dot((product - top.astype(f32)).astype(bf16), picker)
        d_scr[part, :] = d_total
        gain_total, shift_total, bias_total = totals
        return (
            gain_total + jnp.sum(grad * hat, axis=0, keepdims=True),
            shift_total + jnp.sum(grad, axis=0, keepdims=True),
            bias_total + jnp.sum(branch_low.astype(f32), axis=0, keepdims=True),
        )

    zero_row = jnp.zeros((1, width), f32)
    gain_sum, shift_sum, bias_sum = lax.fori_loop(
        0, seq_len // CHUNK, through_norm, (zero_row, zero_row, zero_row)
    )
    grad_scr[:, 3 * width :] += dot(mixed_ref[0], branch_scr[...], TN)

    id_row = ids_ref[pl.ds(row, 1), :]
    starts = image_starts(id_row)
    columns = image_columns(id_row)
    left = lanes_all < LANES // 2
    marks_q = query_marks(columns, lanes_all) - three_parts(lse_ref[0], lanes_all)
    marks_k = key_marks(columns, lanes_all).astype(bf16)
    marks_o = -three_parts(d_scr[...], lanes_all)
    ones = jnp.where(lanes_all < 24, 1.0, 0.0).astype(bf16)
    for p in range(pairs):
        cut = slice(p * LANES, (p + 1) * LANES)
        scaled = qkv_ref[0, :, cut].astype(f32) * scale
        mixed_grad = mixed_grad_scr[:, cut].astype(f32)
        k_scr[p, :, :LANES] = qkv_ref[0, :, width + p * LANES : width + (p + 1) * LANES]
        k_scr[p, :, LANES:] = marks_k
        v_scr[p, :, :LANES] = qkv_ref[0, :, 2 * width + p * LANES : 2 * width + (p + 1) * LANES]
        v_scr[p, :, LANES:] = ones
        for odd in range(2):
            h = 2 * p + odd
            mine = jnp.logical_not(left) if odd else left
            q_scr[h, :, :LANES] = jnp.where(mine, scaled, 0.0).astype(bf16)
            q_scr[h, :, LANES:] = own_lanes(marks_q, lanes_all, h).astype(bf16)
            o_scr[h, :, :LANES] = jnp.where(mine, mixed_grad, 0.0).astype(bf16)
            o_scr[h, :, LANES:] = own_lanes(marks_o, lanes_all, h).astype(bf16)
    dq_scr[...] = jnp.zeros_like(dq_scr)
    dk_scr[...] = jnp.zeros_like(dk_scr)
    dv_scr[...] = jnp.zeros_like(dv_scr)
    tile_left = lane_ids(TILE) < LANES // 2

    def query_tile(i, carry):
        at = pl.ds(pl.multiple_of(i * TILE, TILE), TILE)
        begin, count = key_window(starts, i, seq_len)

        def key_tile(j, inner):
            keys = pl.ds(pl.multiple_of(begin + j * TILE, LANES), TILE)
            for p in range(pairs):
                cut = slice(p * LANES, (p + 1) * LANES)
                k_pair = k_scr[p, keys, :LANES]
                q_pair = qkv_ref[0, at, cut]
                o_pair = mixed_grad_scr[at, cut]
                found = []
                for h in (2 * p, 2 * p + 1):
                    probs = jnp.exp(dot(q_scr[h, at, :], k_scr[p, keys, :], NT))
                    prob_grad = dot(o_scr[h, at, :], v_scr[p, keys, :], NT)
                    score_grad = (probs * prob_grad).astype(bf16)
                    found.append(
                        (
                            dot(score_grad, k_pair),
                            dot(score_grad, q_pair, TN),
                            dot(probs.astype(bf16), o_pair, TN),
                        )
                    )
                dq_scr[p, at, :] += jnp.where(tile_left, found[0][0], found[1][0])
                dk_scr[p, keys, :] += jnp.where(tile_left, found[0][1], found[1][1])
                dv_scr[p, keys, :] += jnp.where(tile_left, found[0][2], found[1][2])
            return inner

        return lax.fori_loop(0, count, key_tile, carry)

    lax.fori_loop(0, seq_len // TILE, query_tile, 0)
    for p in range(pairs):
        for block, (source, factor) in enumerate(
            ((dq_scr, scale), (dk_scr, scale), (dv_scr, 1.0))
        ):
            start = block * width + p * LANES
            qkv_grad_ref[0, :, start : start + LANES] = (source[p] * factor).astype(bf16)
    grad_scr[:, : 3 * width] += dot(low_one_ref[0], qkv_grad_ref[0], TN)
    query_sum = jnp.sum(qkv_grad_ref[0, :, :width].astype(f32), axis=0, keepdims=True)
    value_sum = jnp.sum(qkv_grad_ref[0, :, 2 * width :].astype(f32), axis=0, keepdims=True)
    rows_ref[...] += jnp.concatenate(
        [query_sum, value_sum, bias_sum, gain_sum, shift_sum, moe_sq, zero_row, zero_row], axis=0
    )

    @pl.when(row == pl.num_programs(0) - 1)
    def _():
        for b in range(4):
            weight_grad_ref[b] = grad_scr[:, b * width : (b + 1) * width].astype(bf16)


def back(
    residual, low_two, dispatch, combine, cotangent, returned, mixed, mixed_rest, qkv, lse,
    low_one, image_ids, vecs, phi, out_weight,
):
    rows, seq_len, width = residual.shape
    lanes = phi.shape[0]
    pairs = width // LANES
    per_row = lambda n: pl.BlockSpec((1, seq_len, n), lambda r: (r, 0, 0))
    whole = lambda *shape: pl.BlockSpec(shape, lambda r: (0,) * len(shape))
    return pl.pallas_call(
        back_kernel,
        grid=(rows,),
        in_specs=[
            per_row(width), per_row(width), per_row(lanes), per_row(lanes), per_row(width),
            pl.BlockSpec((1,) + returned.shape[1:], lambda r: (r, 0, 0, 0, 0)),
            per_row(width), per_row(width), per_row(3 * width), per_row(LANES), per_row(width),
            whole(rows, seq_len), whole(8, width), whole(lanes, width), whole(width, width),
        ],
        out_specs=[
            per_row(width), per_row(width), per_row(3 * width), whole(4, width, width),
            whole(lanes, width), whole(8, width),
        ],
        out_shape=[
            jax.ShapeDtypeStruct((rows, seq_len, width), bf16),
            jax.ShapeDtypeStruct((rows, seq_len, width), f32),
            jax.ShapeDtypeStruct((rows, seq_len, 3 * width), bf16),
            jax.ShapeDtypeStruct((4, width, width), bf16),
            jax.ShapeDtypeStruct((lanes, width), f32),
            jax.ShapeDtypeStruct((8, width), f32),
        ],
        scratch_shapes=[
            pltpu.VMEM((seq_len, lanes), f32),
            pltpu.VMEM((seq_len, lanes), f32),
            pltpu.VMEM((seq_len, lanes), bf16),
            pltpu.VMEM((seq_len, width), bf16),
            pltpu.VMEM((seq_len, width), bf16),
            pltpu.VMEM((seq_len, LANES), f32),
            pltpu.VMEM((HEADS, seq_len, 2 * LANES), bf16),
            pltpu.VMEM((pairs, seq_len, 2 * LANES), bf16),
            pltpu.VMEM((HEADS, seq_len, 2 * LANES), bf16),
            pltpu.VMEM((pairs, seq_len, 2 * LANES), bf16),
            pltpu.VMEM((pairs, seq_len, LANES), f32),
            pltpu.VMEM((pairs, seq_len, LANES), f32),
            pltpu.VMEM((pairs, seq_len, LANES), f32),
            pltpu.VMEM((width, 4 * width), f32),
        ],
        cost_estimate=pl.CostEstimate(
            flops=60 * 10**9, bytes_accessed=20 * 10**6, transcendentals=10**7
        ),
        compiler_params=pltpu.CompilerParams(vmem_limit_bytes=VMEM_BYTES),
        name="back",
    )(
        residual, low_two, dispatch, combine, cotangent, returned, mixed, mixed_rest, qkv, lse,
        low_one, image_ids, vecs, phi, out_weight,
    )


def input_kernel(tokens_ref, qkv_grad_ref, resid_grad_ref, vecs_ref, qkv_w_ref, out_ref, rows_ref):
    seq_len, width = tokens_ref.shape[1:]

    @pl.when(pl.program_id(0) == 0)
    def _():
        rows_ref[...] = jnp.zeros_like(rows_ref)

    def chunk(c, totals):
        part = pl.ds(pl.multiple_of(c * CHUNK, CHUNK), CHUNK)
        grad = dot(qkv_grad_ref[0, part, :], qkv_w_ref[...], NT)
        hat, recip = norm_parts(tokens_ref[0, part, :].astype(f32))
        through = norm_back(grad, hat, recip, vecs_ref[0:1, :])
        out_ref[0, part, :] = (resid_grad_ref[0, part, :] + through).astype(bf16)
        return (
            totals[0] + jnp.sum(grad * hat, axis=0, keepdims=True),
            totals[1] + jnp.sum(grad, axis=0, keepdims=True),
        )

    zero_row = jnp.zeros((1, width), f32)
    gain_sum, shift_sum = lax.fori_loop(0, seq_len // CHUNK, chunk, (zero_row, zero_row))
    rows_ref[...] += jnp.concatenate([gain_sum, shift_sum, jnp.zeros((6, width), f32)], axis=0)


def input_back(tokens, qkv_grad, resid_grad, vecs, qkv_weight):
    rows, seq_len, width = tokens.shape
    per_row = lambda n: pl.BlockSpec((1, seq_len, n), lambda r: (r, 0, 0))
    whole = lambda *shape: pl.BlockSpec(shape, lambda r: (0,) * len(shape))
    return pl.pallas_call(
        input_kernel,
        grid=(rows,),
        in_specs=[
            per_row(width), per_row(3 * width), per_row(width), whole(8, width),
            whole(width, 3 * width),
        ],
        out_specs=[per_row(width), whole(8, width)],
        out_shape=[
            jax.ShapeDtypeStruct((rows, seq_len, width), bf16),
            jax.ShapeDtypeStruct((8, width), f32),
        ],
        cost_estimate=pl.CostEstimate(
            flops=6 * 10**9, bytes_accessed=10**7, transcendentals=0
        ),
        compiler_params=pltpu.CompilerParams(vmem_limit_bytes=VMEM_BYTES),
        name="input_back",
    )(tokens, qkv_grad, resid_grad, vecs, qkv_weight)


def local(
    tokens, image_ids, slot_image, ln1_gain, ln1_bias, qkv_weight, query_bias, value_bias,
    out_weight, out_bias, ln2_gain, ln2_bias, slot_params, up_weight, up_bias, down_weight,
    down_bias, cotangent,
):
    axes = ("dp", "expert")
    dp, ep = lax.axis_size("dp"), lax.axis_size("expert")
    devices = dp * ep
    seqs, seq_len, width = tokens.shape
    own = slot_params.shape[1]
    slots = own * ep
    lanes = -(-slots // LANES) * LANES

    def exchange(values, over):
        return lax.all_to_all(values, over, split_axis=0, concat_axis=0, tiled=True)

    phi = exchange(jnp.broadcast_to(slot_params.T[None], (ep, own, width)), "expert")
    phi = jnp.pad(phi.reshape(slots, width), ((0, lanes - slots), (0, 0)))
    slot_rows = jnp.pad(slot_image, ((0, 0), (0, lanes - slots)), constant_values=-1)
    vecs = jnp.stack(
        [ln1_gain, ln1_bias, query_bias, value_bias, out_bias, ln2_gain, ln2_bias, ln2_bias]
    )

    low_one, qkv, mixed, mixed_rest, lse, residual, low_two, sums = attend(
        tokens, image_ids, vecs, qkv_weight, out_weight
    )
    dispatch, combine, slot_rows_out = route(
        low_two, cotangent, image_ids, slot_rows, phi, slots
    )

    sent = slot_rows_out.reshape(seqs, 2, ep, own, width).transpose(2, 0, 1, 3, 4)
    sent = jnp.broadcast_to(sent[None], (dp,) + sent.shape)
    arrived = exchange(sent.reshape(devices, seqs * 2 * own, width), axes)
    arrived = arrived.reshape(devices, seqs, 2, own, width).transpose(3, 2, 0, 1, 4)
    arrived = arrived.reshape(own, 2, devices * seqs, width)
    parts, hidden, pre_grad = experts(
        arrived, up_weight, up_bias, down_weight, down_bias * (1.0 / dp)
    )
    parts = parts.reshape(own, 2, devices, seqs, width).transpose(2, 3, 1, 0, 4)
    returned = exchange(parts.reshape(devices, seqs * 2 * own, width), axes)
    returned = returned.reshape(dp, ep, seqs, 2, own, width).transpose(2, 0, 3, 1, 4, 5)
    returned = returned.reshape(seqs, dp, 2, slots, width)
    up_grad, up_bias_grad, down_grad, down_bias_grad = expert_grads(arrived, hidden, pre_grad)

    output, resid_grad, qkv_grad, weight_grad, phi_grad, vec_rows = back(
        residual, low_two, dispatch, combine, cotangent, returned, mixed, mixed_rest, qkv, lse,
        low_one, image_ids, vecs, phi, out_weight,
    )

    vec_rows = jnp.concatenate([vec_rows[:6], jnp.sum(sums, axis=0)[:2]], axis=0)
    flat = jnp.concatenate(
        [weight_grad.reshape(4 * width, width), phi_grad[:slots].astype(bf16), vec_rows.astype(bf16)]
    )
    share = -(-flat.shape[0] // devices)
    flat = jnp.pad(flat, ((0, share * devices - flat.shape[0]), (0, 0)))
    collected = exchange(flat.reshape(devices, share, width), axes)
    summed = jnp.sum(collected.astype(f32), axis=0)

    input_grad, ln1_rows = input_back(tokens, qkv_grad, resid_grad, vecs, qkv_weight)
    outgoing = jnp.concatenate([summed.astype(bf16), ln1_rows[:2].astype(bf16)])
    everything = exchange(jnp.broadcast_to(outgoing[None], (devices,) + outgoing.shape), axes)
    ln1_total = jnp.sum(everything[:, share:].astype(f32), axis=0)
    total = everything[:, :share].reshape(devices * share, width).astype(f32)
    weights = total[: 4 * width].reshape(4, width, width)
    qkv_weight_grad = weights[:3].transpose(1, 0, 2).reshape(width, 3 * width)
    phi_total = lax.dynamic_slice_in_dim(
        total, 4 * width + lax.axis_index("expert") * own, own, 0
    )
    rows = total[4 * width + slots :]
    squares = jnp.stack([jnp.sum(rows[6]), jnp.sum(rows[7]), jnp.sum(rows[5])])
    stream_rms = jnp.sqrt(squares / (devices * seqs * seq_len * width))
    return (
        output,
        input_grad,
        ln1_total[0],
        ln1_total[1],
        qkv_weight_grad,
        rows[0],
        rows[1],
        weights[3],
        rows[2],
        rows[3],
        rows[4],
        phi_total.T,
        up_grad,
        up_bias_grad,
        down_grad,
        down_bias_grad,
        stream_rms,
    )


def solution(mesh):
    split = P(("dp", "expert"), None, None)
    flat = P(("dp", "expert"), None)
    return jax.shard_map(
        local,
        mesh=mesh,
        in_specs=(
            split, flat, flat, P(), P(), P(), P(), P(), P(), P(), P(), P(),
            P(None, "expert"), P("expert", "dp", None), P("expert", "dp"),
            P("expert", "dp", None), P("expert", None), split,
        ),
        out_specs=(
            split, split, P(), P(), P(), P(), P(), P(), P(), P(), P(),
            P(None, "expert"), P("expert", "dp", None), P("expert", "dp"),
            P("expert", "dp", None), P("expert", None), P(),
        ),
        check_vma=False,
    )
```

time: 743 us -> 279 us (0.38); the launches traced: 734 us -> 278 us
  matrix products: 279 us -> 0 us
  Pallas kernels: 0 us -> 133 us
  waiting for transfers between devices: 169 us -> 72.4 us
  local copies, waits for them, and re-layouts: 111 us -> 32.4 us
  blocking collectives: 77.5 us -> 0 us
  other arithmetic: 48.1 us -> 7.62 us
  loops' own time: 16.8 us -> 0 us
  between operations: 14.9 us -> 0.84 us
  starting transfers between devices: 18.9 us -> 32.1 us
    dot_general x48 -> x0, matrix products: 278 us -> none  [the longest x4 78.2 us: attend_back(): jnp.einsum('hqk,qhd->khd', score_low, query_part, preferred_element_type=...]
    pallas_call x0 -> x6, Pallas kernels: none -> 133 us  [the longest x1 76.2 us: back(): pl.pallas_call(back_kernel, grid=(rows,), in_specs=[per_row(width), per_r...]
    psum x1 -> x0, waiting for transfers between devices: 130 us -> none  [local(): lax.psum((ln1_gain_grad, ln1_bias_grad, qkv_weight_grad, query_bias_grad,...]
    all_to_all x4 -> x5, waiting for transfers between devices: 8.18 us -> 72.4 us  [exchange(): return lax.all_to_all(values, over, split_axis=0, concat_axis=0, tiled=True)]
    psum x1 -> x0, blocking collectives: 39.2 us -> none  [local(): lax.psum((ln1_gain_grad, ln1_bias_grad, qkv_weight_grad, query_bias_grad,...]
    all_gather x3 -> x0, blocking collectives: 38.4 us -> none  [the longest x1 27.7 us: local(): phi_all = lax.all_gather(slot_params, 'expert', axis=1, tiled=True)]
    while x76 -> x0, local copies, waits for them, and re-layouts: 34.8 us -> none
    reduce_scatter x2 -> x0, waiting for transfers between devices: 30.7 us -> none  [the longest x1 16.2 us: local(): lax.psum_scatter(partial_out.astype(jnp.bfloat16), 'dp', scatter_dimensio...]
  transfers between devices with their start and end apart: 7 -> 5, of which waited for: 6 -> 4; matrix products, arithmetic and copies ran while one was open for 2% -> 3% of each run, Pallas kernels for 0% -> 17%
where the time goes in v1:
time: 279 us; the launch traced here: 278 us
  Pallas kernels  133 us (48%)
  waiting for transfers between devices  72.4 us (26%)
  local copies, waits for them, and re-layouts  32.4 us (12%)
  starting transfers between devices  32.1 us (12%)
  other arithmetic  7.62 us (3%)
    pallas_call x1, Pallas kernels, back(): pl.pallas_call(back_kernel, grid=(rows,), in_specs=[per_row(width), per_r...  76.2 us
    all_to_all x5, waiting for transfers between devices, exchange(): return lax.all_to_all(values, over, split_axis=0, concat_axis=0, tiled=True)  72.4 us
    pallas_call x1, Pallas kernels, attend(): pl.pallas_call(attend_kernel, grid=(rows,), in_specs=[per_row(width), who...  36.2 us
    all_to_all x5, starting transfers between devices, exchange(): return lax.all_to_all(values, over, split_axis=0, concat_axis=0, tiled=True)  32.1 us
    pallas_call x1, Pallas kernels, input_back(): pl.pallas_call(input_kernel, grid=(rows,), in_specs=[per_row(width), per_...  9.54 us
  transfers between devices with their start and end apart: 5, of which 4 were waited for; matrix products, arithmetic and copies ran while one was open for 3% of the time, Pallas kernels for 17%

profile of v1, /device:TPU:0, one launch (start us, length us, event | category | flops | bytes accessed | tf_op | source)
XLA Modules:
  0.0 277.8 jit_solution(2274552218928102843)
XLA Ops:
  0.7 1.3 broadcast_in_dim.6
  1.9 7.3 %all-to-all-start = ((bf16[8,2,384]{2,1,0:T(2,128)(2,1)}), bf16[8,2,384]{2,1,0:T(2,128)(2,1)S(1)}, u32[]{:S(2)}, u32[]{:S(2)}) async-start(bf16[8,2,384]{2,1,0:T(2,128)(2,1)} %broadcast_in_dim.6), calls=%async_computation | async-start | bytes 24576 | tf_op jit(solution)/shard_map/all_to_all | solution.py:640
  14.6 36.2 %attend.1 = (bf16[2,1024,384]{2,1,0:T(8,128)(2,1)}, bf16[2,1024,1152]{2,1,0:T(8,128)(2,1)}, bf16[2,1024,384]{2,1,0:T(8,128)(2,1)}, bf16[2,1024,384]{2,1,0:T(8,12...) custom-call(bf16[2,1024,384]{2,1,0:T(8,128)(2,1)} %tokens_ref.3, ...), custom_call_target="tpu_custom_call" | custom-call | flops 20000000000 | bytes 20000000 | tf_op jit(solution)/shard_map/attend/pallas_call | solution.py:214
  52.0 4.9 %route.1 = (f32[2,1024,128]{2,1,0:T(8,128)}, f32[2,1024,128]{2,1,0:T(8,128)}, bf16[2,2,16,384]{3,2,1,0:T(8,128)(2,1)}) custom-call(bf16[2,1024,384]{2,1,0:T(8,128)(2,1)} %get-tuple-element.44.low_two_ref, bf16[2,1024,384]{2,1,0:T(8,128)(2,1)} %cot_ref.3, s32[2,1024]{1,0:T(2,128)} %ids_ref.5, s32[2,128]{1,0:T(2,128)} %pad.12.slot_ref, ...), custom_call_target="tpu_custom_call" | custom-call | tf_op jit(solution)/shard_map/route/pallas_call | solution.py:277
  56.9 0.8 reshape.81
  57.9 0.8 reshape.82
  58.6 7.6 %all-to-all-start.1 = ((bf16[32,8,384]{2,1,0:T(8,128)(2,1)}), bf16[32,8,384]{2,1,0:T(8,128)(2,1)S(1)}, u32[]{:S(2)}, u32[]{:S(2)}) async-start(bf16[32,8,384]{2,1,0:T(8,128)(2,1)} %reshape.82), calls=%async_computation.1 | async-start | bytes 393216 | tf_op jit(solution)/shard_map/all_to_all | solution.py:640
  66.8 8.0 %all-to-all-done.1 = bf16[32,8,384]{2,1,0:T(8,128)(2,1)S(1)} async-done(((bf16[32,8,384]{2,1,0:T(8,128)(2,1)}), bf16[32,8,384]{2,1,0:T(8,128)(2,1)S(1)}, u32[]{:S(2)}, u32[]{:S(2)}) %all-to-all-start.1) | async-done | bytes 196640 | tf_op jit(solution)/shard_map/all_to_all | solution.py:640
  75.7 2.8 %experts.1 = (bf16[2,2,64,384]{3,2,1,0:T(8,128)(2,1)}, bf16[2,64,384]{2,1,0:T(8,128)(2,1)}, bf16[2,64,384]{2,1,0:T(8,128)(2,1)}) custom-call(bf16[2,2,64,384]{3,2,1,0:T(8,128)(2,1)} %reshape.84.rows_ref, bf16[2,384,384]{2,1,0:T(8,128)(2,1)} %up_ref.1, bf16[2,384]{1,0:T(2,128)(2,1)} %up_bias_ref.1, bf16[2,384,384]{2,1,0:T(8,128)(2,1)} %down_ref.1, ...), custom_call_target="tpu_custom_call" | custom-call | tf_op jit(solution)/shard_map/experts/pallas_call | solution.py:332
  78.6 1.0 reshape.85
  80.4 3.2 %all-to-all-start.2 = ((bf16[32,8,384]{2,1,0:T(8,128)(2,1)}), bf16[32,8,384]{2,1,0:T(8,128)(2,1)S(1)}, u32[]{:S(2)}, u32[]{:S(2)}) async-start(bf16[32,8,384]{2,1,0:T(8,128)(2,1)} %copy.47), calls=%async_computation.2 | async-start | bytes 393216 | tf_op jit(solution)/shard_map/all_to_all | solution.py:640
  83.6 8.3 %all-to-all-done.2 = bf16[32,8,384]{2,1,0:T(8,128)(2,1)S(1)} async-done(((bf16[32,8,384]{2,1,0:T(8,128)(2,1)}), bf16[32,8,384]{2,1,0:T(8,128)(2,1)S(1)}, u32[]{:S(2)}, u32[]{:S(2)}) %all-to-all-start.2) | async-done | bytes 196640 | tf_op jit(solution)/shard_map/all_to_all | solution.py:640
  92.9 76.2 %back.1 = (bf16[2,1024,384]{2,1,0:T(8,128)(2,1)}, f32[2,1024,384]{2,1,0:T(8,128)}, bf16[2,1024,1152]{2,1,0:T(8,128)(2,1)}, bf16[4,384,384]{2,1,0:T(8,128)(2,1)}, f32[128,384]{1,0:T(8,128)}, /*index=5*/f32[8,384]{1,0:T(8,128)}) custom-call(f32[2,1024,384]{2,1,0:T(8,128)} %get-tuple-element.43.residual_ref, ...), custom_call_target="tpu_custom_call" | custom-call | flops 60000002048 | bytes 20000000 | tf_op jit(solution)/shard_map/back/pallas_call | solution.py:531
  170.6 4.8 %concatenate.9 = bf16[1560,384]{1,0:T(8,128)(2,1)S(1)} concatenate(bf16[1536,384]{1,0:T(8,128)(2,1)} %bitcast.27, bf16[16,384]{1,0:T(8,128)(2,1)S(1)} %slice.127, bf16[6,384]{1,0:T(8,128)(2,1)S(1)} %slice.128, bf16[2,384]{1,0:T(2,128)(2,1)S(1)} %slice.130), dimensions={0} | concatenate | bytes 2396160 | tf_op jit(solution)/shard_map/concatenate | solution.py:676
  175.5 1.3 reshape.90
  176.8 10.7 %all-to-all-start.3 = ((bf16[32,49,384]{2,1,0:T(8,128)(2,1)}), bf16[32,49,384]{2,1,0:T(8,128)(2,1)S(1)}, u32[]{:S(2)}, u32[]{:S(2)}) async-start(bf16[32,49,384]{2,1,0:T(8,128)(2,1)} %reshape.90), calls=%async_computation.3 | async-start | bytes 2752512 | tf_op jit(solution)/shard_map/all_to_all | solution.py:640
  187.5 9.5 %input_back.1 = (bf16[2,1024,384]{2,1,0:T(8,128)(2,1)}, f32[8,384]{1,0:T(8,128)}) custom-call(bf16[2,1024,384]{2,1,0:T(8,128)(2,1)} %tokens_ref.3, bf16[2,1024,1152]{2,1,0:T(8,128)(2,1)} %get-tuple-element.55.qkv_grad_ref, f32[2,1024,384]{2,1,0:T(8,128)} %get-tuple-element.56.resid_grad_ref, f32[8,384]{1,0:T(8,128)} %stack.44.vecs_ref, ...), custom_call_target="tpu_custom_call" | custom-call | flops 6000000000 | bytes 10000000 | tf_op jit(solution)/shard_map/input_back/pallas_call | solution.py:606
  197.7 24.4 %all-to-all-done.3 = bf16[32,49,384]{2,1,0:T(8,128)(2,1)S(1)} async-done(((bf16[32,49,384]{2,1,0:T(8,128)(2,1)}), bf16[32,49,384]{2,1,0:T(8,128)(2,1)S(1)}, u32[]{:S(2)}, u32[]{:S(2)}) %all-to-all-start.3) | async-done | bytes 1204256 | tf_op jit(solution)/shard_map/all_to_all | solution.py:640
  222.3 1.2 broadcast_in_dim.8
  223.5 3.4 %all-to-all-start.4 = ((bf16[32,51,384]{2,1,0:T(8,128)(2,1)}), bf16[32,51,384]{2,1,0:T(8,128)(2,1)}, u32[]{:S(2)}, u32[]{:S(2)}) async-start(bf16[32,51,384]{2,1,0:T(8,128)(2,1)} %broadcast_in_dim.8), calls=%async_computation.4 | async-start | bytes 2752512 | tf_op jit(solution)/shard_map/all_to_all | solution.py:640
  226.9 2.9 %expert_grads.1 = (f32[2,384,384]{2,1,0:T(8,128)}, f32[2,384]{1,0:T(2,128)}, f32[2,384,384]{2,1,0:T(8,128)}, f32[2,384]{1,0:T(2,128)}) custom-call(bf16[2,2,64,384]{3,2,1,0:T(8,128)(2,1)} %reshape.84.rows_ref, bf16[2,64,384]{2,1,0:T(8,128)(2,1)} %get-tuple-element.63.hidden_ref, bf16[2,64,384]{2,1,0:T(8,128)(2,1)} %get-tuple-element.64.pre_grad_ref), custom_call_target="tpu_custom_call" | custom-call | flops 75497472 | bytes 4000000 | tf_op jit(solution)/shard_map/expert_grads/pallas_call | solution.py:344
  229.8 31.7 %all-to-all-done.4 = bf16[32,51,384]{2,1,0:T(8,128)(2,1)} async-done(((bf16[32,51,384]{2,1,0:T(8,128)(2,1)}), bf16[32,51,384]{2,1,0:T(8,128)(2,1)}, u32[]{:S(2)}, u32[]{:S(2)}) %all-to-all-start.4) | async-done | bytes 1253408 | tf_op jit(solution)/shard_map/all_to_all | solution.py:640
  261.5 1.5 slice_convert_fusion
  263.0 1.7 reshape.92
  264.7 1.9 slice.104
  266.6 1.6 slice.101
  268.2 1.3 dynamic-slice_bitcast_fusion
  269.5 1.0 convert_reduce_fusion
  270.5 1.9 slice_reduce_fusion.2
  272.4 1.2 copy.50
  273.6 1.9 copy.51
  275.5 2.4 fusion
  (37 shorter events, 12.5 us)
Async XLA Ops:
  1.9 49.4 %all-to-all-start = ((bf16[8,2,384]{2,1,0:T(2,128)(2,1)}), bf16[8,2,384]{2,1,0:T(2,128)(2,1)S(1)}, u32[]{:S(2)}, u32[]{:S(2)}) async-start(bf16[8,2,384]{2,1,0:T(2,128)(2,1)} %broadcast_in_dim.6), calls=%async_computation | async-start | bytes 24576 | tf_op jit(solution)/shard_map/all_to_all | solution.py:640
  14.6 36.2 %copy-start.2 = (s32[2,16]{1,0:T(2,128)S(1)}, s32[2,16]{1,0:T(2,128)}, u32[]{:S(2)}) copy-start(s32[2,16]{1,0:T(2,128)} %param.20) | copy-start | bytes 388
  52.0 14.2 %copy-start.1 = (f32[2,384]{1,0:T(2,128)S(1)}, f32[2,384]{1,0:T(2,128)}, u32[]{:S(2)}) copy-start(f32[2,384]{1,0:T(2,128)} %param.34) | copy-start | bytes 9220
  58.6 16.1 %all-to-all-start.1 = ((bf16[32,8,384]{2,1,0:T(8,128)(2,1)}), bf16[32,8,384]{2,1,0:T(8,128)(2,1)S(1)}, u32[]{:S(2)}, u32[]{:S(2)}) async-start(bf16[32,8,384]{2,1,0:T(8,128)(2,1)} %reshape.82), calls=%async_computation.1 | async-start | bytes 393216 | tf_op jit(solution)/shard_map/all_to_all | solution.py:640
  75.7 7.8 %copy-start = (f32[2,8,384]{2,1,0:T(8,128)S(1)}, f32[2,8,384]{2,1,0:T(8,128)}, u32[]{:S(2)}) copy-start(f32[2,8,384]{2,1,0:T(8,128)} %get-tuple-element.61) | copy-start | bytes 73732
  80.4 11.6 %all-to-all-start.2 = ((bf16[32,8,384]{2,1,0:T(8,128)(2,1)}), bf16[32,8,384]{2,1,0:T(8,128)(2,1)S(1)}, u32[]{:S(2)}, u32[]{:S(2)}) async-start(bf16[32,8,384]{2,1,0:T(8,128)(2,1)} %copy.47), calls=%async_computation.2 | async-start | bytes 393216 | tf_op jit(solution)/shard_map/all_to_all | solution.py:640
  176.8 45.3 %all-to-all-start.3 = ((bf16[32,49,384]{2,1,0:T(8,128)(2,1)}), bf16[32,49,384]{2,1,0:T(8,128)(2,1)S(1)}, u32[]{:S(2)}, u32[]{:S(2)}) async-start(bf16[32,49,384]{2,1,0:T(8,128)(2,1)} %reshape.90), calls=%async_computation.3 | async-start | bytes 2752512 | tf_op jit(solution)/shard_map/all_to_all | solution.py:640
  223.5 38.0 %all-to-all-start.4 = ((bf16[32,51,384]{2,1,0:T(8,128)(2,1)}), bf16[32,51,384]{2,1,0:T(8,128)(2,1)}, u32[]{:S(2)}, u32[]{:S(2)}) async-start(bf16[32,51,384]{2,1,0:T(8,128)(2,1)} %broadcast_in_dim.8), calls=%async_computation.4 | async-start | bytes 2752512 | tf_op jit(solution)/shard_map/all_to_all | solution.py:640

commit v2 on v1

v2 whole, which is shorter than its diff:
```python
import jax
import jax.numpy as jnp
from jax import lax
from jax.experimental import pallas as pl
from jax.experimental.pallas import tpu as pltpu
from jax.sharding import Mesh
from jax.sharding import PartitionSpec as P

HEADS = 6
IMAGES = 6
EPSILON = 1e-06
MASKED = -1e30
LANES = 128
TILE = 256
SAFE = 60.0
PIECE = 16
VMEM_BYTES = 60 * 1024 * 1024

bf16 = jnp.bfloat16
f32 = jnp.float32

NN = (((1,), (0,)), ((), ()))
NT = (((1,), (1,)), ((), ()))
TN = (((0,), (0,)), ((), ()))


def dot(left, right, dims=NN):
    return lax.dot_general(left, right, dims, preferred_element_type=f32)


def lane_ids(rows):
    return lax.broadcasted_iota(jnp.int32, (rows, LANES), 1)


def norm_parts(values):
    width = values.shape[-1]
    centre = values - jnp.sum(values, axis=-1, keepdims=True) * (1.0 / width)
    power = jnp.sum(centre * centre, axis=-1, keepdims=True) * (1.0 / width)
    recip = lax.rsqrt(power + EPSILON)
    return centre * recip, recip


def norm_back(grad, hat, recip, gain):
    width = grad.shape[-1]
    scaled = grad * gain
    first = jnp.sum(scaled, axis=-1, keepdims=True) * (1.0 / width)
    second = jnp.sum(scaled * hat, axis=-1, keepdims=True) * (1.0 / width)
    return recip * (scaled - first - hat * second)


def image_columns(id_row):
    return jnp.transpose(jnp.broadcast_to(id_row.astype(f32), (LANES, id_row.shape[1])))


def image_starts(id_row):
    as_float = id_row.astype(f32)
    return [
        jnp.sum(jnp.where(as_float < float(v), 1.0, 0.0)).astype(jnp.int32)
        for v in range(1, IMAGES)
    ]


def key_tiles(starts, seq_len, list_ref):
    total = 0
    for i in range(seq_len // TILE):
        begin, count = key_window(starts, i, seq_len)

        def note(j, carry, i=i, begin=begin, total=total):
            list_ref[0, total + j] = i
            list_ref[1, total + j] = begin + j * TILE
            return carry

        lax.fori_loop(0, count, note, 0)
        total = total + count
    return total


def head_picker(width):
    head = lax.broadcasted_iota(jnp.int32, (width, LANES), 0) // (width // HEADS)
    return jnp.where(head == lax.broadcasted_iota(jnp.int32, (width, LANES), 1), 1.0, 0.0).astype(
        bf16
    )


def as_row(ref):
    return ref[...].reshape(1, ref.shape[0])


def selector(rows, columns, wanted):
    row = lax.broadcasted_iota(jnp.int32, (rows, columns), 0)
    column = lax.broadcasted_iota(jnp.int32, (rows, columns), 1)
    return jnp.where(column == wanted(row), 1.0, 0.0).astype(bf16)


def key_window(starts, tile, seq_len):
    first, last = tile * TILE, tile * TILE + TILE - 1
    low, high = 0, seq_len
    for s in starts:
        low = jnp.maximum(low, jnp.where(s <= first, s, 0))
        high = jnp.minimum(high, jnp.where(s > last, s, seq_len))
    low = lax.div(low, LANES) * LANES
    count = lax.div(high - low + (TILE - 1), TILE)
    low = jnp.minimum(low, seq_len - count * TILE)
    return low, count


def query_marks(columns, lanes):
    return jnp.where(columns == (lanes - 24).astype(f32), 1.0, 0.0)


def key_marks(columns, lanes):
    other = jnp.where(columns == (lanes - 24).astype(f32), 0.0, MASKED)
    inside = jnp.logical_and(lanes >= 24, lanes < 24 + IMAGES)
    return jnp.where(inside, other, jnp.where(lanes < 24, 1.0, 0.0))


def three_parts(values, lanes):
    values = jnp.where(lanes < 8, values, 0.0)
    top = values.astype(bf16).astype(f32)
    rest = values - top
    mid = rest.astype(bf16).astype(f32)
    low = (rest - mid).astype(bf16).astype(f32)
    return top + pltpu.roll(mid, 8, 1) + pltpu.roll(low, 16, 1)


def own_lanes(values, lanes, head):
    keep = jnp.logical_or(lanes >= 24, lax.rem(lanes, 8) == head)
    return jnp.where(keep, values, 0.0)


def attend_kernel(
    tokens_ref, ids_ref, gain1_ref, shift1_ref, q_bias_ref, v_bias_ref, qkv_w_ref, out_w_ref,
    out_bias_ref, gain2_ref, shift2_ref,
    low_one_ref, qkv_ref, mixed_ref, mixed_rest_ref, lse_ref, residual_ref, low_two_ref, sums_ref,
    q_scr, k_scr, v_scr, s_scr, top_scr, acc_scr, p_scr, list_scr,
):
    row = pl.program_id(0)
    seq_len, width = tokens_ref.shape[1:]
    pairs = width // LANES
    tiles = seq_len // TILE
    scale = (width // HEADS) ** -0.5
    id_row = ids_ref[pl.ds(row, 1), :]
    starts = image_starts(id_row)
    total_tiles = key_tiles(starts, seq_len, list_scr)
    columns = image_columns(id_row)
    lanes = lane_ids(seq_len)
    left = lanes < LANES // 2
    marks_q = query_marks(columns, lanes).astype(bf16)
    marks_k = key_marks(columns, lanes).astype(bf16)

    stream = tokens_ref[0].astype(f32)
    hat, _ = norm_parts(stream)
    low_one = (hat * as_row(gain1_ref) + as_row(shift1_ref)).astype(bf16)
    low_one_ref[0] = low_one
    projected = dot(low_one, qkv_w_ref[...])
    query = (projected[:, :width] + as_row(q_bias_ref)).astype(bf16)
    key = projected[:, width : 2 * width].astype(bf16)
    value = (projected[:, 2 * width :] + as_row(v_bias_ref)).astype(bf16)
    qkv_ref[0, :, :width] = query
    qkv_ref[0, :, width : 2 * width] = key
    qkv_ref[0, :, 2 * width :] = value
    for p in range(pairs):
        cut = slice(p * LANES, (p + 1) * LANES)
        scaled = query[:, cut].astype(f32) * scale
        v_pair = value[:, cut].astype(f32)
        k_scr[p, :, :LANES] = key[:, cut]
        k_scr[p, :, LANES:] = marks_k
        v_scr[2 * p] = jnp.where(left, v_pair, 1.0).astype(bf16)
        v_scr[2 * p + 1] = jnp.where(left, 1.0, v_pair).astype(bf16)
        for odd in range(2):
            own = jnp.where(left, 0.0, scaled) if odd else jnp.where(left, scaled, 0.0)
            own = own.astype(bf16)
            for t in range(tiles):
                q_scr[p, t, odd, :, :LANES] = own[t * TILE : (t + 1) * TILE]
                q_scr[p, t, odd, :, LANES:] = marks_q[t * TILE : (t + 1) * TILE]
    acc_scr[...] = jnp.zeros_like(acc_scr)
    lse_ref[...] = jnp.zeros_like(lse_ref)

    picker = head_picker(width)

    def longest(low):
        wide = low.astype(f32)
        return jnp.max(dot((wide * wide).astype(bf16), picker), axis=0, keepdims=True)

    bound = jnp.max(longest(query) * longest(key)) * (scale * scale)
    small = bound <= SAFE * SAFE

    @pl.when(small)
    def _():
        def tile(n, carry):
            i = list_scr[0, n]
            at = pl.ds(pl.multiple_of(i * TILE, TILE), TILE)
            keys = pl.ds(pl.multiple_of(list_scr[1, n], LANES), TILE)
            for p in range(pairs):
                q2 = q_scr[p, i].reshape(2 * TILE, 2 * LANES)
                p_scr[p] = jnp.exp(dot(q2, k_scr[p, keys, :], NT)).astype(bf16)
            for h in range(HEADS):
                part = slice((h % 2) * TILE, (h % 2 + 1) * TILE)
                acc_scr[h, at, :] += dot(p_scr[h // 2, part, :], v_scr[h, keys, :])
            return carry

        lax.fori_loop(0, total_tiles, tile, 0)

    @pl.when(jnp.logical_not(small))
    def _():
        def query_tile(i, carry):
            at = pl.ds(pl.multiple_of(i * TILE, TILE), TILE)
            begin, count = key_window(starts, i, seq_len)
            top_scr[...] = jnp.full_like(top_scr, -3e38)

            def scores(j, inner):
                keys = pl.ds(pl.multiple_of(begin + j * TILE, LANES), TILE)
                for p in range(pairs):
                    q2 = q_scr[p, i].reshape(2 * TILE, 2 * LANES)
                    s = dot(q2, k_scr[p, keys, :], NT)
                    s_scr[j, p] = s
                    best = s[:, :LANES]
                    for o in range(LANES, TILE, LANES):
                        best = jnp.maximum(best, s[:, o : o + LANES])
                    top_scr[p] = jnp.maximum(top_scr[p], best)
                return inner

            lax.fori_loop(0, count, scores, 0)
            tile_lanes = lane_ids(TILE)
            lse = jnp.zeros((TILE, LANES), f32)
            for p in range(pairs):
                top = jnp.broadcast_to(
                    jnp.max(top_scr[p], axis=-1, keepdims=True), top_scr.shape[1:]
                )
                top_scr[p] = top
                lse = jnp.where(tile_lanes == 2 * p, top[:TILE], lse)
                lse = jnp.where(tile_lanes == 2 * p + 1, top[TILE:], lse)
            lse_ref[0, at, :] = lse

            def weigh(j, inner):
                keys = pl.ds(pl.multiple_of(begin + j * TILE, LANES), TILE)
                for p in range(pairs):
                    top = jnp.concatenate([top_scr[p]] * (TILE // LANES), axis=1)
                    p_scr[p] = jnp.exp(s_scr[j, p] - top).astype(bf16)
                for h in range(HEADS):
                    part = slice((h % 2) * TILE, (h % 2 + 1) * TILE)
                    acc_scr[h, at, :] += dot(p_scr[h // 2, part, :], v_scr[h, keys, :])
                return inner

            lax.fori_loop(0, count, weigh, 0)
            return carry

        lax.fori_loop(0, tiles, query_tile, 0)

    lse = lse_ref[0]
    for p in range(pairs):
        even, odd = acc_scr[2 * p], acc_scr[2 * p + 1]
        swapped = jnp.where(left, odd, even)
        sums = pltpu.roll(swapped, LANES // 2, 1)
        mixed = jnp.where(left, even, odd) / sums
        lse += jnp.where(lanes == 2 * p, jnp.log(sums), 0.0)
        lse += jnp.where(lanes == 2 * p + 1, jnp.log(swapped), 0.0)
        low = mixed.astype(bf16)
        mixed_ref[0, :, p * LANES : (p + 1) * LANES] = low
        mixed_rest_ref[0, :, p * LANES : (p + 1) * LANES] = (mixed - low.astype(f32)).astype(bf16)
    lse_ref[0] = lse
    branch = dot(mixed_ref[0], out_w_ref[...]) + as_row(out_bias_ref)
    residual = tokens_ref[0].astype(f32) + branch
    residual_ref[0] = residual
    hat_two, _ = norm_parts(residual)
    low_two_ref[0] = (hat_two * as_row(gain2_ref) + as_row(shift2_ref)).astype(bf16)
    stream = tokens_ref[0].astype(f32)
    sums_ref[0] = jnp.concatenate(
        [
            jnp.sum(stream * stream, axis=0, keepdims=True),
            jnp.sum(branch * branch, axis=0, keepdims=True),
            jnp.zeros((6, width), f32),
        ],
        axis=0,
    )


def whole(*shape):
    return pl.BlockSpec(shape, lambda r: (0,) * len(shape))


def per_row(seq_len, width):
    return pl.BlockSpec((1, seq_len, width), lambda r: (r, 0, 0))


def params():
    return pltpu.CompilerParams(vmem_limit_bytes=VMEM_BYTES)


def attend(
    tokens, image_ids, gain1, shift1, q_bias, v_bias, qkv_weight, out_weight, out_bias, gain2, shift2
):
    rows, seq_len, width = tokens.shape
    pairs, tiles = width // LANES, seq_len // TILE
    block = lambda lanes: per_row(seq_len, lanes)
    shape = lambda lanes, kind: jax.ShapeDtypeStruct((rows, seq_len, lanes), kind)
    return pl.pallas_call(
        attend_kernel,
        grid=(rows,),
        in_specs=[
            block(width), whole(rows, seq_len), whole(width), whole(width), whole(width),
            whole(width), whole(width, 3 * width), whole(width, width), whole(width),
            whole(width), whole(width),
        ],
        out_specs=[
            block(width), block(3 * width), block(width), block(width), block(LANES),
            block(width), block(width), pl.BlockSpec((1, 8, width), lambda r: (r, 0, 0)),
        ],
        out_shape=[
            shape(width, bf16), shape(3 * width, bf16), shape(width, bf16), shape(width, bf16),
            shape(LANES, f32), shape(width, f32), shape(width, bf16),
            jax.ShapeDtypeStruct((rows, 8, width), f32),
        ],
        scratch_shapes=[
            pltpu.VMEM((pairs, tiles, 2, TILE, 2 * LANES), bf16),
            pltpu.VMEM((pairs, seq_len, 2 * LANES), bf16),
            pltpu.VMEM((HEADS, seq_len, LANES), bf16),
            pltpu.VMEM((tiles, pairs, 2 * TILE, TILE), f32),
            pltpu.VMEM((pairs, 2 * TILE, LANES), f32),
            pltpu.VMEM((HEADS, seq_len, LANES), f32),
            pltpu.VMEM((pairs, 2 * TILE, TILE), bf16),
            pltpu.SMEM((2, tiles * tiles), jnp.int32),
        ],
        cost_estimate=pl.CostEstimate(
            flops=20 * 10**9, bytes_accessed=20 * 10**6, transcendentals=10**7
        ),
        compiler_params=params(),
        name="attend",
    )(
        tokens, image_ids, gain1, shift1, q_bias, v_bias, qkv_weight, out_weight, out_bias, gain2,
        shift2,
    )


def padded_phi(phi_ref, lanes):
    slots, width = phi_ref.shape
    phi = phi_ref[...]
    if lanes > slots:
        phi = jnp.concatenate([phi, jnp.zeros((lanes - slots, width), bf16)], axis=0)
    return phi


def route_kernel(
    low_two_ref, cot_ref, ids_ref, slot_ref, phi_ref, dispatch_ref, combine_ref, sent_ref, slots_scr
):
    row = pl.program_id(0)
    rows, slots = slot_ref.shape
    lanes = dispatch_ref.shape[2]
    dp, ep, per_device, width = sent_ref.shape
    own = slots // ep
    columns = image_columns(ids_ref[pl.ds(row, 1), :])
    if lanes > LANES:
        columns = jnp.concatenate([columns] * (lanes // LANES), axis=1)
    slot_row = dot(
        slot_ref[pl.ds(row, 1), :].astype(bf16), selector(slots, lanes, lambda r: r)
    )
    slot_row = jnp.where(
        lax.broadcasted_iota(jnp.int32, (1, lanes), 1) < slots, slot_row, -1.0
    )
    allowed = columns == slot_row
    low_two = low_two_ref[0]
    logits = jnp.where(allowed, dot(low_two, padded_phi(phi_ref, lanes), NT), MASKED)

    def select(axis):
        top = jnp.max(logits, axis=axis, keepdims=True)
        weights = jnp.where(allowed, jnp.exp(logits - top), 0.0)
        total = jnp.sum(weights, axis=axis, keepdims=True)
        return weights / jnp.where(total == 0.0, 1.0, total)

    dispatch = select(0)
    combine = select(1)
    dispatch_ref[0] = dispatch
    combine_ref[0] = combine
    slots_scr[row, 0] = dot(dispatch.astype(bf16), low_two, TN)[:slots].astype(bf16)
    slots_scr[row, 1] = dot(combine.astype(bf16), cot_ref[0], TN)[:slots].astype(bf16)

    @pl.when(row == rows - 1)
    def _():
        count = ep * per_device

        def source(n):
            device, rest = n // per_device, n % per_device
            return (rest // own) * slots + device * own + rest % own

        flat = slots_scr[...].reshape(rows * 2 * slots, width)
        moved = dot(selector(count, rows * 2 * slots, source), flat)
        moved = moved.reshape(ep, per_device, width).astype(bf16)
        for d in range(dp):
            sent_ref[d] = moved


def route(low_two, cotangent, image_ids, slot_image, phi, dp, ep):
    rows, seq_len, width = low_two.shape
    slots = slot_image.shape[1]
    lanes = -(-slots // LANES) * LANES
    per_device = rows * 2 * slots // ep
    block = lambda n: per_row(seq_len, n)
    return pl.pallas_call(
        route_kernel,
        grid=(rows,),
        in_specs=[
            block(width), block(width), whole(rows, seq_len), whole(rows, slots),
            whole(slots, width),
        ],
        out_specs=[block(lanes), block(lanes), whole(dp, ep, per_device, width)],
        out_shape=[
            jax.ShapeDtypeStruct((rows, seq_len, lanes), f32),
            jax.ShapeDtypeStruct((rows, seq_len, lanes), f32),
            jax.ShapeDtypeStruct((dp, ep, per_device, width), bf16),
        ],
        scratch_shapes=[pltpu.VMEM((rows, 2, slots, width), bf16)],
        compiler_params=params(),
        name="route",
    )(low_two, cotangent, image_ids, slot_image, phi)


def expert_kernel(
    arrived_ref, up_ref, up_bias_ref, down_ref, down_bias_ref,
    parts_ref, rows_ref, hidden_ref, pre_grad_ref, parts_scr,
):
    devices, per_device, width = arrived_ref.shape
    own, units, _ = up_ref.shape
    seqs = per_device // (2 * own)
    group = min(devices, TILE // per_device)
    count = group * per_device
    part = seqs * group

    def arrived_at(n):
        which, place = n // part, n % part
        return (place % group) * per_device + (place // group) * 2 * own + (
            which % 2
        ) * own + which // 2

    def sent_at(n):
        device, rest = n // per_device, n % per_device
        which = (rest % own) * 2 + rest // own % 2
        return which * part + rest // (2 * own) * group + device

    order = selector(count, count, arrived_at)
    for g in range(devices // group):
        flat = arrived_ref[g * group : (g + 1) * group].astype(f32).reshape(count, width)
        moved = dot(order, flat.astype(bf16)).astype(bf16)
        for n in range(2 * own):
            rows_ref[n // 2, n % 2, g * part : (g + 1) * part, :] = moved[n * part : (n + 1) * part]
    for e in range(own):
        slot_in, out_grad = rows_ref[e, 0], rows_ref[e, 1]
        up, down = up_ref[e], down_ref[e]
        pre_act = dot(slot_in, up, NT) + up_bias_ref[e : e + 1, :].astype(f32)
        cdf = 0.5 * (1.0 + lax.erf(pre_act * 0.7071067811865476))
        density = jnp.exp(-0.5 * pre_act * pre_act) * 0.3989422804014327
        hidden = (pre_act * cdf).astype(bf16)
        pre_grad = (dot(out_grad, down, NT) * (cdf + pre_act * density)).astype(bf16)
        hidden_ref[e] = hidden
        pre_grad_ref[e] = pre_grad
        parts_scr[e, 0] = (dot(hidden, down) + down_bias_ref[e : e + 1, :]).astype(bf16)
        parts_scr[e, 1] = dot(pre_grad, up).astype(bf16)
    order = selector(count, count, sent_at)
    for g in range(devices // group):
        flat = jnp.concatenate(
            [parts_scr[n // 2, n % 2, g * part : (g + 1) * part, :] for n in range(2 * own)], axis=0
        )
        moved = dot(order, flat).reshape(group, per_device, width)
        parts_ref[g * group : (g + 1) * group] = moved.astype(bf16)


def expert_grad_kernel(
    rows_ref, hidden_ref, pre_grad_ref, up_grad_ref, up_bias_grad_ref, down_grad_ref,
    down_bias_grad_ref,
):
    for e in range(rows_ref.shape[0]):
        slot_in, out_grad = rows_ref[e, 0], rows_ref[e, 1]
        pre_grad = pre_grad_ref[e]
        down_grad_ref[e] = dot(hidden_ref[e], out_grad, TN)
        up_grad_ref[e] = dot(pre_grad, slot_in, TN)
        up_bias_grad_ref[e : e + 1, :] = jnp.sum(pre_grad.astype(f32), axis=0, keepdims=True)
        down_bias_grad_ref[e : e + 1, :] = jnp.sum(out_grad.astype(f32), axis=0, keepdims=True)


def experts(arrived, up_weight, up_bias, down_weight, down_bias_part):
    devices, per_device, width = arrived.shape
    own, units, _ = up_weight.shape
    count = devices * per_device // (2 * own)
    low = lambda *shape: jax.ShapeDtypeStruct(shape, bf16)
    return pl.pallas_call(
        expert_kernel,
        out_shape=[
            low(*arrived.shape), low(own, 2, count, width), low(own, count, units),
            low(own, count, units),
        ],
        scratch_shapes=[pltpu.VMEM((own, 2, count, width), bf16)],
        compiler_params=params(),
        name="experts",
    )(arrived, up_weight, up_bias, down_weight, down_bias_part)


def expert_grads(rows, hidden, pre_grad):
    own, _, count, width = rows.shape
    units = hidden.shape[-1]
    full = lambda *shape: jax.ShapeDtypeStruct(shape, f32)
    return pl.pallas_call(
        expert_grad_kernel,
        out_shape=[
            full(own, units, width), full(own, units), full(own, units, width), full(own, width),
        ],
        cost_estimate=pl.CostEstimate(
            flops=4 * own * count * units * width, bytes_accessed=4 * 10**6, transcendentals=0
        ),
        compiler_params=params(),
        name="expert_grads",
    )(rows, hidden, pre_grad)


def back_kernel(
    core_ref, residual_ref, low_two_ref, dispatch_ref, combine_ref, cot_ref, back_ref, mixed_ref,
    mixed_rest_ref, qkv_ref, lse_ref, low_one_ref, sums_ref, ids_ref, gain2_ref, phi_ref, out_w_ref,
    output_ref, resid_grad_ref, qkv_grad_ref, mine_ref, other_ref,
    logit_scr, branch_scr, mixed_grad_scr, q_scr, k_scr, o_scr, v_scr, dq_scr, dk_scr, dv_scr,
    grad_scr, p_scr, ds_scr, phi_grad_scr, rows_scr, list_scr,
):
    row = pl.program_id(0)
    seq_len, width = residual_ref.shape[1:]
    pairs, tiles = width // LANES, seq_len // TILE
    scale = (width // HEADS) ** -0.5
    lanes_all = lane_ids(seq_len)
    slots = phi_ref.shape[0]
    slot_lanes = dispatch_ref.shape[2]

    @pl.when(row == 0)
    def _():
        grad_scr[...] = jnp.zeros_like(grad_scr)
        phi_grad_scr[...] = jnp.zeros_like(phi_grad_scr)
        rows_scr[...] = jnp.zeros_like(rows_scr)

    id_row = ids_ref[pl.ds(row, 1), :]
    starts = image_starts(id_row)
    total_tiles = key_tiles(starts, seq_len, list_scr)

    dp, ep, per_device, _ = back_ref.shape
    own = slots // ep
    held = back_ref[0].astype(f32)
    for d in range(1, dp):
        held += back_ref[d].astype(f32)
    held = held.reshape(ep * per_device, width).astype(bf16)

    def of_kind(kind):
        def wanted(slot):
            place = slot // own * per_device + (row * 2 + kind) * own + slot % own
            return jnp.where(slot < slots, place, -1)

        return dot(selector(slot_lanes, ep * per_device, wanted), held).astype(bf16)

    expert_out = of_kind(0)
    slot_grad = of_kind(1)
    phi = padded_phi(phi_ref, slot_lanes)
    combine, dispatch = combine_ref[0], dispatch_ref[0]
    cot = cot_ref[0]
    low_two = low_two_ref[0]
    moe_out = dot(combine.astype(bf16), expert_out)
    output_ref[0] = (residual_ref[0] + moe_out).astype(bf16)
    moe_sq = jnp.sum(moe_out * moe_out, axis=0, keepdims=True)
    combine_grad = dot(cot, expert_out, NT)
    dispatch_grad = dot(low_two, slot_grad, NT)
    logit_grad = combine * (
        combine_grad - jnp.sum(combine * combine_grad, axis=1, keepdims=True)
    ) + dispatch * (dispatch_grad - jnp.sum(dispatch * dispatch_grad, axis=0, keepdims=True))
    logit_scr[...] = logit_grad.astype(bf16)
    phi_grad_scr[...] += dot(logit_scr[...], low_two, TN)

    grad = dot(dispatch.astype(bf16), slot_grad) + dot(logit_scr[...], phi)
    hat, recip = norm_parts(residual_ref[0])
    resid = cot.astype(f32) + norm_back(grad, hat, recip, as_row(gain2_ref))
    gain_sum = jnp.sum(grad * hat, axis=0, keepdims=True)
    shift_sum = jnp.sum(grad, axis=0, keepdims=True)
    resid_grad_ref[0] = resid
    branch_scr[...] = resid.astype(bf16)
    bias_sum = jnp.sum(branch_scr[...].astype(f32), axis=0, keepdims=True)
    mixed_grad_scr[...] = dot(branch_scr[...], out_w_ref[...], NT).astype(bf16)
    grad_scr[:, 3 * width :] += dot(mixed_ref[0], branch_scr[...], TN)
    product = (mixed_ref[0].astype(f32) + mixed_rest_ref[0].astype(f32)) * mixed_grad_scr[
        ...
    ].astype(f32)
    product_top = product.astype(bf16)
    picker = head_picker(width)
    row_dots = dot(product_top, picker) + dot(
        (product - product_top.astype(f32)).astype(bf16), picker
    )

    columns = image_columns(id_row)
    left = lanes_all < LANES // 2
    marks_q = query_marks(columns, lanes_all) - three_parts(lse_ref[0], lanes_all)
    marks_k = key_marks(columns, lanes_all).astype(bf16)
    marks_o = -three_parts(row_dots, lanes_all)
    ones = jnp.where(lanes_all < 24, 1.0, 0.0).astype(bf16)
    for p in range(pairs):
        cut = slice(p * LANES, (p + 1) * LANES)
        scaled = qkv_ref[0, :, cut].astype(f32) * scale
        mixed_grad = mixed_grad_scr[:, cut].astype(f32)
        k_scr[p, :, :LANES] = qkv_ref[0, :, width + p * LANES : width + (p + 1) * LANES]
        k_scr[p, :, LANES:] = marks_k
        v_scr[p, :, :LANES] = qkv_ref[0, :, 2 * width + p * LANES : 2 * width + (p + 1) * LANES]
        v_scr[p, :, LANES:] = ones
        for odd in range(2):
            mine = jnp.logical_not(left) if odd else left
            for ref, values, marks in ((q_scr, scaled, marks_q), (o_scr, mixed_grad, marks_o)):
                masked = jnp.where(mine, values, 0.0).astype(bf16)
                extra = own_lanes(marks, lanes_all, 2 * p + odd).astype(bf16)
                for t in range(tiles):
                    ref[p, t, odd, :, :LANES] = masked[t * TILE : (t + 1) * TILE]
                    ref[p, t, odd, :, LANES:] = extra[t * TILE : (t + 1) * TILE]
    dq_scr[...] = jnp.zeros_like(dq_scr)
    dk_scr[...] = jnp.zeros_like(dk_scr)
    dv_scr[...] = jnp.zeros_like(dv_scr)
    tile_left = lane_ids(TILE) < LANES // 2

    def tile(n, carry):
        i = list_scr[0, n]
        at = pl.ds(pl.multiple_of(i * TILE, TILE), TILE)
        keys = pl.ds(pl.multiple_of(list_scr[1, n], LANES), TILE)
        for p in range(pairs):
            q2 = q_scr[p, i].reshape(2 * TILE, 2 * LANES)
            o2 = o_scr[p, i].reshape(2 * TILE, 2 * LANES)
            probs = jnp.exp(dot(q2, k_scr[p, keys, :], NT))
            prob_grad = dot(o2, v_scr[p, keys, :], NT)
            ds_scr[p] = (probs * prob_grad).astype(bf16)
            p_scr[p] = probs.astype(bf16)
        for p in range(pairs):
            q2 = q_scr[p, i].reshape(2 * TILE, 2 * LANES)
            o2 = o_scr[p, i].reshape(2 * TILE, 2 * LANES)
            dq2 = dot(ds_scr[p], k_scr[p, keys, :LANES])
            dq_scr[p, at, :] += jnp.where(tile_left, dq2[:TILE], dq2[TILE:])
            dk_scr[p, keys, :] += dot(ds_scr[p], q2[:, :LANES], TN)
            dv_scr[p, keys, :] += dot(p_scr[p], o2[:, :LANES], TN)
        return carry

    lax.fori_loop(0, total_tiles, tile, 0)
    for p in range(pairs):
        for block, (source, factor) in enumerate(((dq_scr, scale), (dk_scr, 1.0), (dv_scr, 1.0))):
            start = block * width + p * LANES
            qkv_grad_ref[0, :, start : start + LANES] = (source[p] * factor).astype(bf16)
    grad_scr[:, : 3 * width] += dot(low_one_ref[0], qkv_grad_ref[0], TN)
    query_sum = jnp.sum(qkv_grad_ref[0, :, :width].astype(f32), axis=0, keepdims=True)
    value_sum = jnp.sum(qkv_grad_ref[0, :, 2 * width :].astype(f32), axis=0, keepdims=True)
    rows_scr[...] += jnp.concatenate(
        [query_sum, value_sum, bias_sum, gain_sum, shift_sum, moe_sq, sums_ref[0, 0:2, :]], axis=0
    )

    @pl.when(row == pl.num_programs(0) - 1)
    def _():
        half, share, _ = mine_ref.shape
        main = share - PIECE
        extras = extra_rows(slots, width, 2 * half)
        small = jnp.concatenate(
            [phi_grad_scr[:slots, b * LANES : (b + 1) * LANES] for b in range(pairs)]
            + [rows_scr[:, b * LANES : (b + 1) * LANES] for b in range(pairs)],
            axis=0,
        )
        filled = small.shape[0]
        padded = 2 * half * extras
        if padded > filled:
            small = jnp.concatenate([small, jnp.zeros((padded - filled, LANES), f32)], axis=0)
        pieces = 4 * width * pairs // PIECE
        per_block = width // PIECE
        for core in range(2):

            @pl.when(core_ref[0] == core)
            def _():
                for share_of in range(2):
                    ref = mine_ref if share_of == core else other_ref
                    for n in range(half):
                        device = share_of * half + n
                        for m in range(main // PIECE):
                            g = device * (main // PIECE) + m
                            if g >= pieces:
                                ref[n, m * PIECE : (m + 1) * PIECE, :] = jnp.zeros(
                                    (PIECE, LANES), bf16
                                )
                                continue
                            r, b = g % per_block * PIECE, g // per_block * LANES
                            ref[n, m * PIECE : (m + 1) * PIECE, :] = grad_scr[
                                r : r + PIECE, b : b + LANES
                            ].astype(bf16)
                        tail = jnp.concatenate(
                            [
                                small[device * extras : (device + 1) * extras],
                                jnp.zeros((PIECE - extras, LANES), f32),
                            ],
                            axis=0,
                        )
                        ref[n, main:, :] = tail.astype(bf16)


def extra_rows(slots, width, devices):
    return -(-((slots + 8) * (width // LANES)) // devices)


def share_rows(width, devices):
    pieces = 4 * width * (width // LANES) // PIECE
    return -(-pieces // devices) * PIECE + PIECE


def back(
    core, residual, low_two, dispatch, combine, cotangent, returned, mixed, mixed_rest, qkv, lse,
    low_one, sums, image_ids, gain2, phi, out_weight,
):
    rows, seq_len, width = residual.shape
    lanes = dispatch.shape[2]
    pairs, tiles = width // LANES, seq_len // TILE
    devices = returned.shape[0] * returned.shape[1]
    share = share_rows(width, devices)
    block = lambda n: per_row(seq_len, n)
    return pl.pallas_call(
        back_kernel,
        grid=(rows,),
        in_specs=[
            pl.BlockSpec(memory_space=pltpu.SMEM),
            block(width), block(width), block(lanes), block(lanes), block(width),
            whole(*returned.shape), block(width), block(width), block(3 * width), block(LANES),
            block(width), pl.BlockSpec((1, 8, width), lambda r: (r, 0, 0)), whole(rows, seq_len),
            whole(width), whole(*phi.shape), whole(width, width),
        ],
        out_specs=[
            block(width), block(width), block(3 * width), whole(devices // 2, share, LANES),
            whole(devices // 2, share, LANES),
        ],
        out_shape=[
            jax.ShapeDtypeStruct((rows, seq_len, width), bf16),
            jax.ShapeDtypeStruct((rows, seq_len, width), f32),
            jax.ShapeDtypeStruct((rows, seq_len, 3 * width), bf16),
            jax.ShapeDtypeStruct((devices // 2, share, LANES), bf16),
            jax.ShapeDtypeStruct((devices // 2, share, LANES), bf16),
        ],
        scratch_shapes=[
            pltpu.VMEM((seq_len, lanes), bf16),
            pltpu.VMEM((seq_len, width), bf16),
            pltpu.VMEM((seq_len, width), bf16),
            pltpu.VMEM((pairs, tiles, 2, TILE, 2 * LANES), bf16),
            pltpu.VMEM((pairs, seq_len, 2 * LANES), bf16),
            pltpu.VMEM((pairs, tiles, 2, TILE, 2 * LANES), bf16),
            pltpu.VMEM((pairs, seq_len, 2 * LANES), bf16),
            pltpu.VMEM((pairs, seq_len, LANES), f32),
            pltpu.VMEM((pairs, seq_len, LANES), f32),
            pltpu.VMEM((pairs, seq_len, LANES), f32),
            pltpu.VMEM((width, 4 * width), f32),
            pltpu.VMEM((pairs, 2 * TILE, TILE), bf16),
            pltpu.VMEM((pairs, 2 * TILE, TILE), bf16),
            pltpu.VMEM((lanes, width), f32),
            pltpu.VMEM((8, width), f32),
            pltpu.SMEM((2, tiles * tiles), jnp.int32),
        ],
        cost_estimate=pl.CostEstimate(
            flops=60 * 10**9, bytes_accessed=20 * 10**6, transcendentals=10**7
        ),
        compiler_params=params(),
        name="back",
    )(
        core, residual, low_two, dispatch, combine, cotangent, returned, mixed, mixed_rest, qkv,
        lse, low_one, sums, image_ids, gain2, phi, out_weight,
    )


def input_kernel(tokens_ref, qkv_grad_ref, resid_grad_ref, gain1_ref, qkv_w_ref, out_ref, rows_ref):
    width = tokens_ref.shape[2]

    @pl.when(pl.program_id(0) == 0)
    def _():
        rows_ref[...] = jnp.zeros_like(rows_ref)

    grad = dot(qkv_grad_ref[0], qkv_w_ref[...], NT)
    hat, recip = norm_parts(tokens_ref[0].astype(f32))
    through = norm_back(grad, hat, recip, as_row(gain1_ref))
    out_ref[0] = (resid_grad_ref[0] + through).astype(bf16)
    rows_ref[...] += jnp.concatenate(
        [
            jnp.sum(grad * hat, axis=0, keepdims=True),
            jnp.sum(grad, axis=0, keepdims=True),
            jnp.zeros((6, width), f32),
        ],
        axis=0,
    )


def input_back(tokens, qkv_grad, resid_grad, gain1, qkv_weight):
    rows, seq_len, width = tokens.shape
    block = lambda n: per_row(seq_len, n)
    return pl.pallas_call(
        input_kernel,
        grid=(rows,),
        in_specs=[
            block(width), block(3 * width), block(width), whole(width), whole(width, 3 * width),
        ],
        out_specs=[block(width), whole(8, width)],
        out_shape=[
            jax.ShapeDtypeStruct((rows, seq_len, width), bf16),
            jax.ShapeDtypeStruct((8, width), f32),
        ],
        cost_estimate=pl.CostEstimate(
            flops=6 * 10**9, bytes_accessed=10**7, transcendentals=0
        ),
        compiler_params=params(),
        name="input_back",
    )(tokens, qkv_grad, resid_grad, gain1, qkv_weight)


def fold_kernel(collected_ref, ln1_ref, shared_ref):
    half, share, _ = collected_ref.shape
    main = share - PIECE
    width = ln1_ref.shape[1]
    total = collected_ref[0].astype(f32)
    for d in range(1, half):
        total += collected_ref[d].astype(f32)
    ln1 = [ln1_ref[0:2, b * LANES : (b + 1) * LANES] for b in range(width // LANES)]
    count = 2 * (width // LANES)
    keep = PIECE - count
    tail = jnp.concatenate([total[main : main + keep]] + ln1, axis=0)
    low = jnp.concatenate([total[:main], tail], axis=0).astype(bf16)
    for d in range(half):
        shared_ref[d] = low


def fold(collected, ln1_rows):
    return pl.pallas_call(
        fold_kernel,
        out_shape=jax.ShapeDtypeStruct(collected.shape, bf16),
        compiler_params=params(),
        name="fold",
    )(collected, ln1_rows)


def finish_kernel(
    place_ref, mine_ref, other_ref, qkv_grad_ref, out_grad_ref, ln1_gain_ref, ln1_bias_ref,
    q_bias_ref, v_bias_ref, out_bias_ref, gain2_ref, shift2_ref, phi_ref, rms_ref, small_scr,
    *, slots, count,
):
    half, share, _ = mine_ref.shape
    main = share - PIECE
    width = out_grad_ref.shape[0]
    pairs = width // LANES
    extras = extra_rows(slots, width, 2 * half)
    per_block = width // PIECE
    pieces = 4 * width * pairs // PIECE
    for core in range(2):

        @pl.when(place_ref[0] == core)
        def _():
            for share_of in range(2):
                ref = mine_ref if share_of == core else other_ref
                for n in range(half):
                    device = share_of * half + n
                    for m in range(main // PIECE):
                        g = device * (main // PIECE) + m
                        if g >= pieces:
                            continue
                        r, b = g % per_block * PIECE, g // per_block * LANES
                        values = ref[n, m * PIECE : (m + 1) * PIECE, :].astype(f32)
                        if b < 3 * width:
                            qkv_grad_ref[r : r + PIECE, b : b + LANES] = values
                        else:
                            out_grad_ref[r : r + PIECE, b - 3 * width : b - 3 * width + LANES] = values
                small_scr[share_of * half : (share_of + 1) * half] = ref[:, main:, :].astype(f32)

    small = small_scr[...]
    ln1 = jnp.sum(small, axis=0)
    keep = PIECE - 2 * pairs
    ln1 = [
        jnp.concatenate([ln1[keep + 2 * b + k : keep + 2 * b + k + 1] for b in range(pairs)], axis=1)
        for k in range(2)
    ]
    ln1_gain_ref[...] = ln1[0].reshape(width)
    ln1_bias_ref[...] = ln1[1].reshape(width)

    def line(n):
        return small_scr[n // extras, n % extras : n % extras + 1, :]

    def vector(k):
        first = slots * pairs
        return jnp.concatenate([line(first + 8 * b + k) for b in range(pairs)], axis=1)

    q_bias_ref[...] = vector(0).reshape(width)
    v_bias_ref[...] = vector(1).reshape(width)
    out_bias_ref[...] = vector(2).reshape(width)
    gain2_ref[...] = vector(3).reshape(width)
    shift2_ref[...] = vector(4).reshape(width)
    squares = [jnp.sum(vector(k), axis=1, keepdims=True) for k in (6, 7, 5)]
    rms_ref[...] = jnp.sqrt(jnp.concatenate(squares, axis=1) * (1.0 / count)).reshape(3)
    own = phi_ref.shape[0]
    ep = slots // own
    for e in range(ep):

        @pl.when(place_ref[1] == e)
        def _():
            for s in range(own):
                phi_ref[s : s + 1, :] = jnp.concatenate(
                    [line(slots * b + e * own + s) for b in range(pairs)], axis=1
                )


def finish(place, mine, other, width, own, slots, count):
    half, share, _ = mine.shape
    vector = jax.ShapeDtypeStruct((width,), f32)
    vmem = pl.BlockSpec(memory_space=pltpu.VMEM)
    return pl.pallas_call(
        lambda *refs: finish_kernel(*refs, slots=slots, count=count),
        in_specs=[pl.BlockSpec(memory_space=pltpu.SMEM), vmem, vmem],
        out_shape=[
            jax.ShapeDtypeStruct((width, 3 * width), f32),
            jax.ShapeDtypeStruct((width, width), f32),
            vector, vector, vector, vector, vector, vector, vector,
            jax.ShapeDtypeStruct((own, width), f32),
            jax.ShapeDtypeStruct((3,), f32),
        ],
        scratch_shapes=[pltpu.VMEM((2 * half, PIECE, LANES), f32)],
        compiler_params=params(),
        name="finish",
    )(place, mine, other)


def local(
    tokens, image_ids, slot_image, ln1_gain, ln1_bias, qkv_weight, query_bias, value_bias,
    out_weight, out_bias, ln2_gain, ln2_bias, slot_params, up_weight, up_bias, down_weight,
    down_bias, cotangent,
):
    across, swap = ("y", "expert"), [(0, 1), (1, 0)]
    dp, ep = lax.axis_size("y") * lax.axis_size("core"), lax.axis_size("expert")
    devices = dp * ep
    seqs, seq_len, width = tokens.shape
    own = slot_params.shape[1]
    slots = own * ep
    core = lax.axis_index("core").astype(jnp.int32)
    expert = lax.axis_index("expert").astype(jnp.int32)

    def exchange(values, over):
        return lax.all_to_all(values, over, split_axis=0, concat_axis=0, tiled=True)

    phi = exchange(jnp.broadcast_to(slot_params.T[None], (ep, own, width)), "expert")
    phi = phi.reshape(slots, width)

    low_one, qkv, mixed, mixed_rest, lse, residual, low_two, sums = attend(
        tokens, image_ids, ln1_gain, ln1_bias, query_bias, value_bias, qkv_weight, out_weight,
        out_bias, ln2_gain, ln2_bias,
    )
    dispatch, combine, sent = route(low_two, cotangent, image_ids, slot_image, phi, dp, ep)
    per_device = sent.shape[2]
    arrived = exchange(sent.reshape(devices, per_device, width), ("y", "core", "expert"))
    parts, rows, hidden, pre_grad = experts(
        arrived, up_weight, up_bias, down_weight, down_bias * (1.0 / dp)
    )
    returned = exchange(parts, ("y", "core", "expert"))
    up_grad, up_bias_grad, down_grad, down_bias_grad = expert_grads(rows, hidden, pre_grad)

    output, resid_grad, qkv_grad, mine, other = back(
        core.reshape(1), residual, low_two, dispatch, combine, cotangent,
        returned.reshape(dp, ep, per_device, width), mixed, mixed_rest, qkv, lse, low_one, sums,
        image_ids, ln2_gain, phi, out_weight,
    )

    met = lax.ppermute(other, "core", swap)
    chip = (mine.astype(f32) + met.astype(f32)).astype(bf16)
    collected = exchange(chip, across)
    input_grad, ln1_rows = input_back(tokens, qkv_grad, resid_grad, ln1_gain, qkv_weight)
    shares = exchange(fold(collected, ln1_rows), across)
    others = lax.ppermute(shares, "core", swap)
    (
        qkv_weight_grad, out_weight_grad, ln1_gain_grad, ln1_bias_grad, query_bias_grad,
        value_bias_grad, out_bias_grad, ln2_gain_grad, ln2_bias_grad, phi_grad, stream_rms,
    ) = finish(
        jnp.stack([core, expert]), shares, others, width, own, slots,
        devices * seqs * seq_len * width,
    )
    return (
        output, input_grad, ln1_gain_grad, ln1_bias_grad, qkv_weight_grad, query_bias_grad,
        value_bias_grad, out_weight_grad, out_bias_grad, ln2_gain_grad, ln2_bias_grad, phi_grad.T,
        up_grad, up_bias_grad, down_grad, down_bias_grad, stream_rms,
    )


def solution(mesh):
    dp, ep = mesh.shape["dp"], mesh.shape["expert"]
    split_mesh = Mesh(mesh.devices.reshape(dp // 2, 2, ep), ("y", "core", "expert"))
    rows = ("y", "core", "expert")
    split, flat = P(rows, None, None), P(rows, None)
    units = ("y", "core")
    return jax.shard_map(
        local,
        mesh=split_mesh,
        in_specs=(
            split, flat, flat, P(), P(), P(), P(), P(), P(), P(), P(), P(),
            P(None, "expert"), P("expert", units, None), P("expert", units),
            P("expert", units, None), P("expert", None), split,
        ),
        out_specs=(
            split, split, P(), P(), P(), P(), P(), P(), P(), P(), P(),
            P(None, "expert"), P("expert", units, None), P("expert", units),
            P("expert", units, None), P("expert", None), P(),
        ),
        check_vma=False,
    )
```

time: 279 us -> 189 us (0.68)
  waiting for transfers between devices: 72.4 us -> 27.8 us
  Pallas kernels: 133 us -> 103 us
  local copies, waits for them, and re-layouts: 32.4 us -> 4.93 us
  blocking collectives: 0 us -> 22.1 us
  starting transfers between devices: 32.1 us -> 26.7 us
  other arithmetic: 7.62 us -> 3.41 us
    all_to_all x5 -> x4, waiting for transfers between devices: 72.4 us -> 25.9 us  [exchange(): return lax.all_to_all(values, over, split_axis=0, concat_axis=0, tiled=True)]
    pallas_call x5 -> x7, Pallas kernels: 130 us -> 100 us  [the longest x1 51.2 us: back(): pl.pallas_call(back_kernel, grid=(rows,), in_specs=[pl.BlockSpec(memory_s...]
    all_to_all x0 -> x1, blocking collectives: none -> 22.1 us  [exchange(): return lax.all_to_all(values, over, split_axis=0, concat_axis=0, tiled=True)]
    all_to_all x5 -> x4, starting transfers between devices: 32.1 us -> 24 us  [exchange(): return lax.all_to_all(values, over, split_axis=0, concat_axis=0, tiled=True)]
    slice x7 -> x0, local copies, waits for them, and re-layouts: 6.84 us -> none  [the longest x2 2.76 us: local(): qkv_weight_grad = weights[:3].transpose(1, 0, 2).reshape(width, 3 * width)]
    reshape x9 -> x1, local copies, waits for them, and re-layouts: 6.13 us -> 0.61 us  [local(): phi = phi.reshape(slots, width)]
    another operation x8 -> x0, local copies, waits for them, and re-layouts: 5.4 us -> none  [local(): jnp.stack([ln1_gain, ln1_bias, query_bias, value_bias, out_bias, ln2_gain...]
    concatenate x1 -> x0, local copies, waits for them, and re-layouts: 4.79 us -> none  [local(): jnp.concatenate([weight_grad.reshape(4 * width, width), phi_grad[:slots]....]
  transfers between devices with their start and end apart: 5 -> 6, of which waited for: 4 -> 4; matrix products, arithmetic and copies ran while one was open for 3% -> 1% of each run, Pallas kernels for 17% -> 20%
where the time goes in v2:
time: 189 us
  Pallas kernels  103 us (54%)
  waiting for transfers between devices  27.8 us (15%)
  starting transfers between devices  26.7 us (14%)
  blocking collectives  22.1 us (12%)
  local copies, waits for them, and re-layouts  4.93 us (3%)
  other arithmetic  3.41 us (2%)
    pallas_call x1, Pallas kernels, back(): pl.pallas_call(back_kernel, grid=(rows,), in_specs=[pl.BlockSpec(memory_s...  51.2 us
    pallas_call x1, Pallas kernels, attend(): pl.pallas_call(attend_kernel, grid=(rows,), in_specs=[block(width), whole...  27 us
    all_to_all x4, waiting for transfers between devices, exchange(): return lax.all_to_all(values, over, split_axis=0, concat_axis=0, tiled=True)  25.9 us
    all_to_all x4, starting transfers between devices, exchange(): return lax.all_to_all(values, over, split_axis=0, concat_axis=0, tiled=True)  24 us
    all_to_all x1, blocking collectives, exchange(): return lax.all_to_all(values, over, split_axis=0, concat_axis=0, tiled=True)  22.1 us
    pallas_call x1, Pallas kernels, input_back(): pl.pallas_call(input_kernel, grid=(rows,), in_specs=[block(width), block(...  8.41 us
    pallas_call x1, Pallas kernels, route(): pl.pallas_call(route_kernel, grid=(rows,), in_specs=[block(width), block(...  5.23 us
  transfers between devices with their start and end apart: 6, of which 4 were waited for; matrix products, arithmetic and copies ran while one was open for 1% of the time, Pallas kernels for 20%

profile of v2, /device:TPU:0, one launch (start us, length us, event | category | flops | bytes accessed | tf_op | source)
XLA Modules:
  0.0 188.7 jit_solution(12087049305855714154)
XLA Ops:
  0.7 1.3 broadcast_in_dim.2
  1.9 7.3 %all-to-all-start = ((bf16[8,2,384]{2,1,0:T(2,128)(2,1)}), bf16[8,2,384]{2,1,0:T(2,128)(2,1)S(1)}, u32[]{:S(2)}, u32[]{:S(2)}) async-start(bf16[8,2,384]{2,1,0:T(2,128)(2,1)} %broadcast_in_dim.2), calls=%async_computation | async-start | bytes 24576 | tf_op jit(solution)/shard_map/all_to_all | solution.py:932
  9.2 27.0 %attend.1 = (bf16[2,1024,384]{2,1,0:T(8,128)(2,1)}, bf16[2,1024,1152]{2,1,0:T(8,128)(2,1)}, bf16[2,1024,384]{2,1,0:T(8,128)(2,1)}, bf16[2,1024,384]{2,1,0:T(8,12...) custom-call(bf16[2,1024,384]{2,1,0:T(8,128)(2,1)} %tokens_ref.3, ...), custom_call_target="tpu_custom_call" | custom-call | flops 20000000000 | bytes 20000000 | tf_op jit(solution)/shard_map/attend/pallas_call | solution.py:297
  36.2 0.0 all-to-all-done
  36.2 0.6 reshape.48.phi_ref
  36.9 5.2 %route.1 = (f32[2,1024,128]{2,1,0:T(8,128)}, f32[2,1024,128]{2,1,0:T(8,128)}, bf16[4,8,8,384]{3,2,1,0:T(8,128)(2,1)}) custom-call(bf16[2,1024,384]{2,1,0:T(8,128)(2,1)} %get-tuple-element.55.low_two_ref, bf16[2,1024,384]{2,1,0:T(8,128)(2,1)} %cot_ref.3, s32[2,1024]{1,0:T(2,128)} %ids_ref.5, s32[2,16]{1,0:T(2,128)} %slot_ref.1, bf16[16,384]{1,0:T(8,128)(2,1)} %reshape.48.phi_ref), custom_call_target="tpu_custom_call" | custom-call | tf_op jit(solution)/shard_map/route/pallas_call | solution.py:398
  42.1 7.6 %all-to-all-start.1 = ((bf16[32,8,384]{2,1,0:T(8,128)(2,1)}), bf16[32,8,384]{2,1,0:T(8,128)(2,1)S(1)}, u32[]{:S(2)}, u32[]{:S(2)}) async-start(bf16[32,8,384]{2,1,0:T(8,128)(2,1)} %bitcast.7), calls=%async_computation.1 | async-start | bytes 393216 | tf_op jit(solution)/shard_map/all_to_all | solution.py:932
  49.7 0.0 copy-done.5
  49.7 0.6 broadcast_multiply_fusion.down_bias_ref
  50.3 8.0 %all-to-all-done.1.arrived_ref = bf16[32,8,384]{2,1,0:T(8,128)(2,1)S(1)} async-done(((bf16[32,8,384]{2,1,0:T(8,128)(2,1)}), bf16[32,8,384]{2,1,0:T(8,128)(2,1)S(1)}, u32[]{:S(2)}, u32[]{:S(2)}) %all-to-all-start.1) | async-done | bytes 196640 | tf_op jit(solution)/shard_map/all_to_all | solution.py:932
  58.3 0.7 copy-done.2
  58.9 3.2 %experts.1 = (bf16[32,8,384]{2,1,0:T(8,128)(2,1)}, bf16[2,2,64,384]{3,2,1,0:T(8,128)(2,1)}, bf16[2,64,384]{2,1,0:T(8,128)(2,1)}, bf16[2,64,384]{2,1,0:T(8,128)(2,1)}) custom-call(bf16[32,8,384]{2,1,0:T(8,128)(2,1)} %copy-done.2, bf16[2,384,384]{2,1,0:T(8,128)(2,1)} %up_ref.1, bf16[2,384]{1,0:T(2,128)(2,1)} %up_bias_ref.1, bf16[2,384,384]{2,1,0:T(8,128)(2,1)} %down_ref.1, ...), custom_call_target="tpu_custom_call" | custom-call | tf_op jit(solution)/shard_map/experts/pallas_call | solution.py:484
  62.1 3.2 %all-to-all-start.2 = ((bf16[32,8,384]{2,1,0:T(8,128)(2,1)}), bf16[32,8,384]{2,1,0:T(8,128)(2,1)S(1)}, u32[]{:S(2)}, u32[]{:S(2)}) async-start(bf16[32,8,384]{2,1,0:T(8,128)(2,1)} %get-tuple-element.59), calls=%async_computation.2 | async-start | bytes 393216 | tf_op jit(solution)/shard_map/all_to_all | solution.py:932
  65.4 8.4 %all-to-all-done.2 = bf16[32,8,384]{2,1,0:T(8,128)(2,1)S(1)} async-done(((bf16[32,8,384]{2,1,0:T(8,128)(2,1)}), bf16[32,8,384]{2,1,0:T(8,128)(2,1)S(1)}, u32[]{:S(2)}, u32[]{:S(2)}) %all-to-all-start.2) | async-done | bytes 196640 | tf_op jit(solution)/shard_map/all_to_all | solution.py:932
  73.7 0.7 copy-done.4
  74.4 51.2 %back.1 = (bf16[2,1024,384]{2,1,0:T(8,128)(2,1)}, f32[2,1024,384]{2,1,0:T(8,128)}, bf16[2,1024,1152]{2,1,0:T(8,128)(2,1)}, bf16[16,160,128]{2,1,0:T(8,128)(2,1)}, bf16[16,160,128]{2,1,0:T(8,128)(2,1)}) custom-call(s32[1]{0:T(128)} %bitcast.core_ref, f32[2,1024,384]{2,1,0:T(8,128)} %get-tuple-element.54.residual_ref, ...), custom_call_target="tpu_custom_call" | custom-call | flops 60000002048 | bytes 20000000 | tf_op jit(solution)/shard_map/back/pallas_call | solution.py:711
  125.6 2.7 %collective-permute-start = (bf16[16,160,128]{2,1,0:T(8,128)(2,1)}, bf16[16,160,128]{2,1,0:T(8,128)(2,1)S(1)}, u32[]{:S(2)}, u32[]{:S(2)}) collective-permute-start(bf16[16,160,128]{2,1,0:T(8,128)(2,1)} %get-tuple-element.71), channel_id=1, source_target_pairs={{0,8},{8,0},{1,9},{9,1},{2,10},{10,2},{3,11},{11,3},{4,12},{12,4},... | collective-permute-start | bytes 1966088 | tf_op jit(solution)/shard_map/ppermute | solution.py:956
  128.3 1.9 %collective-permute-done = bf16[16,160,128]{2,1,0:T(8,128)(2,1)S(1)} collective-permute-done((bf16[16,160,128]{2,1,0:T(8,128)(2,1)}, bf16[16,160,128]{2,1,0:T(8,128)(2,1)S(1)}, u32[]{:S(2)}, u32[]{:S(2)}) %collective-permute-start) | collective-permute-done | bytes 655392 | tf_op jit(solution)/shard_map/ppermute | solution.py:956
  130.2 2.1 %add_convert_fusion = bf16[16,160,128]{2,1,0:T(8,128)(2,1)} fusion(bf16[16,160,128]{2,1,0:T(8,128)(2,1)S(1)} %collective-permute-done, bf16[16,160,128]{2,1,0:T(8,128)(2,1)} %get-tuple-element.70), kind=kLoop, calls=%fused_computation | loop fusion | flops 1310720 | bytes 1966080 | tf_op jit(solution)/shard_map/convert_element_type | solution.py:957
  132.3 5.9 %all-to-all-start.3 = ((bf16[16,160,128]{2,1,0:T(8,128)(2,1)}), bf16[16,160,128]{2,1,0:T(8,128)(2,1)S(1)}, u32[]{:S(2)}, u32[]{:S(2)}) async-start(bf16[16,160,128]{2,1,0:T(8,128)(2,1)} %add_convert_fusion), calls=%async_computation.3 | async-start | bytes 1310720 | tf_op jit(solution)/shard_map/all_to_all | solution.py:932
  138.2 8.4 %input_back.1 = (bf16[2,1024,384]{2,1,0:T(8,128)(2,1)}, f32[8,384]{1,0:T(8,128)}) custom-call(bf16[2,1024,384]{2,1,0:T(8,128)(2,1)} %tokens_ref.3, bf16[2,1024,1152]{2,1,0:T(8,128)(2,1)} %get-tuple-element.67.qkv_grad_ref, f32[2,1024,384]{2,1,0:T(8,128)} %get-tuple-element.68.resid_grad_ref, f32[384]{0:T(512)} %gain1_ref.3, bf16[384,1152]{1,0:T(8,128)(2,1)} %qkv_w_ref.3), custom_call_target="tpu_custom_call" | custom-call | flops 6000000000 | bytes 10000000 | tf_op jit(solution)/shard_map/input_back/pallas_call | solution.py:785
  146.6 9.5 %all-to-all-done.3.collected_ref = bf16[16,160,128]{2,1,0:T(8,128)(2,1)S(1)} async-done(((bf16[16,160,128]{2,1,0:T(8,128)(2,1)}), bf16[16,160,128]{2,1,0:T(8,128)(2,1)S(1)}, u32[]{:S(2)}, u32[]{:S(2)}) %all-to-all-start.3) | async-done | bytes 655392 | tf_op jit(solution)/shard_map/all_to_all | solution.py:932
  156.2 0.8 copy-done.1
  157.0 2.0 %fold.1 = bf16[16,160,128]{2,1,0:T(8,128)(2,1)} custom-call(bf16[16,160,128]{2,1,0:T(8,128)(2,1)} %copy-done.1, f32[8,384]{1,0:T(8,128)} %get-tuple-element.72.ln1_ref), custom_call_target="tpu_custom_call" | custom-call | tf_op jit(solution)/shard_map/fold/pallas_call | solution.py:821
  159.0 22.1 %all_to_all.25.refs_1_ = bf16[16,160,128]{2,1,0:T(8,128)(2,1)S(1)} all-to-all(bf16[16,160,128]{2,1,0:T(8,128)(2,1)} %fold.1), channel_id=1, replica_groups=mesh['y'=2,'core'=2,'expert'=8] {'y','expert'}, dimensions={0} | all-to-all | bytes 1310720 | tf_op jit(solution)/shard_map/all_to_all | solution.py:932
  181.1 0.0 collective-permute-start.1
  181.1 0.7 pad_add_fusion.refs_0_
  181.8 2.9 %expert_grads.1 = (f32[2,384,384]{2,1,0:T(8,128)}, f32[2,384]{1,0:T(2,128)}, f32[2,384,384]{2,1,0:T(8,128)}, f32[2,384]{1,0:T(2,128)}) custom-call(bf16[2,2,64,384]{3,2,1,0:T(8,128)(2,1)} %get-tuple-element.83.rows_ref, bf16[2,64,384]{2,1,0:T(8,128)(2,1)} %get-tuple-element.84.hidden_ref, bf16[2,64,384]{2,1,0:T(8,128)(2,1)} %get-tuple-element.85.pre_grad_ref), custom_call_target="tpu_custom_call" | custom-call | flops 75497472 | bytes 4000000 | tf_op jit(solution)/shard_map/expert_grads/pallas_call | solution.py:500
  184.7 0.0 collective-permute-done.1.refs_2_
  184.7 0.0 copy-start.3
  184.7 0.8 copy-done.3
  185.6 3.0 %finish.1 = (f32[384,1152]{1,0:T(8,128)}, f32[384,384]{1,0:T(8,128)}, f32[384]{0:T(512)}, f32[384]{0:T(512)}, f32[384]{0:T(512)}, /*index=5*/f32[384]{0:T(512)},...) custom-call(s32[2]{0:T(128)} %pad_add_fusion.refs_0_, ...), custom_call_target="tpu_custom_call" | custom-call | tf_op jit(solution)/shard_map/finish/pallas_call | solution.py:901
  (6 shorter events, 0.0 us)
Async XLA Ops:
  1.9 34.3 %all-to-all-start = ((bf16[8,2,384]{2,1,0:T(2,128)(2,1)}), bf16[8,2,384]{2,1,0:T(2,128)(2,1)S(1)}, u32[]{:S(2)}, u32[]{:S(2)}) async-start(bf16[8,2,384]{2,1,0:T(2,128)(2,1)} %broadcast_in_dim.2), calls=%async_computation | async-start | bytes 24576 | tf_op jit(solution)/shard_map/all_to_all | solution.py:932
  36.9 12.9 %copy-start.5 = (f32[2,384]{1,0:T(2,128)S(1)}, f32[2,384]{1,0:T(2,128)}, u32[]{:S(2)}) copy-start(f32[2,384]{1,0:T(2,128)} %param.34) | copy-start | bytes 9220
  42.1 16.2 %all-to-all-start.1 = ((bf16[32,8,384]{2,1,0:T(8,128)(2,1)}), bf16[32,8,384]{2,1,0:T(8,128)(2,1)S(1)}, u32[]{:S(2)}, u32[]{:S(2)}) async-start(bf16[32,8,384]{2,1,0:T(8,128)(2,1)} %bitcast.7), calls=%async_computation.1 | async-start | bytes 393216 | tf_op jit(solution)/shard_map/all_to_all | solution.py:932
  58.3 0.7 copy-start.2
  62.1 11.6 %all-to-all-start.2 = ((bf16[32,8,384]{2,1,0:T(8,128)(2,1)}), bf16[32,8,384]{2,1,0:T(8,128)(2,1)S(1)}, u32[]{:S(2)}, u32[]{:S(2)}) async-start(bf16[32,8,384]{2,1,0:T(8,128)(2,1)} %get-tuple-element.59), calls=%async_computation.2 | async-start | bytes 393216 | tf_op jit(solution)/shard_map/all_to_all | solution.py:932
  73.7 0.7 copy-start.4
  125.6 4.6 %collective-permute-start = (bf16[16,160,128]{2,1,0:T(8,128)(2,1)}, bf16[16,160,128]{2,1,0:T(8,128)(2,1)S(1)}, u32[]{:S(2)}, u32[]{:S(2)}) collective-permute-start(bf16[16,160,128]{2,1,0:T(8,128)(2,1)} %get-tuple-element.71), channel_id=1, source_target_pairs={{0,8},{8,0},{1,9},{9,1},{2,10},{10,2},{3,11},{11,3},{4,12},{12,4},... | collective-permute-start | bytes 1966088 | tf_op jit(solution)/shard_map/ppermute | solution.py:956
  132.3 23.8 %all-to-all-start.3 = ((bf16[16,160,128]{2,1,0:T(8,128)(2,1)}), bf16[16,160,128]{2,1,0:T(8,128)(2,1)S(1)}, u32[]{:S(2)}, u32[]{:S(2)}) async-start(bf16[16,160,128]{2,1,0:T(8,128)(2,1)} %add_convert_fusion), calls=%async_computation.3 | async-start | bytes 1310720 | tf_op jit(solution)/shard_map/all_to_all | solution.py:932
  156.2 0.8 copy-start.1
  181.1 3.6 %copy-start = (bf16[16,160,128]{2,1,0:T(8,128)(2,1)}, bf16[16,160,128]{2,1,0:T(8,128)(2,1)S(1)}, u32[]{:S(2)}) copy-start(bf16[16,160,128]{2,1,0:T(8,128)(2,1)S(1)} %all_to_all.25.refs_1_) | copy-start | bytes 1966084
  181.1 3.6 %collective-permute-start.1 = (bf16[16,160,128]{2,1,0:T(8,128)(2,1)S(1)}, bf16[16,160,128]{2,1,0:T(8,128)(2,1)S(1)}, u32[]{:S(2)}, u32[]{:S(2)}) collective-permute-start(bf16[16,160,128]{2,1,0:T(8,128)(2,1)S(1)} %all_to_all.25.refs_1_), channel_id=1, source_target_pairs={{0,8},{8,0},{1,9},{9,1},{2,10},{10,2},{3,11},{11,3},{4,12},{12,4},... | collective-permute-start | bytes 1966088 | tf_op jit(solution)/shard_map/ppermute | solution.py:961
  184.7 0.8 copy-start.3

commit v3 on v2

--- a/solution.py
+++ b/solution.py
@@ -13,8 +13,9 @@
 LANES = 128
 TILE = 256
 SAFE = 60.0
+GROUP = 2
+SLOTS = 2 * GROUP
 PIECE = 16
-VMEM_BYTES = 60 * 1024 * 1024
 
 bf16 = jnp.bfloat16
 f32 = jnp.float32
@@ -75,11 +76,31 @@
     return total
 
 
+def over_tiles(total, work):
+    def together(g, carry):
+        work([g * GROUP + k for k in range(GROUP)])
+        return carry
+
+    def alone(n, carry):
+        work([n])
+        return carry
+
+    whole_groups = lax.div(total, GROUP)
+    lax.fori_loop(0, whole_groups, together, 0)
+    lax.fori_loop(whole_groups * GROUP, total, alone, 0)
+
+
 def head_picker(width):
-    head = lax.broadcasted_iota(jnp.int32, (width, LANES), 0) // (width // HEADS)
+    head, _ = split(lax.broadcasted_iota(jnp.int32, (width, LANES), 0), width // HEADS)
     return jnp.where(head == lax.broadcasted_iota(jnp.int32, (width, LANES), 1), 1.0, 0.0).astype(
         bf16
     )
+
+
+def split(values, size):
+    if size & (size - 1) == 0:
+        return jnp.right_shift(values, size.bit_length() - 1), jnp.bitwise_and(values, size - 1)
+    return lax.div(values, size), lax.rem(values, size)
 
 
 def as_row(ref):
@@ -124,15 +145,15 @@
 
 
 def own_lanes(values, lanes, head):
-    keep = jnp.logical_or(lanes >= 24, lax.rem(lanes, 8) == head)
+    keep = jnp.logical_or(lanes >= 24, jnp.bitwise_and(lanes, 7) == head)
     return jnp.where(keep, values, 0.0)
 
 
 def attend_kernel(
     tokens_ref, ids_ref, gain1_ref, shift1_ref, q_bias_ref, v_bias_ref, qkv_w_ref, out_w_ref,
     out_bias_ref, gain2_ref, shift2_ref,
-    low_one_ref, qkv_ref, mixed_ref, mixed_rest_ref, lse_ref, residual_ref, low_two_ref, sums_ref,
-    q_scr, k_scr, v_scr, s_scr, top_scr, acc_scr, p_scr, list_scr,
+    low_one_ref, qkv_ref, mixed_ref, mixed_rest_ref, recip_ref, residual_ref, low_two_ref, sums_ref,
+    probs_ref, q_scr, k_scr, v_scr, s_scr, top_scr, acc_scr, p_scr, list_scr, sem,
 ):
     row = pl.program_id(0)
     seq_len, width = tokens_ref.shape[1:]
@@ -174,7 +195,6 @@
                 q_scr[p, t, odd, :, :LANES] = own[t * TILE : (t + 1) * TILE]
                 q_scr[p, t, odd, :, LANES:] = marks_q[t * TILE : (t + 1) * TILE]
     acc_scr[...] = jnp.zeros_like(acc_scr)
-    lse_ref[...] = jnp.zeros_like(lse_ref)
 
     picker = head_picker(width)
 
@@ -185,34 +205,48 @@
     bound = jnp.max(longest(query) * longest(key)) * (scale * scale)
     small = bound <= SAFE * SAFE
 
+    def leave(n):
+        slot = lax.rem(n, SLOTS)
+        return pltpu.make_async_copy(p_scr.at[slot], probs_ref.at[row, n], sem.at[slot])
+
+    def weigh(numbers, weights):
+        for n in numbers:
+
+            @pl.when(n >= SLOTS)
+            def _(n=n):
+                leave(n - SLOTS).wait()
+
+        for n in numbers:
+            for p in range(pairs):
+                p_scr[lax.rem(n, SLOTS), p] = weights(n, p).astype(bf16)
+        for n in numbers:
+            leave(n).start()
+        for n in numbers:
+            at = pl.ds(pl.multiple_of(list_scr[0, n] * TILE, TILE), TILE)
+            keys = pl.ds(pl.multiple_of(list_scr[1, n], LANES), TILE)
+            for h in range(HEADS):
+                part = slice((h % 2) * TILE, (h % 2 + 1) * TILE)
+                probs = p_scr[lax.rem(n, SLOTS), h // 2, part, :]
+                acc_scr[h, at, :] += dot(probs, v_scr[h, keys, :])
+
+    def scores(n, p):
+        q2 = q_scr[p, list_scr[0, n]].reshape(2 * TILE, 2 * LANES)
+        keys = pl.ds(pl.multiple_of(list_scr[1, n], LANES), TILE)
+        return dot(q2, k_scr[p, keys, :], NT)
+
     @pl.when(small)
     def _():
-        def tile(n, carry):
-            i = list_scr[0, n]
-            at = pl.ds(pl.multiple_of(i * TILE, TILE), TILE)
-            keys = pl.ds(pl.multiple_of(list_scr[1, n], LANES), TILE)
-            for p in range(pairs):
-                q2 = q_scr[p, i].reshape(2 * TILE, 2 * LANES)
-                p_scr[p] = jnp.exp(dot(q2, k_scr[p, keys, :], NT)).astype(bf16)
-            for h in range(HEADS):
-                part = slice((h % 2) * TILE, (h % 2 + 1) * TILE)
-                acc_scr[h, at, :] += dot(p_scr[h // 2, part, :], v_scr[h, keys, :])
-            return carry
-
-        lax.fori_loop(0, total_tiles, tile, 0)
+        over_tiles(total_tiles, lambda numbers: weigh(numbers, lambda n, p: jnp.exp(scores(n, p))))
 
     @pl.when(jnp.logical_not(small))
     def _():
-        def query_tile(i, carry):
-            at = pl.ds(pl.multiple_of(i * TILE, TILE), TILE)
-            begin, count = key_window(starts, i, seq_len)
+        def query_tile(i, begin):
+            _, count = key_window(starts, i, seq_len)
             top_scr[...] = jnp.full_like(top_scr, -3e38)
 
-            def scores(j, inner):
-                keys = pl.ds(pl.multiple_of(begin + j * TILE, LANES), TILE)
+            def look(j, inner):
                 for p in range(pairs):
-                    q2 = q_scr[p, i].reshape(2 * TILE, 2 * LANES)
-                    s = dot(q2, k_scr[p, keys, :], NT)
+                    s = scores(begin + j, p)
                     s_scr[j, p] = s
                     best = s[:, :LANES]
                     for o in range(LANES, TILE, LANES):
@@ -220,50 +254,45 @@
                     top_scr[p] = jnp.maximum(top_scr[p], best)
                 return inner
 
-            lax.fori_loop(0, count, scores, 0)
-            tile_lanes = lane_ids(TILE)
-            lse = jnp.zeros((TILE, LANES), f32)
+            lax.fori_loop(0, count, look, 0)
             for p in range(pairs):
-                top = jnp.broadcast_to(
+                top_scr[p] = jnp.broadcast_to(
                     jnp.max(top_scr[p], axis=-1, keepdims=True), top_scr.shape[1:]
                 )
-                top_scr[p] = top
-                lse = jnp.where(tile_lanes == 2 * p, top[:TILE], lse)
-                lse = jnp.where(tile_lanes == 2 * p + 1, top[TILE:], lse)
-            lse_ref[0, at, :] = lse
-
-            def weigh(j, inner):
-                keys = pl.ds(pl.multiple_of(begin + j * TILE, LANES), TILE)
-                for p in range(pairs):
+
+            def tile(j, inner):
+                def weights(n, p):
                     top = jnp.concatenate([top_scr[p]] * (TILE // LANES), axis=1)
-                    p_scr[p] = jnp.exp(s_scr[j, p] - top).astype(bf16)
-                for h in range(HEADS):
-                    part = slice((h % 2) * TILE, (h % 2 + 1) * TILE)
-                    acc_scr[h, at, :] += dot(p_scr[h // 2, part, :], v_scr[h, keys, :])
+                    return jnp.exp(s_scr[j, p] - top)
+
+                weigh([begin + j], weights)
                 return inner
 
-            lax.fori_loop(0, count, weigh, 0)
-            return carry
+            lax.fori_loop(0, count, tile, 0)
+            return begin + count
 
         lax.fori_loop(0, tiles, query_tile, 0)
 
-    lse = lse_ref[0]
+    recips = jnp.zeros((seq_len, LANES), f32)
     for p in range(pairs):
         even, odd = acc_scr[2 * p], acc_scr[2 * p + 1]
         swapped = jnp.where(left, odd, even)
-        sums = pltpu.roll(swapped, LANES // 2, 1)
-        mixed = jnp.where(left, even, odd) / sums
-        lse += jnp.where(lanes == 2 * p, jnp.log(sums), 0.0)
-        lse += jnp.where(lanes == 2 * p + 1, jnp.log(swapped), 0.0)
+        recip = 1.0 / swapped
+        own = pltpu.roll(recip, LANES // 2, 1)
+        mixed = jnp.where(left, even, odd) * own
+        recips = jnp.where(lanes == 2 * p, own, recips)
+        recips = jnp.where(lanes == 2 * p + 1, recip, recips)
         low = mixed.astype(bf16)
         mixed_ref[0, :, p * LANES : (p + 1) * LANES] = low
         mixed_rest_ref[0, :, p * LANES : (p + 1) * LANES] = (mixed - low.astype(f32)).astype(bf16)
-    lse_ref[0] = lse
+    recip_ref[0] = recips
     branch = dot(mixed_ref[0], out_w_ref[...]) + as_row(out_bias_ref)
     residual = tokens_ref[0].astype(f32) + branch
     residual_ref[0] = residual
     hat_two, _ = norm_parts(residual)
     low_two_ref[0] = (hat_two * as_row(gain2_ref) + as_row(shift2_ref)).astype(bf16)
+    for late in range(SLOTS):
+        leave(total_tiles - SLOTS + late).wait()
     stream = tokens_ref[0].astype(f32)
     sums_ref[0] = jnp.concatenate(
         [
@@ -283,8 +312,8 @@
     return pl.BlockSpec((1, seq_len, width), lambda r: (r, 0, 0))
 
 
-def params():
-    return pltpu.CompilerParams(vmem_limit_bytes=VMEM_BYTES)
+def params(mebibytes):
+    return pltpu.CompilerParams(vmem_limit_bytes=mebibytes * 1024 * 1024)
 
 
 def attend(
@@ -305,11 +334,13 @@
         out_specs=[
             block(width), block(3 * width), block(width), block(width), block(LANES),
             block(width), block(width), pl.BlockSpec((1, 8, width), lambda r: (r, 0, 0)),
+            pl.BlockSpec(memory_space=pl.ANY),
         ],
         out_shape=[
             shape(width, bf16), shape(3 * width, bf16), shape(width, bf16), shape(width, bf16),
             shape(LANES, f32), shape(width, f32), shape(width, bf16),
             jax.ShapeDtypeStruct((rows, 8, width), f32),
+            jax.ShapeDtypeStruct((rows, tiles * tiles, pairs, 2 * TILE, TILE), bf16),
         ],
         scratch_shapes=[
             pltpu.VMEM((pairs, tiles, 2, TILE, 2 * LANES), bf16),
@@ -318,13 +349,14 @@
             pltpu.VMEM((tiles, pairs, 2 * TILE, TILE), f32),
             pltpu.VMEM((pairs, 2 * TILE, LANES), f32),
             pltpu.VMEM((HEADS, seq_len, LANES), f32),
-            pltpu.VMEM((pairs, 2 * TILE, TILE), bf16),
+            pltpu.VMEM((SLOTS, pairs, 2 * TILE, TILE), bf16),
             pltpu.SMEM((2, tiles * tiles), jnp.int32),
+            pltpu.SemaphoreType.DMA((SLOTS,)),
         ],
         cost_estimate=pl.CostEstimate(
             flops=20 * 10**9, bytes_accessed=20 * 10**6, transcendentals=10**7
         ),
-        compiler_params=params(),
+        compiler_params=params(60),
         name="attend",
     )(
         tokens, image_ids, gain1, shift1, q_bias, v_bias, qkv_weight, out_weight, out_bias, gain2,
@@ -379,8 +411,9 @@
         count = ep * per_device
 
         def source(n):
-            device, rest = n // per_device, n % per_device
-            return (rest // own) * slots + device * own + rest % own
+            device, rest = split(n, per_device)
+            which, slot = split(rest, own)
+            return which * slots + device * own + slot
 
         flat = slots_scr[...].reshape(rows * 2 * slots, width)
         moved = dot(selector(count, rows * 2 * slots, source), flat)
@@ -409,7 +442,7 @@
             jax.ShapeDtypeStruct((dp, ep, per_device, width), bf16),
         ],
         scratch_shapes=[pltpu.VMEM((rows, 2, slots, width), bf16)],
-        compiler_params=params(),
+        compiler_params=params(60),
         name="route",
     )(low_two, cotangent, image_ids, slot_image, phi)
 
@@ -426,15 +459,16 @@
     part = seqs * group
 
     def arrived_at(n):
-        which, place = n // part, n % part
-        return (place % group) * per_device + (place // group) * 2 * own + (
-            which % 2
-        ) * own + which // 2
+        which, place = split(n, part)
+        seq, device = split(place, group)
+        slot, kind = split(which, 2)
+        return device * per_device + (seq * 2 + kind) * own + slot
 
     def sent_at(n):
-        device, rest = n // per_device, n % per_device
-        which = (rest % own) * 2 + rest // own % 2
-        return which * part + rest // (2 * own) * group + device
+        device, rest = split(n, per_device)
+        seq_kind, slot = split(rest, own)
+        seq, kind = split(seq_kind, 2)
+        return (slot * 2 + kind) * part + seq * group + device
 
     order = selector(count, count, arrived_at)
     for g in range(devices // group):
@@ -488,7 +522,7 @@
             low(own, count, units),
         ],
         scratch_shapes=[pltpu.VMEM((own, 2, count, width), bf16)],
-        compiler_params=params(),
+        compiler_params=params(24),
         name="experts",
     )(arrived, up_weight, up_bias, down_weight, down_bias_part)
 
@@ -505,17 +539,18 @@
         cost_estimate=pl.CostEstimate(
             flops=4 * own * count * units * width, bytes_accessed=4 * 10**6, transcendentals=0
         ),
-        compiler_params=params(),
+        compiler_params=params(24),
         name="expert_grads",
     )(rows, hidden, pre_grad)
 
 
 def back_kernel(
     core_ref, residual_ref, low_two_ref, dispatch_ref, combine_ref, cot_ref, back_ref, mixed_ref,
-    mixed_rest_ref, qkv_ref, lse_ref, low_one_ref, sums_ref, ids_ref, gain2_ref, phi_ref, out_w_ref,
+    mixed_rest_ref, qkv_ref, recip_ref, low_one_ref, sums_ref, ids_ref, gain2_ref, phi_ref, out_w_ref,
+    probs_ref,
     output_ref, resid_grad_ref, qkv_grad_ref, mine_ref, other_ref,
-    logit_scr, branch_scr, mixed_grad_scr, q_scr, k_scr, o_scr, v_scr, dq_scr, dk_scr, dv_scr,
-    grad_scr, p_scr, ds_scr, phi_grad_scr, rows_scr, list_scr,
+    logit_scr, branch_scr, q_scr, o_scr, v_scr, dq_scr, dk_scr, dv_scr, grad_scr, p_scr, ds_scr,
+    phi_grad_scr, rows_scr, list_scr, sem,
 ):
     row = pl.program_id(0)
     seq_len, width = residual_ref.shape[1:]
@@ -535,6 +570,13 @@
     starts = image_starts(id_row)
     total_tiles = key_tiles(starts, seq_len, list_scr)
 
+    def fetch(n):
+        slot = lax.rem(n, SLOTS)
+        return pltpu.make_async_copy(probs_ref.at[row, n], p_scr.at[slot], sem.at[slot])
+
+    for n in range(SLOTS):
+        fetch(n).start()
+
     dp, ep, per_device, _ = back_ref.shape
     own = slots // ep
     held = back_ref[0].astype(f32)
@@ -544,7 +586,8 @@
 
     def of_kind(kind):
         def wanted(slot):
-            place = slot // own * per_device + (row * 2 + kind) * own + slot % own
+            device, mine = split(slot, own)
+            place = device * per_device + (row * 2 + kind) * own + mine
             return jnp.where(slot < slots, place, -1)
 
         return dot(selector(slot_lanes, ep * per_device, wanted), held).astype(bf16)
@@ -574,65 +617,73 @@
     resid_grad_ref[0] = resid
     branch_scr[...] = resid.astype(bf16)
     bias_sum = jnp.sum(branch_scr[...].astype(f32), axis=0, keepdims=True)
-    mixed_grad_scr[...] = dot(branch_scr[...], out_w_ref[...], NT).astype(bf16)
     grad_scr[:, 3 * width :] += dot(mixed_ref[0], branch_scr[...], TN)
-    product = (mixed_ref[0].astype(f32) + mixed_rest_ref[0].astype(f32)) * mixed_grad_scr[
-        ...
-    ].astype(f32)
+    mixed_grad = dot(branch_scr[...], out_w_ref[...], NT).astype(bf16).astype(f32)
+    picker = head_picker(width)
+    recips = recip_ref[0]
+    recips_top = recips.astype(bf16)
+    recips_low = (recips - recips_top.astype(f32)).astype(bf16)
+    mixed_grad *= dot(recips_top, picker, NT) + dot(recips_low, picker, NT)
+    mixed_grad = mixed_grad.astype(bf16).astype(f32)
+    product = (mixed_ref[0].astype(f32) + mixed_rest_ref[0].astype(f32)) * mixed_grad
     product_top = product.astype(bf16)
-    picker = head_picker(width)
     row_dots = dot(product_top, picker) + dot(
         (product - product_top.astype(f32)).astype(bf16), picker
     )
 
-    columns = image_columns(id_row)
     left = lanes_all < LANES // 2
-    marks_q = query_marks(columns, lanes_all) - three_parts(lse_ref[0], lanes_all)
-    marks_k = key_marks(columns, lanes_all).astype(bf16)
     marks_o = -three_parts(row_dots, lanes_all)
     ones = jnp.where(lanes_all < 24, 1.0, 0.0).astype(bf16)
     for p in range(pairs):
         cut = slice(p * LANES, (p + 1) * LANES)
         scaled = qkv_ref[0, :, cut].astype(f32) * scale
-        mixed_grad = mixed_grad_scr[:, cut].astype(f32)
-        k_scr[p, :, :LANES] = qkv_ref[0, :, width + p * LANES : width + (p + 1) * LANES]
-        k_scr[p, :, LANES:] = marks_k
         v_scr[p, :, :LANES] = qkv_ref[0, :, 2 * width + p * LANES : 2 * width + (p + 1) * LANES]
         v_scr[p, :, LANES:] = ones
         for odd in range(2):
             mine = jnp.logical_not(left) if odd else left
-            for ref, values, marks in ((q_scr, scaled, marks_q), (o_scr, mixed_grad, marks_o)):
-                masked = jnp.where(mine, values, 0.0).astype(bf16)
-                extra = own_lanes(marks, lanes_all, 2 * p + odd).astype(bf16)
-                for t in range(tiles):
-                    ref[p, t, odd, :, :LANES] = masked[t * TILE : (t + 1) * TILE]
-                    ref[p, t, odd, :, LANES:] = extra[t * TILE : (t + 1) * TILE]
+            query = jnp.where(mine, scaled, 0.0).astype(bf16)
+            masked = jnp.where(mine, mixed_grad[:, cut], 0.0).astype(bf16)
+            extra = own_lanes(marks_o, lanes_all, 2 * p + odd).astype(bf16)
+            for t in range(tiles):
+                rows_at = slice(t * TILE, (t + 1) * TILE)
+                q_scr[p, t, odd] = query[rows_at]
+                o_scr[p, t, odd, :, :LANES] = masked[rows_at]
+                o_scr[p, t, odd, :, LANES:] = extra[rows_at]
     dq_scr[...] = jnp.zeros_like(dq_scr)
     dk_scr[...] = jnp.zeros_like(dk_scr)
     dv_scr[...] = jnp.zeros_like(dv_scr)
     tile_left = lane_ids(TILE) < LANES // 2
 
-    def tile(n, carry):
-        i = list_scr[0, n]
-        at = pl.ds(pl.multiple_of(i * TILE, TILE), TILE)
-        keys = pl.ds(pl.multiple_of(list_scr[1, n], LANES), TILE)
-        for p in range(pairs):
-            q2 = q_scr[p, i].reshape(2 * TILE, 2 * LANES)
-            o2 = o_scr[p, i].reshape(2 * TILE, 2 * LANES)
-            probs = jnp.exp(dot(q2, k_scr[p, keys, :], NT))
-            prob_grad = dot(o2, v_scr[p, keys, :], NT)
-            ds_scr[p] = (probs * prob_grad).astype(bf16)
-            p_scr[p] = probs.astype(bf16)
-        for p in range(pairs):
-            q2 = q_scr[p, i].reshape(2 * TILE, 2 * LANES)
-            o2 = o_scr[p, i].reshape(2 * TILE, 2 * LANES)
-            dq2 = dot(ds_scr[p], k_scr[p, keys, :LANES])
-            dq_scr[p, at, :] += jnp.where(tile_left, dq2[:TILE], dq2[TILE:])
-            dk_scr[p, keys, :] += dot(ds_scr[p], q2[:, :LANES], TN)
-            dv_scr[p, keys, :] += dot(p_scr[p], o2[:, :LANES], TN)
-        return carry
-
-    lax.fori_loop(0, total_tiles, tile, 0)
+    def gradients(numbers):
+        for n in numbers:
+            fetch(n).wait()
+        places = []
+        for n in numbers:
+            i = list_scr[0, n]
+            at = pl.ds(pl.multiple_of(i * TILE, TILE), TILE)
+            keys = pl.ds(pl.multiple_of(list_scr[1, n], LANES), TILE)
+            places.append((i, at, keys, lax.rem(n, SLOTS)))
+        for k, (i, at, keys, slot) in enumerate(places):
+            for p in range(pairs):
+                o2 = o_scr[p, i].reshape(2 * TILE, 2 * LANES)
+                prob_grad = dot(o2, v_scr[p, keys, :], NT)
+                ds_scr[k, p] = (p_scr[slot, p].astype(f32) * prob_grad).astype(bf16)
+        for k, (i, at, keys, slot) in enumerate(places):
+            for p in range(pairs):
+                q2 = q_scr[p, i].reshape(2 * TILE, LANES)
+                o2 = o_scr[p, i].reshape(2 * TILE, 2 * LANES)[:, :LANES]
+                k_pair = qkv_ref[0, keys, width + p * LANES : width + (p + 1) * LANES]
+                dq2 = dot(ds_scr[k, p], k_pair)
+                dq_scr[p, at, :] += jnp.where(tile_left, dq2[:TILE], dq2[TILE:])
+                dk_scr[p, keys, :] += dot(ds_scr[k, p], q2, TN)
+                dv_scr[p, keys, :] += dot(p_scr[slot, p], o2, TN)
+        for n in numbers:
+
+            @pl.when(n + SLOTS < total_tiles)
+            def _(n=n):
+                fetch(n + SLOTS).start()
+
+    over_tiles(total_tiles, gradients)
     for p in range(pairs):
         for block, (source, factor) in enumerate(((dq_scr, scale), (dk_scr, 1.0), (dv_scr, 1.0))):
             start = block * width + p * LANES
@@ -699,8 +750,8 @@
 
 
 def back(
-    core, residual, low_two, dispatch, combine, cotangent, returned, mixed, mixed_rest, qkv, lse,
-    low_one, sums, image_ids, gain2, phi, out_weight,
+    core, residual, low_two, dispatch, combine, cotangent, returned, mixed, mixed_rest, qkv,
+    recips, low_one, sums, image_ids, gain2, phi, out_weight, probs,
 ):
     rows, seq_len, width = residual.shape
     lanes = dispatch.shape[2]
@@ -717,6 +768,7 @@
             whole(*returned.shape), block(width), block(width), block(3 * width), block(LANES),
             block(width), pl.BlockSpec((1, 8, width), lambda r: (r, 0, 0)), whole(rows, seq_len),
             whole(width), whole(*phi.shape), whole(width, width),
+            pl.BlockSpec(memory_space=pl.ANY),
         ],
         out_specs=[
             block(width), block(width), block(3 * width), whole(devices // 2, share, LANES),
@@ -732,29 +784,28 @@
         scratch_shapes=[
             pltpu.VMEM((seq_len, lanes), bf16),
             pltpu.VMEM((seq_len, width), bf16),
-            pltpu.VMEM((seq_len, width), bf16),
-            pltpu.VMEM((pairs, tiles, 2, TILE, 2 * LANES), bf16),
-            pltpu.VMEM((pairs, seq_len, 2 * LANES), bf16),
+            pltpu.VMEM((pairs, tiles, 2, TILE, LANES), bf16),
             pltpu.VMEM((pairs, tiles, 2, TILE, 2 * LANES), bf16),
             pltpu.VMEM((pairs, seq_len, 2 * LANES), bf16),
             pltpu.VMEM((pairs, seq_len, LANES), f32),
             pltpu.VMEM((pairs, seq_len, LANES), f32),
             pltpu.VMEM((pairs, seq_len, LANES), f32),
             pltpu.VMEM((width, 4 * width), f32),
-            pltpu.VMEM((pairs, 2 * TILE, TILE), bf16),
-            pltpu.VMEM((pairs, 2 * TILE, TILE), bf16),
+            pltpu.VMEM((SLOTS, pairs, 2 * TILE, TILE), bf16),
+            pltpu.VMEM((GROUP, pairs, 2 * TILE, TILE), bf16),
             pltpu.VMEM((lanes, width), f32),
             pltpu.VMEM((8, width), f32),
             pltpu.SMEM((2, tiles * tiles), jnp.int32),
+            pltpu.SemaphoreType.DMA((SLOTS,)),
         ],
         cost_estimate=pl.CostEstimate(
             flops=60 * 10**9, bytes_accessed=20 * 10**6, transcendentals=10**7
         ),
-        compiler_params=params(),
+        compiler_params=params(60),
         name="back",
     )(
         core, residual, low_two, dispatch, combine, cotangent, returned, mixed, mixed_rest, qkv,
-        lse, low_one, sums, image_ids, gain2, phi, out_weight,
+        recips, low_one, sums, image_ids, gain2, phi, out_weight, probs,
     )
 
 
@@ -796,9 +847,22 @@
         cost_estimate=pl.CostEstimate(
             flops=6 * 10**9, bytes_accessed=10**7, transcendentals=0
         ),
-        compiler_params=params(),
+        compiler_params=params(60),
         name="input_back",
     )(tokens, qkv_grad, resid_grad, gain1, qkv_weight)
+
+
+def add_kernel(one_ref, two_ref, sum_ref):
+    sum_ref[...] = (one_ref[...].astype(f32) + two_ref[...].astype(f32)).astype(bf16)
+
+
+def add(one, two):
+    return pl.pallas_call(
+        add_kernel,
+        out_shape=jax.ShapeDtypeStruct(one.shape, bf16),
+        compiler_params=params(16),
+        name="add",
+    )(one, two)
 
 
 def fold_kernel(collected_ref, ln1_ref, shared_ref):
@@ -821,7 +885,7 @@
     return pl.pallas_call(
         fold_kernel,
         out_shape=jax.ShapeDtypeStruct(collected.shape, bf16),
-        compiler_params=params(),
+        compiler_params=params(16),
         name="fold",
     )(collected, ln1_rows)
 
@@ -909,7 +973,7 @@
             jax.ShapeDtypeStruct((3,), f32),
         ],
         scratch_shapes=[pltpu.VMEM((2 * half, PIECE, LANES), f32)],
-        compiler_params=params(),
+        compiler_params=params(16),
         name="finish",
     )(place, mine, other)
 
@@ -934,7 +998,7 @@
     phi = exchange(jnp.broadcast_to(slot_params.T[None], (ep, own, width)), "expert")
     phi = phi.reshape(slots, width)
 
-    low_one, qkv, mixed, mixed_rest, lse, residual, low_two, sums = attend(
+    low_one, qkv, mixed, mixed_rest, recips, residual, low_two, sums, probs = attend(
         tokens, image_ids, ln1_gain, ln1_bias, query_bias, value_bias, qkv_weight, out_weight,
         out_bias, ln2_gain, ln2_bias,
     )
@@ -945,17 +1009,18 @@
         arrived, up_weight, up_bias, down_weight, down_bias * (1.0 / dp)
     )
     returned = exchange(parts, ("y", "core", "expert"))
-    up_grad, up_bias_grad, down_grad, down_bias_grad = expert_grads(rows, hidden, pre_grad)
+    returned, (up_grad, up_bias_grad, down_grad, down_bias_grad) = lax.optimization_barrier(
+        (returned, tuple(expert_grads(rows, hidden, pre_grad)))
+    )
 
     output, resid_grad, qkv_grad, mine, other = back(
         core.reshape(1), residual, low_two, dispatch, combine, cotangent,
-        returned.reshape(dp, ep, per_device, width), mixed, mixed_rest, qkv, lse, low_one, sums,
-        image_ids, ln2_gain, phi, out_weight,
+        returned.reshape(dp, ep, per_device, width), mixed, mixed_rest, qkv, recips, low_one, sums,
+        image_ids, ln2_gain, phi, out_weight, probs,
     )
 
     met = lax.ppermute(other, "core", swap)
-    chip = (mine.astype(f32) + met.astype(f32)).astype(bf16)
-    collected = exchange(chip, across)
+    collected = exchange(add(mine, met), across)
     input_grad, ln1_rows = input_back(tokens, qkv_grad, resid_grad, ln1_gain, qkv_weight)
     shares = exchange(fold(collected, ln1_rows), across)
     others = lax.ppermute(shares, "core", swap)

time: 189 us -> 175 us (0.926)
  Pallas kernels: 103 us -> 92.9 us
  other arithmetic: 3.41 us -> 0.08 us
    pallas_call x1, Pallas kernels: 51.2 us -> 45 us  [back(): pl.pallas_call(back_kernel, grid=(rows,), in_specs=[pl.BlockSpec(memory_s...]
    all_to_all x4, starting transfers between devices: 24 us -> 26.5 us  [exchange(): return lax.all_to_all(values, over, split_axis=0, concat_axis=0, tiled=True)]
    ppermute x1, starting transfers between devices: 2.68 us -> 0.21 us  [local(): met = lax.ppermute(other, 'core', swap)]
    convert_element_type x1 -> x0, other arithmetic: 2.09 us -> none  [local(): chip = (mine.astype(f32) + met.astype(f32)).astype(bf16)]
    ppermute x1, waiting for transfers between devices: 0.01 us -> 2.02 us  [local(): others = lax.ppermute(shares, 'core', swap)]
    pallas_call x1, Pallas kernels: 2.02 us -> 0.1 us  [fold(): pl.pallas_call(fold_kernel, out_shape=jax.ShapeDtypeStruct(collected.shap...]
  transfers between devices with their start and end apart: 6 -> 6, of which waited for: 4 -> 5; matrix products, arithmetic and copies ran while one was open for 1% -> 0% of each run, Pallas kernels for 20% -> 21%
where the time goes in v3:
time: 175 us; the launch traced here: 176 us
  Pallas kernels  92.9 us (53%)
  waiting for transfers between devices  28.8 us (16%)
  starting transfers between devices  26.7 us (15%)
  blocking collectives  21.9 us (13%)
  local copies, waits for them, and re-layouts  4.38 us (3%)
    pallas_call x1, Pallas kernels, back(): pl.pallas_call(back_kernel, grid=(rows,), in_specs=[pl.BlockSpec(memory_s...  45 us
    pallas_call x1, Pallas kernels, attend(): pl.pallas_call(attend_kernel, grid=(rows,), in_specs=[block(width), whole...  27.2 us
    all_to_all x4, starting transfers between devices, exchange(): return lax.all_to_all(values, over, split_axis=0, concat_axis=0, tiled=True)  26.5 us
    all_to_all x4, waiting for transfers between devices, exchange(): return lax.all_to_all(values, over, split_axis=0, concat_axis=0, tiled=True)  24.6 us
    all_to_all x1, blocking collectives, exchange(): return lax.all_to_all(values, over, split_axis=0, concat_axis=0, tiled=True)  21.9 us
    pallas_call x1, Pallas kernels, input_back(): pl.pallas_call(input_kernel, grid=(rows,), in_specs=[block(width), block(...  8.41 us
    pallas_call x1, Pallas kernels, route(): pl.pallas_call(route_kernel, grid=(rows,), in_specs=[block(width), block(...  5.33 us
  transfers between devices with their start and end apart: 6, of which 5 were waited for; matrix products, arithmetic and copies ran while one was open for 0% of the time, Pallas kernels for 21%

profile of v3, /device:TPU:0, one launch (start us, length us, event | category | flops | bytes accessed | tf_op | source)
XLA Modules:
  0.0 175.7 jit_solution(7627640819605576267)
XLA Ops:
  0.7 1.3 broadcast_in_dim.2
  1.9 7.3 %all-to-all-start = ((bf16[8,2,384]{2,1,0:T(2,128)(2,1)}), bf16[8,2,384]{2,1,0:T(2,128)(2,1)S(1)}, u32[]{:S(2)}, u32[]{:S(2)}) async-start(bf16[8,2,384]{2,1,0:T(2,128)(2,1)} %broadcast_in_dim.2), calls=%async_computation | async-start | bytes 24576 | tf_op jit(solution)/shard_map/all_to_all | solution.py:996
  9.2 27.2 %attend.1 = (bf16[2,1024,384]{2,1,0:T(8,128)(2,1)}, bf16[2,1024,1152]{2,1,0:T(8,128)(2,1)}, bf16[2,1024,384]{2,1,0:T(8,128)(2,1)}, bf16[2,1024,384]{2,1,0:T(8,12...) custom-call(bf16[2,1024,384]{2,1,0:T(8,128)(2,1)} %tokens_ref.3, ...), custom_call_target="tpu_custom_call" | custom-call | flops 20000000000 | bytes 20000000 | tf_op jit(solution)/shard_map/attend/pallas_call | solution.py:326
  36.4 0.0 all-to-all-done
  36.4 0.6 reshape.48.phi_ref
  37.0 5.3 %route.1 = (f32[2,1024,128]{2,1,0:T(8,128)}, f32[2,1024,128]{2,1,0:T(8,128)}, bf16[4,8,8,384]{3,2,1,0:T(8,128)(2,1)}) custom-call(bf16[2,1024,384]{2,1,0:T(8,128)(2,1)} %get-tuple-element.61.low_two_ref, bf16[2,1024,384]{2,1,0:T(8,128)(2,1)} %cot_ref.3, s32[2,1024]{1,0:T(2,128)} %ids_ref.5, s32[2,16]{1,0:T(2,128)} %slot_ref.1, bf16[16,384]{1,0:T(8,128)(2,1)} %reshape.48.phi_ref), custom_call_target="tpu_custom_call" | custom-call | tf_op jit(solution)/shard_map/route/pallas_call | solution.py:431
  42.4 8.4 %all-to-all-start.1 = ((bf16[32,8,384]{2,1,0:T(8,128)(2,1)}), bf16[32,8,384]{2,1,0:T(8,128)(2,1)S(1)}, u32[]{:S(2)}, u32[]{:S(2)}) async-start(bf16[32,8,384]{2,1,0:T(8,128)(2,1)} %bitcast.7), calls=%async_computation.1 | async-start | bytes 393216 | tf_op jit(solution)/shard_map/all_to_all | solution.py:996
  50.8 0.0 copy-done.6
  50.8 8.5 %all-to-all-done.1.arrived_ref = bf16[32,8,384]{2,1,0:T(8,128)(2,1)S(1)} async-done(((bf16[32,8,384]{2,1,0:T(8,128)(2,1)}), bf16[32,8,384]{2,1,0:T(8,128)(2,1)S(1)}, u32[]{:S(2)}, u32[]{:S(2)}) %all-to-all-start.1) | async-done | bytes 196640 | tf_op jit(solution)/shard_map/all_to_all | solution.py:996
  59.3 0.0 copy-done.1
  59.3 0.0 copy-done.2
  59.3 0.0 copy-done.4
  59.3 1.9 %experts.1 = (bf16[32,8,384]{2,1,0:T(8,128)(2,1)}, bf16[2,2,64,384]{3,2,1,0:T(8,128)(2,1)S(1)}, bf16[2,64,384]{2,1,0:T(8,128)(2,1)S(1)}, bf16[2,64,384]{2,1,0:T(8,128)(2,1)S(1)}) custom-call(bf16[32,8,384]{2,1,0:T(8,128)(2,1)S(1)} %all-to-all-done.1.arrived_ref, bf16[2,384,384]{2,1,0:T(8,128)(2,1)S(1)} %copy-done.1, bf16[2,384]{1,0:T(2,128)(2,1)S(1)} %copy-done.4, ...), custom_call_target="tpu_custom_call" | custom-call | tf_op jit(solution)/shard_map/experts/pallas_call | solution.py:518
  61.2 3.2 %all-to-all-start.2 = ((bf16[32,8,384]{2,1,0:T(8,128)(2,1)}), bf16[32,8,384]{2,1,0:T(8,128)(2,1)S(1)}, u32[]{:S(2)}, u32[]{:S(2)}) async-start(bf16[32,8,384]{2,1,0:T(8,128)(2,1)} %get-tuple-element.65), calls=%async_computation.2 | async-start | bytes 393216 | tf_op jit(solution)/shard_map/all_to_all | solution.py:996
  64.4 1.8 %expert_grads.1 = (f32[2,384,384]{2,1,0:T(8,128)}, f32[2,384]{1,0:T(2,128)}, f32[2,384,384]{2,1,0:T(8,128)}, f32[2,384]{1,0:T(2,128)}) custom-call(bf16[2,2,64,384]{3,2,1,0:T(8,128)(2,1)S(1)} %get-tuple-element.66.rows_ref, bf16[2,64,384]{2,1,0:T(8,128)(2,1)S(1)} %get-tuple-element.67.hidden_ref, bf16[2,64,384]{2,1,0:T(8,128)(2,1)S(1)} %get-tuple-element.68.pre_grad_ref), custom_call_target="tpu_custom_call" | custom-call | flops 75497472 | bytes 4000000 | tf_op jit(solution)/shard_map/expert_grads/pallas_call | solution.py:534
  66.3 6.5 %all-to-all-done.2 = bf16[32,8,384]{2,1,0:T(8,128)(2,1)S(1)} async-done(((bf16[32,8,384]{2,1,0:T(8,128)(2,1)}), bf16[32,8,384]{2,1,0:T(8,128)(2,1)S(1)}, u32[]{:S(2)}, u32[]{:S(2)}) %all-to-all-start.2) | async-done | bytes 196640 | tf_op jit(solution)/shard_map/all_to_all | solution.py:996
  72.8 0.7 copy-done.5
  73.5 45.0 %back.1 = (bf16[2,1024,384]{2,1,0:T(8,128)(2,1)}, f32[2,1024,384]{2,1,0:T(8,128)}, bf16[2,1024,1152]{2,1,0:T(8,128)(2,1)}, bf16[16,160,128]{2,1,0:T(8,128)(2,1)}, bf16[16,160,128]{2,1,0:T(8,128)(2,1)}) custom-call(s32[1]{0:T(128)} %bitcast.core_ref, f32[2,1024,384]{2,1,0:T(8,128)} %get-tuple-element.60.residual_ref, ...), custom_call_target="tpu_custom_call" | custom-call | flops 60000002048 | bytes 20000000 | tf_op jit(solution)/shard_map/back/pallas_call | solution.py:762
  118.5 0.2 collective-permute-start
  118.7 2.2 %collective-permute-done.two_ref = bf16[16,160,128]{2,1,0:T(8,128)(2,1)S(1)} collective-permute-done((bf16[16,160,128]{2,1,0:T(8,128)(2,1)}, bf16[16,160,128]{2,1,0:T(8,128)(2,1)S(1)}, u32[]{:S(2)}, u32[]{:S(2)}) %collective-permute-start) | collective-permute-done | bytes 655392 | tf_op jit(solution)/shard_map/ppermute | solution.py:1022
  120.8 1.1 copy-done
  121.9 1.0 add.3
  122.9 7.6 %all-to-all-start.3 = ((bf16[16,160,128]{2,1,0:T(8,128)(2,1)}), bf16[16,160,128]{2,1,0:T(8,128)(2,1)S(1)}, u32[]{:S(2)}, u32[]{:S(2)}) async-start(bf16[16,160,128]{2,1,0:T(8,128)(2,1)} %add.3), calls=%async_computation.3 | async-start | bytes 1310720 | tf_op jit(solution)/shard_map/all_to_all | solution.py:996
  130.5 8.4 %input_back.1 = (bf16[2,1024,384]{2,1,0:T(8,128)(2,1)}, f32[8,384]{1,0:T(8,128)}) custom-call(bf16[2,1024,384]{2,1,0:T(8,128)(2,1)} %tokens_ref.3, bf16[2,1024,1152]{2,1,0:T(8,128)(2,1)} %get-tuple-element.82.qkv_grad_ref, f32[2,1024,384]{2,1,0:T(8,128)} %get-tuple-element.83.resid_grad_ref, f32[384]{0:T(512)} %gain1_ref.3, bf16[384,1152]{1,0:T(8,128)(2,1)} %qkv_w_ref.3), custom_call_target="tpu_custom_call" | custom-call | flops 6000000000 | bytes 10000000 | tf_op jit(solution)/shard_map/input_back/pallas_call | solution.py:836
  138.9 9.5 %all-to-all-done.3.collected_ref = bf16[16,160,128]{2,1,0:T(8,128)(2,1)S(1)} async-done(((bf16[16,160,128]{2,1,0:T(8,128)(2,1)}), bf16[16,160,128]{2,1,0:T(8,128)(2,1)S(1)}, u32[]{:S(2)}, u32[]{:S(2)}) %all-to-all-start.3) | async-done | bytes 655392 | tf_op jit(solution)/shard_map/all_to_all | solution.py:996
  148.5 0.7 copy-done.3
  149.2 0.1 fold.1
  149.3 21.9 %all_to_all.25.refs_1_ = bf16[16,160,128]{2,1,0:T(8,128)(2,1)S(1)} all-to-all(bf16[16,160,128]{2,1,0:T(8,128)(2,1)S(1)} %fold.1), channel_id=1, replica_groups=mesh['y'=2,'core'=2,'expert'=8] {'y','expert'}, dimensions={0} | all-to-all | bytes 1310720 | tf_op jit(solution)/shard_map/all_to_all | solution.py:996
  171.2 0.0 collective-permute-start.1
  171.2 0.1 pad_add_fusion.refs_0_
  171.3 2.0 %collective-permute-done.1.refs_2_ = bf16[16,160,128]{2,1,0:T(8,128)(2,1)S(1)} collective-permute-done((bf16[16,160,128]{2,1,0:T(8,128)(2,1)S(1)}, bf16[16,160,128]{2,1,0:T(8,128)(2,1)S(1)}, u32[]{:S(2)}, u32[]{:S(2)}) %collective-permute-start.1) | collective-permute-done | bytes 655392 | tf_op jit(solution)/shard_map/ppermute | solution.py:1026
  173.3 2.2 %finish.1 = (f32[384,1152]{1,0:T(8,128)}, f32[384,384]{1,0:T(8,128)}, f32[384]{0:T(512)}, f32[384]{0:T(512)}, f32[384]{0:T(512)}, /*index=5*/f32[384]{0:T(512)},...) custom-call(s32[2]{0:T(128)S(1)} %pad_add_fusion.refs_0_, ...), custom_call_target="tpu_custom_call" | custom-call | tf_op jit(solution)/shard_map/finish/pallas_call | solution.py:965
  (8 shorter events, 0.0 us)
Async XLA Ops:
  1.9 34.5 %all-to-all-start = ((bf16[8,2,384]{2,1,0:T(2,128)(2,1)}), bf16[8,2,384]{2,1,0:T(2,128)(2,1)S(1)}, u32[]{:S(2)}, u32[]{:S(2)}) async-start(bf16[8,2,384]{2,1,0:T(2,128)(2,1)} %broadcast_in_dim.2), calls=%async_computation | async-start | bytes 24576 | tf_op jit(solution)/shard_map/all_to_all | solution.py:996
  37.0 13.8 %copy-start.6 = (f32[2,384]{1,0:T(2,128)S(1)}, f32[2,384]{1,0:T(2,128)}, u32[]{:S(2)}) copy-start(f32[2,384]{1,0:T(2,128)} %param.34) | copy-start | bytes 9220
  37.0 22.3 %copy-start.1 = (bf16[2,384,384]{2,1,0:T(8,128)(2,1)S(1)}, bf16[2,384,384]{2,1,0:T(8,128)(2,1)}, u32[]{:S(2)}) copy-start(bf16[2,384,384]{2,1,0:T(8,128)(2,1)} %up_ref.1) | copy-start | bytes 1769476
  37.0 22.3 %copy-start.2 = (bf16[2,384,384]{2,1,0:T(8,128)(2,1)S(1)}, bf16[2,384,384]{2,1,0:T(8,128)(2,1)}, u32[]{:S(2)}) copy-start(bf16[2,384,384]{2,1,0:T(8,128)(2,1)} %down_ref.1) | copy-start | bytes 1769476
  37.0 22.3 %copy-start.4 = (bf16[2,384]{1,0:T(2,128)(2,1)S(1)}, bf16[2,384]{1,0:T(2,128)(2,1)}, u32[]{:S(2)}) copy-start(bf16[2,384]{1,0:T(2,128)(2,1)} %up_bias_ref.1) | copy-start | bytes 4612
  42.4 17.0 %all-to-all-start.1 = ((bf16[32,8,384]{2,1,0:T(8,128)(2,1)}), bf16[32,8,384]{2,1,0:T(8,128)(2,1)S(1)}, u32[]{:S(2)}, u32[]{:S(2)}) async-start(bf16[32,8,384]{2,1,0:T(8,128)(2,1)} %bitcast.7), calls=%async_computation.1 | async-start | bytes 393216 | tf_op jit(solution)/shard_map/all_to_all | solution.py:996
  61.2 11.6 %all-to-all-start.2 = ((bf16[32,8,384]{2,1,0:T(8,128)(2,1)}), bf16[32,8,384]{2,1,0:T(8,128)(2,1)S(1)}, u32[]{:S(2)}, u32[]{:S(2)}) async-start(bf16[32,8,384]{2,1,0:T(8,128)(2,1)} %get-tuple-element.65), calls=%async_computation.2 | async-start | bytes 393216 | tf_op jit(solution)/shard_map/all_to_all | solution.py:996
  72.8 0.7 copy-start.5
  118.5 2.4 %collective-permute-start = (bf16[16,160,128]{2,1,0:T(8,128)(2,1)}, bf16[16,160,128]{2,1,0:T(8,128)(2,1)S(1)}, u32[]{:S(2)}, u32[]{:S(2)}) collective-permute-start(bf16[16,160,128]{2,1,0:T(8,128)(2,1)} %get-tuple-element.86), channel_id=1, source_target_pairs={{0,8},{8,0},{1,9},{9,1},{2,10},{10,2},{3,11},{11,3},{4,12},{12,4},... | collective-permute-start | bytes 1966088 | tf_op jit(solution)/shard_map/ppermute | solution.py:1022
  120.8 1.1 copy-start
  122.9 25.6 %all-to-all-start.3 = ((bf16[16,160,128]{2,1,0:T(8,128)(2,1)}), bf16[16,160,128]{2,1,0:T(8,128)(2,1)S(1)}, u32[]{:S(2)}, u32[]{:S(2)}) async-start(bf16[16,160,128]{2,1,0:T(8,128)(2,1)} %add.3), calls=%async_computation.3 | async-start | bytes 1310720 | tf_op jit(solution)/shard_map/all_to_all | solution.py:996
  148.5 0.7 copy-start.3
  171.2 2.1 %collective-permute-start.1 = (bf16[16,160,128]{2,1,0:T(8,128)(2,1)S(1)}, bf16[16,160,128]{2,1,0:T(8,128)(2,1)S(1)}, u32[]{:S(2)}, u32[]{:S(2)}) collective-permute-start(bf16[16,160,128]{2,1,0:T(8,128)(2,1)S(1)} %all_to_all.25.refs_1_), channel_id=1, source_target_pairs={{0,8},{8,0},{1,9},{9,1},{2,10},{10,2},{3,11},{11,3},{4,12},{12,4},... | collective-permute-start | bytes 1966088 | tf_op jit(solution)/shard_map/ppermute | solution.py:1026

commit v4 on v3

--- a/solution.py
+++ b/solution.py
@@ -153,7 +153,8 @@
     tokens_ref, ids_ref, gain1_ref, shift1_ref, q_bias_ref, v_bias_ref, qkv_w_ref, out_w_ref,
     out_bias_ref, gain2_ref, shift2_ref,
     low_one_ref, qkv_ref, mixed_ref, mixed_rest_ref, recip_ref, residual_ref, low_two_ref, sums_ref,
-    probs_ref, q_scr, k_scr, v_scr, s_scr, top_scr, acc_scr, p_scr, list_scr, sem,
+    probs_ref, low_one_scr, qkv_scr, q_scr, k_scr, v_scr, s_scr, top_scr, acc_scr, p_scr, list_scr,
+    sem, out_sem,
 ):
     row = pl.program_id(0)
     seq_len, width = tokens_ref.shape[1:]
@@ -169,17 +170,30 @@
     marks_q = query_marks(columns, lanes).astype(bf16)
     marks_k = key_marks(columns, lanes).astype(bf16)
 
+    def store_one(r):
+        return pltpu.make_async_copy(low_one_scr, low_one_ref.at[r], out_sem.at[0])
+
+    def store_qkv(r):
+        return pltpu.make_async_copy(qkv_scr, qkv_ref.at[r], out_sem.at[1])
+
+    @pl.when(row > 0)
+    def _():
+        store_one(row - 1).wait()
+        store_qkv(row - 1).wait()
+
     stream = tokens_ref[0].astype(f32)
     hat, _ = norm_parts(stream)
     low_one = (hat * as_row(gain1_ref) + as_row(shift1_ref)).astype(bf16)
-    low_one_ref[0] = low_one
+    low_one_scr[...] = low_one
     projected = dot(low_one, qkv_w_ref[...])
     query = (projected[:, :width] + as_row(q_bias_ref)).astype(bf16)
     key = projected[:, width : 2 * width].astype(bf16)
     value = (projected[:, 2 * width :] + as_row(v_bias_ref)).astype(bf16)
-    qkv_ref[0, :, :width] = query
-    qkv_ref[0, :, width : 2 * width] = key
-    qkv_ref[0, :, 2 * width :] = value
+    qkv_scr[:, :width] = query
+    qkv_scr[:, width : 2 * width] = key
+    qkv_scr[:, 2 * width :] = value
+    store_one(row).start()
+    store_qkv(row).start()
     for p in range(pairs):
         cut = slice(p * LANES, (p + 1) * LANES)
         scaled = query[:, cut].astype(f32) * scale
@@ -293,6 +307,12 @@
     low_two_ref[0] = (hat_two * as_row(gain2_ref) + as_row(shift2_ref)).astype(bf16)
     for late in range(SLOTS):
         leave(total_tiles - SLOTS + late).wait()
+
+    @pl.when(row == pl.num_programs(0) - 1)
+    def _():
+        store_one(row).wait()
+        store_qkv(row).wait()
+
     stream = tokens_ref[0].astype(f32)
     sums_ref[0] = jnp.concatenate(
         [
@@ -332,7 +352,8 @@
             whole(width), whole(width),
         ],
         out_specs=[
-            block(width), block(3 * width), block(width), block(width), block(LANES),
+            pl.BlockSpec(memory_space=pl.ANY), pl.BlockSpec(memory_space=pl.ANY),
+            block(width), block(width), block(LANES),
             block(width), block(width), pl.BlockSpec((1, 8, width), lambda r: (r, 0, 0)),
             pl.BlockSpec(memory_space=pl.ANY),
         ],
@@ -343,6 +364,8 @@
             jax.ShapeDtypeStruct((rows, tiles * tiles, pairs, 2 * TILE, TILE), bf16),
         ],
         scratch_shapes=[
+            pltpu.VMEM((seq_len, width), bf16),
+            pltpu.VMEM((seq_len, 3 * width), bf16),
             pltpu.VMEM((pairs, tiles, 2, TILE, 2 * LANES), bf16),
             pltpu.VMEM((pairs, seq_len, 2 * LANES), bf16),
             pltpu.VMEM((HEADS, seq_len, LANES), bf16),
@@ -352,6 +375,7 @@
             pltpu.VMEM((SLOTS, pairs, 2 * TILE, TILE), bf16),
             pltpu.SMEM((2, tiles * tiles), jnp.int32),
             pltpu.SemaphoreType.DMA((SLOTS,)),
+            pltpu.SemaphoreType.DMA((2,)),
         ],
         cost_estimate=pl.CostEstimate(
             flops=20 * 10**9, bytes_accessed=20 * 10**6, transcendentals=10**7
@@ -545,12 +569,13 @@
 
 
 def back_kernel(
-    core_ref, residual_ref, low_two_ref, dispatch_ref, combine_ref, cot_ref, back_ref, mixed_ref,
-    mixed_rest_ref, qkv_ref, recip_ref, low_one_ref, sums_ref, ids_ref, gain2_ref, phi_ref, out_w_ref,
-    probs_ref,
-    output_ref, resid_grad_ref, qkv_grad_ref, mine_ref, other_ref,
+    core_ref, residual_ref, low_two_ref, dispatch_ref, combine_ref, cot_ref, back_ref, sums_ref,
+    ids_ref, gain2_ref, phi_ref, out_w_ref, mixed_hbm, mixed_rest_hbm, qkv_hbm, recip_hbm,
+    low_one_hbm, probs_ref,
+    output_hbm, resid_grad_hbm, qkv_grad_ref, mine_ref, other_ref,
+    mixed_ref, mixed_rest_ref, qkv_ref, recip_ref, low_one_ref, output_ref, resid_grad_ref,
     logit_scr, branch_scr, q_scr, o_scr, v_scr, dq_scr, dk_scr, dv_scr, grad_scr, p_scr, ds_scr,
-    phi_grad_scr, rows_scr, list_scr, sem,
+    phi_grad_scr, rows_scr, list_scr, sem, in_sem, out_sem,
 ):
     row = pl.program_id(0)
     seq_len, width = residual_ref.shape[1:]
@@ -574,8 +599,24 @@
         slot = lax.rem(n, SLOTS)
         return pltpu.make_async_copy(probs_ref.at[row, n], p_scr.at[slot], sem.at[slot])
 
+    def brought(k, source, target):
+        return pltpu.make_async_copy(source.at[row], target, in_sem.at[k])
+
+    def taken(k, source, target):
+        return pltpu.make_async_copy(source, target.at[row], out_sem.at[k])
+
+    mixed_in = brought(0, mixed_hbm, mixed_ref)
+    rest_in = brought(1, mixed_rest_hbm, mixed_rest_ref)
+    recip_in = brought(2, recip_hbm, recip_ref)
+    qkv_in = brought(3, qkv_hbm, qkv_ref)
+    low_one_in = brought(4, low_one_hbm, low_one_ref)
+    output_out = taken(0, output_ref, output_hbm)
+    resid_out = taken(1, resid_grad_ref, resid_grad_hbm)
+    for copy in (mixed_in, rest_in, recip_in, qkv_in):
+        copy.start()
     for n in range(SLOTS):
         fetch(n).start()
+    low_one_in.start()
 
     dp, ep, per_device, _ = back_ref.shape
     own = slots // ep
@@ -599,7 +640,8 @@
     cot = cot_ref[0]
     low_two = low_two_ref[0]
     moe_out = dot(combine.astype(bf16), expert_out)
-    output_ref[0] = (residual_ref[0] + moe_out).astype(bf16)
+    output_ref[...] = (residual_ref[0] + moe_out).astype(bf16)
+    output_out.start()
     moe_sq = jnp.sum(moe_out * moe_out, axis=0, keepdims=True)
     combine_grad = dot(cot, expert_out, NT)
     dispatch_grad = dot(low_two, slot_grad, NT)
@@ -614,30 +656,35 @@
     resid = cot.astype(f32) + norm_back(grad, hat, recip, as_row(gain2_ref))
     gain_sum = jnp.sum(grad * hat, axis=0, keepdims=True)
     shift_sum = jnp.sum(grad, axis=0, keepdims=True)
-    resid_grad_ref[0] = resid
+    resid_grad_ref[...] = resid
+    resid_out.start()
     branch_scr[...] = resid.astype(bf16)
     bias_sum = jnp.sum(branch_scr[...].astype(f32), axis=0, keepdims=True)
-    grad_scr[:, 3 * width :] += dot(mixed_ref[0], branch_scr[...], TN)
+    mixed_in.wait()
+    grad_scr[:, 3 * width :] += dot(mixed_ref[...], branch_scr[...], TN)
     mixed_grad = dot(branch_scr[...], out_w_ref[...], NT).astype(bf16).astype(f32)
     picker = head_picker(width)
-    recips = recip_ref[0]
+    recip_in.wait()
+    recips = recip_ref[...]
     recips_top = recips.astype(bf16)
     recips_low = (recips - recips_top.astype(f32)).astype(bf16)
     mixed_grad *= dot(recips_top, picker, NT) + dot(recips_low, picker, NT)
     mixed_grad = mixed_grad.astype(bf16).astype(f32)
-    product = (mixed_ref[0].astype(f32) + mixed_rest_ref[0].astype(f32)) * mixed_grad
+    rest_in.wait()
+    product = (mixed_ref[...].astype(f32) + mixed_rest_ref[...].astype(f32)) * mixed_grad
     product_top = product.astype(bf16)
     row_dots = dot(product_top, picker) + dot(
         (product - product_top.astype(f32)).astype(bf16), picker
     )
 
+    qkv_in.wait()
     left = lanes_all < LANES // 2
     marks_o = -three_parts(row_dots, lanes_all)
     ones = jnp.where(lanes_all < 24, 1.0, 0.0).astype(bf16)
     for p in range(pairs):
         cut = slice(p * LANES, (p + 1) * LANES)
-        scaled = qkv_ref[0, :, cut].astype(f32) * scale
-        v_scr[p, :, :LANES] = qkv_ref[0, :, 2 * width + p * LANES : 2 * width + (p + 1) * LANES]
+        scaled = qkv_ref[:, cut].astype(f32) * scale
+        v_scr[p, :, :LANES] = qkv_ref[:, 2 * width + p * LANES : 2 * width + (p + 1) * LANES]
         v_scr[p, :, LANES:] = ones
         for odd in range(2):
             mine = jnp.logical_not(left) if odd else left
@@ -672,7 +719,7 @@
             for p in range(pairs):
                 q2 = q_scr[p, i].reshape(2 * TILE, LANES)
                 o2 = o_scr[p, i].reshape(2 * TILE, 2 * LANES)[:, :LANES]
-                k_pair = qkv_ref[0, keys, width + p * LANES : width + (p + 1) * LANES]
+                k_pair = qkv_ref[keys, width + p * LANES : width + (p + 1) * LANES]
                 dq2 = dot(ds_scr[k, p], k_pair)
                 dq_scr[p, at, :] += jnp.where(tile_left, dq2[:TILE], dq2[TILE:])
                 dk_scr[p, keys, :] += dot(ds_scr[k, p], q2, TN)
@@ -688,12 +735,16 @@
         for block, (source, factor) in enumerate(((dq_scr, scale), (dk_scr, 1.0), (dv_scr, 1.0))):
             start = block * width + p * LANES
             qkv_grad_ref[0, :, start : start + LANES] = (source[p] * factor).astype(bf16)
-    grad_scr[:, : 3 * width] += dot(low_one_ref[0], qkv_grad_ref[0], TN)
+    low_one_in.wait()
+    grad_scr[:, : 3 * width] += dot(low_one_ref[...], qkv_grad_ref[0], TN)
     query_sum = jnp.sum(qkv_grad_ref[0, :, :width].astype(f32), axis=0, keepdims=True)
     value_sum = jnp.sum(qkv_grad_ref[0, :, 2 * width :].astype(f32), axis=0, keepdims=True)
     rows_scr[...] += jnp.concatenate(
         [query_sum, value_sum, bias_sum, gain_sum, shift_sum, moe_sq, sums_ref[0, 0:2, :]], axis=0
     )
+
+    output_out.wait()
+    resid_out.wait()
 
     @pl.when(row == pl.num_programs(0) - 1)
     def _():
@@ -750,8 +801,8 @@
 
 
 def back(
-    core, residual, low_two, dispatch, combine, cotangent, returned, mixed, mixed_rest, qkv,
-    recips, low_one, sums, image_ids, gain2, phi, out_weight, probs,
+    core, residual, low_two, dispatch, combine, cotangent, returned, sums, image_ids, gain2, phi,
+    out_weight, mixed, mixed_rest, qkv, recips, low_one, probs,
 ):
     rows, seq_len, width = residual.shape
     lanes = dispatch.shape[2]
@@ -765,13 +816,12 @@
         in_specs=[
             pl.BlockSpec(memory_space=pltpu.SMEM),
             block(width), block(width), block(lanes), block(lanes), block(width),
-            whole(*returned.shape), block(width), block(width), block(3 * width), block(LANES),
-            block(width), pl.BlockSpec((1, 8, width), lambda r: (r, 0, 0)), whole(rows, seq_len),
-            whole(width), whole(*phi.shape), whole(width, width),
-            pl.BlockSpec(memory_space=pl.ANY),
-        ],
+            whole(*returned.shape), pl.BlockSpec((1, 8, width), lambda r: (r, 0, 0)),
+            whole(rows, seq_len), whole(width), whole(*phi.shape), whole(width, width),
+        ]
+        + [pl.BlockSpec(memory_space=pl.ANY)] * 6,
         out_specs=[
-            block(width), block(width), block(3 * width), whole(devices // 2, share, LANES),
+            pl.BlockSpec(memory_space=pl.ANY), pl.BlockSpec(memory_space=pl.ANY), block(3 * width), whole(devices // 2, share, LANES),
             whole(devices // 2, share, LANES),
         ],
         out_shape=[
@@ -782,6 +832,13 @@
             jax.ShapeDtypeStruct((devices // 2, share, LANES), bf16),
         ],
         scratch_shapes=[
+            pltpu.VMEM((seq_len, width), bf16),
+            pltpu.VMEM((seq_len, width), bf16),
+            pltpu.VMEM((seq_len, 3 * width), bf16),
+            pltpu.VMEM((seq_len, LANES), f32),
+            pltpu.VMEM((seq_len, width), bf16),
+            pltpu.VMEM((seq_len, width), bf16),
+            pltpu.VMEM((seq_len, width), f32),
             pltpu.VMEM((seq_len, lanes), bf16),
             pltpu.VMEM((seq_len, width), bf16),
             pltpu.VMEM((pairs, tiles, 2, TILE, LANES), bf16),
@@ -797,15 +854,17 @@
             pltpu.VMEM((8, width), f32),
             pltpu.SMEM((2, tiles * tiles), jnp.int32),
             pltpu.SemaphoreType.DMA((SLOTS,)),
+            pltpu.SemaphoreType.DMA((5,)),
+            pltpu.SemaphoreType.DMA((2,)),
         ],
         cost_estimate=pl.CostEstimate(
             flops=60 * 10**9, bytes_accessed=20 * 10**6, transcendentals=10**7
         ),
-        compiler_params=params(60),
+        compiler_params=params(50),
         name="back",
     )(
-        core, residual, low_two, dispatch, combine, cotangent, returned, mixed, mixed_rest, qkv,
-        recips, low_one, sums, image_ids, gain2, phi, out_weight, probs,
+        core, residual, low_two, dispatch, combine, cotangent, returned, sums, image_ids, gain2, phi,
+        out_weight, mixed, mixed_rest, qkv, recips, low_one, probs,
     )
 
 
@@ -847,7 +906,7 @@
         cost_estimate=pl.CostEstimate(
             flops=6 * 10**9, bytes_accessed=10**7, transcendentals=0
         ),
-        compiler_params=params(60),
+        compiler_params=params(40),
         name="input_back",
     )(tokens, qkv_grad, resid_grad, gain1, qkv_weight)
 
@@ -1015,8 +1074,8 @@
 
     output, resid_grad, qkv_grad, mine, other = back(
         core.reshape(1), residual, low_two, dispatch, combine, cotangent,
-        returned.reshape(dp, ep, per_device, width), mixed, mixed_rest, qkv, recips, low_one, sums,
-        image_ids, ln2_gain, phi, out_weight, probs,
+        returned.reshape(dp, ep, per_device, width), sums, image_ids, ln2_gain, phi, out_weight, mixed,
+        mixed_rest, qkv, recips, low_one, probs,
     )
 
     met = lax.ppermute(other, "core", swap)

time: 175 us -> 171 us (0.977)
  Pallas kernels: 92.9 us -> 87.7 us
  local copies, waits for them, and re-layouts: 4.38 us -> 7.39 us
  starting transfers between devices: 26.7 us -> 24.4 us
    all_to_all x4, starting transfers between devices: 26.5 us -> 22.3 us  [exchange(): return lax.all_to_all(values, over, split_axis=0, concat_axis=0, tiled=True)]
    pallas_call x1, Pallas kernels: 8.41 us -> 5.1 us  [input_back(): pl.pallas_call(input_kernel, grid=(rows,), in_specs=[block(width), block(...]
    unnamed x14 -> x32, local copies, waits for them, and re-layouts: 2.49 us -> 5.5 us
    ppermute x1, starting transfers between devices: 0.21 us -> 2.07 us  [local(): met = lax.ppermute(other, 'core', swap)]
  transfers between devices with their start and end apart: 6 -> 6, of which waited for: 5 -> 5; matrix products, arithmetic and copies ran while one was open for 0% -> 0% of each run, Pallas kernels for 21% -> 20%
where the time goes in v4:
time: 171 us; the launch traced here: 170 us
  Pallas kernels  87.7 us (51%)
  waiting for transfers between devices  27.8 us (16%)
  starting transfers between devices  24.4 us (14%)
  blocking collectives  22 us (13%)
  local copies, waits for them, and re-layouts  7.39 us (4%)
    pallas_call x1, Pallas kernels, back(): pl.pallas_call(back_kernel, grid=(rows,), in_specs=[pl.BlockSpec(memory_s...  43.3 us
    pallas_call x1, Pallas kernels, attend(): pl.pallas_call(attend_kernel, grid=(rows,), in_specs=[block(width), whole...  26.9 us
    all_to_all x4, waiting for transfers between devices, exchange(): return lax.all_to_all(values, over, split_axis=0, concat_axis=0, tiled=True)  24.1 us
    all_to_all x4, starting transfers between devices, exchange(): return lax.all_to_all(values, over, split_axis=0, concat_axis=0, tiled=True)  22.3 us
    all_to_all x1, blocking collectives, exchange(): return lax.all_to_all(values, over, split_axis=0, concat_axis=0, tiled=True)  22 us
    unnamed x32, local copies, waits for them, and re-layouts  5.5 us
    pallas_call x1, Pallas kernels, route(): pl.pallas_call(route_kernel, grid=(rows,), in_specs=[block(width), block(...  5.33 us
    pallas_call x1, Pallas kernels, input_back(): pl.pallas_call(input_kernel, grid=(rows,), in_specs=[block(width), block(...  5.1 us
  transfers between devices with their start and end apart: 6, of which 5 were waited for; matrix products, arithmetic and copies ran while one was open for 0% of the time, Pallas kernels for 20%

profile of v4, /device:TPU:0, one launch (start us, length us, event | category | flops | bytes accessed | tf_op | source)
XLA Modules:
  0.0 170.4 jit_solution(6808691509576979564)
XLA Ops:
  0.7 1.3 broadcast_in_dim.2
  1.9 7.3 %all-to-all-start = ((bf16[8,2,384]{2,1,0:T(2,128)(2,1)}), bf16[8,2,384]{2,1,0:T(2,128)(2,1)S(1)}, u32[]{:S(2)}, u32[]{:S(2)}) async-start(bf16[8,2,384]{2,1,0:T(2,128)(2,1)} %broadcast_in_dim.2), calls=%async_computation | async-start | bytes 24576 | tf_op jit(solution)/shard_map/all_to_all | solution.py:1055
  9.2 26.9 %attend.1 = (bf16[2,1024,384]{2,1,0:T(8,128)(2,1)}, bf16[2,1024,1152]{2,1,0:T(8,128)(2,1)}, bf16[2,1024,384]{2,1,0:T(8,128)(2,1)}, bf16[2,1024,384]{2,1,0:T(8,12...) custom-call(bf16[2,1024,384]{2,1,0:T(8,128)(2,1)} %tokens_ref.3, ...), custom_call_target="tpu_custom_call" | custom-call | flops 20000000000 | bytes 20000000 | tf_op jit(solution)/shard_map/attend/pallas_call | solution.py:346
  36.1 0.0 all-to-all-done
  36.1 0.6 reshape.48.phi_ref
  36.8 5.3 %route.1 = (f32[2,1024,128]{2,1,0:T(8,128)}, f32[2,1024,128]{2,1,0:T(8,128)}, bf16[4,8,8,384]{3,2,1,0:T(8,128)(2,1)}) custom-call(bf16[2,1024,384]{2,1,0:T(8,128)(2,1)} %get-tuple-element.61.low_two_ref, bf16[2,1024,384]{2,1,0:T(8,128)(2,1)} %cot_ref.3, s32[2,1024]{1,0:T(2,128)} %ids_ref.5, s32[2,16]{1,0:T(2,128)} %slot_ref.1, bf16[16,384]{1,0:T(8,128)(2,1)} %reshape.48.phi_ref), custom_call_target="tpu_custom_call" | custom-call | tf_op jit(solution)/shard_map/route/pallas_call | solution.py:455
  42.1 0.0 copy-start.3
  42.1 0.0 copy-start.6
  42.1 0.0 copy-start.9
  42.1 0.0 copy-start.10
  42.2 7.2 %all-to-all-start.1 = ((bf16[32,8,384]{2,1,0:T(8,128)(2,1)}), bf16[32,8,384]{2,1,0:T(8,128)(2,1)S(1)}, u32[]{:S(2)}, u32[]{:S(2)}) async-start(bf16[32,8,384]{2,1,0:T(8,128)(2,1)} %bitcast.7), calls=%async_computation.1 | async-start | bytes 393216 | tf_op jit(solution)/shard_map/all_to_all | solution.py:1055
  49.4 8.5 %all-to-all-done.1.arrived_ref = bf16[32,8,384]{2,1,0:T(8,128)(2,1)S(1)} async-done(((bf16[32,8,384]{2,1,0:T(8,128)(2,1)}), bf16[32,8,384]{2,1,0:T(8,128)(2,1)S(1)}, u32[]{:S(2)}, u32[]{:S(2)}) %all-to-all-start.1) | async-done | bytes 196640 | tf_op jit(solution)/shard_map/all_to_all | solution.py:1055
  57.9 1.9 %experts.1 = (bf16[32,8,384]{2,1,0:T(8,128)(2,1)}, bf16[2,2,64,384]{3,2,1,0:T(8,128)(2,1)S(1)}, bf16[2,64,384]{2,1,0:T(8,128)(2,1)S(1)}, bf16[2,64,384]{2,1,0:T(8,128)(2,1)S(1)}) custom-call(bf16[32,8,384]{2,1,0:T(8,128)(2,1)S(1)} %all-to-all-done.1.arrived_ref, bf16[2,384,384]{2,1,0:T(8,128)(2,1)S(1)} %copy-done, bf16[2,384]{1,0:T(2,128)(2,1)S(1)} %copy-done.4, ...), custom_call_target="tpu_custom_call" | custom-call | tf_op jit(solution)/shard_map/experts/pallas_call | solution.py:542
  59.8 3.0 %all-to-all-start.2 = ((bf16[32,8,384]{2,1,0:T(8,128)(2,1)}), bf16[32,8,384]{2,1,0:T(8,128)(2,1)S(1)}, u32[]{:S(2)}, u32[]{:S(2)}) async-start(bf16[32,8,384]{2,1,0:T(8,128)(2,1)} %get-tuple-element.65), calls=%async_computation.2 | async-start | bytes 393216 | tf_op jit(solution)/shard_map/all_to_all | solution.py:1055
  62.9 1.8 %expert_grads.1 = (f32[2,384,384]{2,1,0:T(8,128)}, f32[2,384]{1,0:T(2,128)}, f32[2,384,384]{2,1,0:T(8,128)}, f32[2,384]{1,0:T(2,128)}) custom-call(bf16[2,2,64,384]{3,2,1,0:T(8,128)(2,1)S(1)} %get-tuple-element.66.rows_ref, bf16[2,64,384]{2,1,0:T(8,128)(2,1)S(1)} %get-tuple-element.67.hidden_ref, bf16[2,64,384]{2,1,0:T(8,128)(2,1)S(1)} %get-tuple-element.68.pre_grad_ref), custom_call_target="tpu_custom_call" | custom-call | flops 75497472 | bytes 4000000 | tf_op jit(solution)/shard_map/expert_grads/pallas_call | solution.py:558
  64.7 6.7 %all-to-all-done.2 = bf16[32,8,384]{2,1,0:T(8,128)(2,1)S(1)} async-done(((bf16[32,8,384]{2,1,0:T(8,128)(2,1)}), bf16[32,8,384]{2,1,0:T(8,128)(2,1)S(1)}, u32[]{:S(2)}, u32[]{:S(2)}) %all-to-all-start.2) | async-done | bytes 196640 | tf_op jit(solution)/shard_map/all_to_all | solution.py:1055
  71.5 1.2 copy-done.7
  72.7 43.3 %back.1 = (bf16[2,1024,384]{2,1,0:T(8,128)(2,1)}, f32[2,1024,384]{2,1,0:T(8,128)}, bf16[2,1024,1152]{2,1,0:T(8,128)(2,1)}, bf16[16,160,128]{2,1,0:T(8,128)(2,1)S(1)}, bf16[16,160,128]{2,1,0:T(8,128)(2,1)S(1)}) custom-call(s32[1]{0:T(128)} %bitcast.core_ref, f32[2,1024,384]{2,1,0:T(8,128)} %get-tuple-element.60.residual_ref, ...), custom_call_target="tpu_custom_call" | custom-call | flops 60000002048 | bytes 20000000 | tf_op jit(solution)/shard_map/back/pallas_call | solution.py:813
  116.0 2.1 %collective-permute-start = (bf16[16,160,128]{2,1,0:T(8,128)(2,1)S(1)}, bf16[16,160,128]{2,1,0:T(8,128)(2,1)S(1)}, u32[]{:S(2)}, u32[]{:S(2)}) collective-permute-start(bf16[16,160,128]{2,1,0:T(8,128)(2,1)S(1)} %get-tuple-element.86), channel_id=1, source_target_pairs={{0,8},{8,0},{1,9},{9,1},{2,10},{10,2},{3,11},{11,3},{4,12},{12,4},... | collective-permute-start | bytes 1966088 | tf_op jit(solution)/shard_map/ppermute | solution.py:1081
  118.1 1.7 %collective-permute-done.two_ref = bf16[16,160,128]{2,1,0:T(8,128)(2,1)S(1)} collective-permute-done((bf16[16,160,128]{2,1,0:T(8,128)(2,1)S(1)}, bf16[16,160,128]{2,1,0:T(8,128)(2,1)S(1)}, u32[]{:S(2)}, u32[]{:S(2)}) %collective-permute-start) | collective-permute-done | bytes 655392 | tf_op jit(solution)/shard_map/ppermute | solution.py:1081
  119.8 1.0 add.3
  120.8 4.8 %all-to-all-start.3 = ((bf16[16,160,128]{2,1,0:T(8,128)(2,1)}), bf16[16,160,128]{2,1,0:T(8,128)(2,1)S(1)}, u32[]{:S(2)}, u32[]{:S(2)}) async-start(bf16[16,160,128]{2,1,0:T(8,128)(2,1)} %add.3), calls=%async_computation.3 | async-start | bytes 1310720 | tf_op jit(solution)/shard_map/all_to_all | solution.py:1055
  125.6 2.3 %copy-done.12 = bf16[2,1024,1152]{2,1,0:T(8,128)(2,1)S(1)} copy-done((bf16[2,1024,1152]{2,1,0:T(8,128)(2,1)S(1)}, bf16[2,1024,1152]{2,1,0:T(8,128)(2,1)}, u32[]{:S(2)}) %copy-start.12) | copy-done | bytes 4718616
  128.0 1.9 %copy-done.13 = f32[2,1024,384]{2,1,0:T(8,128)S(1)} copy-done((f32[2,1024,384]{2,1,0:T(8,128)S(1)}, f32[2,1024,384]{2,1,0:T(8,128)}, u32[]{:S(2)}) %copy-start.13) | copy-done | bytes 3145752
  129.9 5.1 %input_back.1 = (bf16[2,1024,384]{2,1,0:T(8,128)(2,1)}, f32[8,384]{1,0:T(8,128)S(1)}) custom-call(bf16[2,1024,384]{2,1,0:T(8,128)(2,1)S(1)} %copy-done.5, bf16[2,1024,1152]{2,1,0:T(8,128)(2,1)S(1)} %copy-done.12, f32[2,1024,384]{2,1,0:T(8,128)S(1)} %copy-done.13, f32[384]{0:T(512)S(1)} %copy-done.11, bf16[384,1152]{1,0:T(8,128)(2,1)S(1)} %copy-done.8), custom_call_target="tpu_custom_call" | custom-call | flops 6000000000 | bytes 10000000 | tf_op jit(solution)/shard_map/input_back/pallas_call | solution.py:895
  135.0 8.8 %all-to-all-done.3.collected_ref = bf16[16,160,128]{2,1,0:T(8,128)(2,1)S(1)} async-done(((bf16[16,160,128]{2,1,0:T(8,128)(2,1)}), bf16[16,160,128]{2,1,0:T(8,128)(2,1)S(1)}, u32[]{:S(2)}, u32[]{:S(2)}) %all-to-all-start.3) | async-done | bytes 655392 | tf_op jit(solution)/shard_map/all_to_all | solution.py:1055
  143.8 0.1 fold.1
  143.9 22.0 %all_to_all.25.refs_1_ = bf16[16,160,128]{2,1,0:T(8,128)(2,1)S(1)} all-to-all(bf16[16,160,128]{2,1,0:T(8,128)(2,1)S(1)} %fold.1), channel_id=1, replica_groups=mesh['y'=2,'core'=2,'expert'=8] {'y','expert'}, dimensions={0} | all-to-all | bytes 1310720 | tf_op jit(solution)/shard_map/all_to_all | solution.py:1055
  165.9 0.0 collective-permute-start.1
  165.9 0.1 pad_add_fusion.refs_0_
  166.0 2.0 %collective-permute-done.1.refs_2_ = bf16[16,160,128]{2,1,0:T(8,128)(2,1)S(1)} collective-permute-done((bf16[16,160,128]{2,1,0:T(8,128)(2,1)S(1)}, bf16[16,160,128]{2,1,0:T(8,128)(2,1)S(1)}, u32[]{:S(2)}, u32[]{:S(2)}) %collective-permute-start.1) | collective-permute-done | bytes 655392 | tf_op jit(solution)/shard_map/ppermute | solution.py:1085
  168.0 2.2 %finish.1 = (f32[384,1152]{1,0:T(8,128)}, f32[384,384]{1,0:T(8,128)}, f32[384]{0:T(512)}, f32[384]{0:T(512)}, f32[384]{0:T(512)}, /*index=5*/f32[384]{0:T(512)},...) custom-call(s32[2]{0:T(128)S(1)} %pad_add_fusion.refs_0_, ...), custom_call_target="tpu_custom_call" | custom-call | tf_op jit(solution)/shard_map/finish/pallas_call | solution.py:1024
  (26 shorter events, 0.1 us)
Async XLA Ops:
  1.9 34.2 %all-to-all-start = ((bf16[8,2,384]{2,1,0:T(2,128)(2,1)}), bf16[8,2,384]{2,1,0:T(2,128)(2,1)S(1)}, u32[]{:S(2)}, u32[]{:S(2)}) async-start(bf16[8,2,384]{2,1,0:T(2,128)(2,1)} %broadcast_in_dim.2), calls=%async_computation | async-start | bytes 24576 | tf_op jit(solution)/shard_map/all_to_all | solution.py:1055
  36.7 12.6 %copy-start.15 = (f32[2,384]{1,0:T(2,128)S(1)}, f32[2,384]{1,0:T(2,128)}, u32[]{:S(2)}) copy-start(f32[2,384]{1,0:T(2,128)} %param.34) | copy-start | bytes 9220
  36.7 21.2 %copy-start = (bf16[2,384,384]{2,1,0:T(8,128)(2,1)S(1)}, bf16[2,384,384]{2,1,0:T(8,128)(2,1)}, u32[]{:S(2)}) copy-start(bf16[2,384,384]{2,1,0:T(8,128)(2,1)} %up_ref.1) | copy-start | bytes 1769476
  36.7 21.2 %copy-start.1 = (bf16[2,384,384]{2,1,0:T(8,128)(2,1)S(1)}, bf16[2,384,384]{2,1,0:T(8,128)(2,1)}, u32[]{:S(2)}) copy-start(bf16[2,384,384]{2,1,0:T(8,128)(2,1)} %down_ref.1) | copy-start | bytes 1769476
  36.7 21.2 %copy-start.4 = (bf16[2,384]{1,0:T(2,128)(2,1)S(1)}, bf16[2,384]{1,0:T(2,128)(2,1)}, u32[]{:S(2)}) copy-start(bf16[2,384]{1,0:T(2,128)(2,1)} %up_bias_ref.1) | copy-start | bytes 4612
  42.1 29.3 %copy-start.2 = (bf16[16,384]{1,0:T(8,128)(2,1)S(1)}, bf16[16,384]{1,0:T(8,128)(2,1)}, u32[]{:S(2)}) copy-start(bf16[16,384]{1,0:T(8,128)(2,1)} %reshape.48.phi_ref) | copy-start | bytes 36868
  42.1 29.3 %copy-start.3 = (s32[2,1024]{1,0:T(2,128)S(1)}, s32[2,1024]{1,0:T(2,128)}, u32[]{:S(2)}) copy-start(s32[2,1024]{1,0:T(2,128)} %ids_ref.5) | copy-start | bytes 24580
  42.1 29.3 %copy-start.6 = (f32[2,1024,128]{2,1,0:T(8,128)S(1)}, f32[2,1024,128]{2,1,0:T(8,128)}, u32[]{:S(2)}) copy-start(f32[2,1024,128]{2,1,0:T(8,128)} %get-tuple-element.62.dispatch_ref) | copy-start | bytes 3145732
  42.1 29.3 %copy-start.9 = (bf16[384,384]{1,0:T(8,128)(2,1)S(1)}, bf16[384,384]{1,0:T(8,128)(2,1)}, u32[]{:S(2)}) copy-start(bf16[384,384]{1,0:T(8,128)(2,1)} %out_w_ref.3) | copy-start | bytes 884740
  42.1 29.3 %copy-start.10 = (f32[384]{0:T(512)S(1)}, f32[384]{0:T(512)}, u32[]{:S(2)}) copy-start(f32[384]{0:T(512)} %gain2_ref.3) | copy-start | bytes 4612
  42.1 29.3 %copy-start.14 = (f32[2,8,384]{2,1,0:T(8,128)S(1)}, f32[2,8,384]{2,1,0:T(8,128)}, u32[]{:S(2)}) copy-start(f32[2,8,384]{2,1,0:T(8,128)} %get-tuple-element.74.sums_ref) | copy-start | bytes 73732
  42.2 15.8 %all-to-all-start.1 = ((bf16[32,8,384]{2,1,0:T(8,128)(2,1)}), bf16[32,8,384]{2,1,0:T(8,128)(2,1)S(1)}, u32[]{:S(2)}, u32[]{:S(2)}) async-start(bf16[32,8,384]{2,1,0:T(8,128)(2,1)} %bitcast.7), calls=%async_computation.1 | async-start | bytes 393216 | tf_op jit(solution)/shard_map/all_to_all | solution.py:1055
  59.8 11.6 %all-to-all-start.2 = ((bf16[32,8,384]{2,1,0:T(8,128)(2,1)}), bf16[32,8,384]{2,1,0:T(8,128)(2,1)S(1)}, u32[]{:S(2)}, u32[]{:S(2)}) async-start(bf16[32,8,384]{2,1,0:T(8,128)(2,1)} %get-tuple-element.65), calls=%async_computation.2 | async-start | bytes 393216 | tf_op jit(solution)/shard_map/all_to_all | solution.py:1055
  71.5 1.2 copy-start.7
  116.0 3.8 %collective-permute-start = (bf16[16,160,128]{2,1,0:T(8,128)(2,1)S(1)}, bf16[16,160,128]{2,1,0:T(8,128)(2,1)S(1)}, u32[]{:S(2)}, u32[]{:S(2)}) collective-permute-start(bf16[16,160,128]{2,1,0:T(8,128)(2,1)S(1)} %get-tuple-element.86), channel_id=1, source_target_pairs={{0,8},{8,0},{1,9},{9,1},{2,10},{10,2},{3,11},{11,3},{4,12},{12,4},... | collective-permute-start | bytes 1966088 | tf_op jit(solution)/shard_map/ppermute | solution.py:1081
  119.8 5.8 %copy-start.5 = (bf16[2,1024,384]{2,1,0:T(8,128)(2,1)S(1)}, bf16[2,1024,384]{2,1,0:T(8,128)(2,1)}, u32[]{:S(2)}) copy-start(bf16[2,1024,384]{2,1,0:T(8,128)(2,1)} %tokens_ref.3) | copy-start | bytes 4718596
  119.8 5.8 %copy-start.8 = (bf16[384,1152]{1,0:T(8,128)(2,1)S(1)}, bf16[384,1152]{1,0:T(8,128)(2,1)}, u32[]{:S(2)}) copy-start(bf16[384,1152]{1,0:T(8,128)(2,1)} %qkv_w_ref.3) | copy-start | bytes 2654212
  119.8 5.8 %copy-start.11 = (f32[384]{0:T(512)S(1)}, f32[384]{0:T(512)}, u32[]{:S(2)}) copy-start(f32[384]{0:T(512)} %gain1_ref.3) | copy-start | bytes 4612
  120.8 23.0 %all-to-all-start.3 = ((bf16[16,160,128]{2,1,0:T(8,128)(2,1)}), bf16[16,160,128]{2,1,0:T(8,128)(2,1)S(1)}, u32[]{:S(2)}, u32[]{:S(2)}) async-start(bf16[16,160,128]{2,1,0:T(8,128)(2,1)} %add.3), calls=%async_computation.3 | async-start | bytes 1310720 | tf_op jit(solution)/shard_map/all_to_all | solution.py:1055
  125.6 2.3 %copy-start.12 = (bf16[2,1024,1152]{2,1,0:T(8,128)(2,1)S(1)}, bf16[2,1024,1152]{2,1,0:T(8,128)(2,1)}, u32[]{:S(2)}) copy-start(bf16[2,1024,1152]{2,1,0:T(8,128)(2,1)} %get-tuple-element.82.qkv_grad_ref) | copy-start | bytes 14155780
  128.0 1.9 %copy-start.13 = (f32[2,1024,384]{2,1,0:T(8,128)S(1)}, f32[2,1024,384]{2,1,0:T(8,128)}, u32[]{:S(2)}) copy-start(f32[2,1024,384]{2,1,0:T(8,128)} %get-tuple-element.83.resid_grad_ref) | copy-start | bytes 9437188
  165.9 2.1 %collective-permute-start.1 = (bf16[16,160,128]{2,1,0:T(8,128)(2,1)S(1)}, bf16[16,160,128]{2,1,0:T(8,128)(2,1)S(1)}, u32[]{:S(2)}, u32[]{:S(2)}) collective-permute-start(bf16[16,160,128]{2,1,0:T(8,128)(2,1)S(1)} %all_to_all.25.refs_1_), channel_id=1, source_target_pairs={{0,8},{8,0},{1,9},{9,1},{2,10},{10,2},{3,11},{11,3},{4,12},{12,4},... | collective-permute-start | bytes 1966088 | tf_op jit(solution)/shard_map/ppermute | solution.py:1085

commit v5 on v4

--- a/solution.py
+++ b/solution.py
@@ -12,7 +12,7 @@
 MASKED = -1e30
 LANES = 128
 TILE = 256
-SAFE = 60.0
+SAFE = 30.0
 GROUP = 2
 SLOTS = 2 * GROUP
 PIECE = 16
@@ -90,11 +90,15 @@
     lax.fori_loop(whole_groups * GROUP, total, alone, 0)
 
 
-def head_picker(width):
+def head_picker(width, copies=1):
     head, _ = split(lax.broadcasted_iota(jnp.int32, (width, LANES), 0), width // HEADS)
-    return jnp.where(head == lax.broadcasted_iota(jnp.int32, (width, LANES), 1), 1.0, 0.0).astype(
-        bf16
-    )
+    lane = lax.broadcasted_iota(jnp.int32, (width, LANES), 1)
+    return jnp.concatenate([jnp.where(head == lane, 1.0, 0.0).astype(bf16)] * copies, axis=0)
+
+
+def low_terms(values):
+    top = values.astype(bf16)
+    return jnp.concatenate([top, (values - top.astype(f32)).astype(bf16)], axis=1)
 
 
 def split(values, size):
@@ -126,34 +130,30 @@
 
 
 def query_marks(columns, lanes):
-    return jnp.where(columns == (lanes - 24).astype(f32), 1.0, 0.0)
+    return jnp.where(columns == lanes.astype(f32), 1.0, 0.0)
 
 
 def key_marks(columns, lanes):
-    other = jnp.where(columns == (lanes - 24).astype(f32), 0.0, MASKED)
-    inside = jnp.logical_and(lanes >= 24, lanes < 24 + IMAGES)
-    return jnp.where(inside, other, jnp.where(lanes < 24, 1.0, 0.0))
-
-
-def three_parts(values, lanes):
+    differs = jnp.logical_and(columns != lanes.astype(f32), lanes < IMAGES)
+    return jnp.where(differs, MASKED, 0.0)
+
+
+def two_parts(values, lanes):
     values = jnp.where(lanes < 8, values, 0.0)
     top = values.astype(bf16).astype(f32)
-    rest = values - top
-    mid = rest.astype(bf16).astype(f32)
-    low = (rest - mid).astype(bf16).astype(f32)
-    return top + pltpu.roll(mid, 8, 1) + pltpu.roll(low, 16, 1)
+    rest = (values - top).astype(bf16).astype(f32)
+    return top + pltpu.roll(rest, 8, 1)
 
 
 def own_lanes(values, lanes, head):
-    keep = jnp.logical_or(lanes >= 24, jnp.bitwise_and(lanes, 7) == head)
-    return jnp.where(keep, values, 0.0)
+    return jnp.where(jnp.bitwise_and(lanes, 7) == head, values, 0.0)
 
 
 def attend_kernel(
     tokens_ref, ids_ref, gain1_ref, shift1_ref, q_bias_ref, v_bias_ref, qkv_w_ref, out_w_ref,
     out_bias_ref, gain2_ref, shift2_ref,
-    low_one_ref, qkv_ref, mixed_ref, mixed_rest_ref, recip_ref, residual_ref, low_two_ref, sums_ref,
-    probs_ref, low_one_scr, qkv_scr, q_scr, k_scr, v_scr, s_scr, top_scr, acc_scr, p_scr, list_scr,
+    low_one_ref, qkv_ref, mixed_hbm, mixed_rest_hbm, recip_hbm, residual_ref, low_two_ref, sums_ref,
+    probs_ref, low_one_scr, qkv_scr, mixed_ref, mixed_rest_ref, recip_ref, q_scr, k_scr, v_scr, s_scr, top_scr, acc_scr, p_scr, list_scr,
     sem, out_sem,
 ):
     row = pl.program_id(0)
@@ -176,10 +176,21 @@
     def store_qkv(r):
         return pltpu.make_async_copy(qkv_scr, qkv_ref.at[r], out_sem.at[1])
 
+    mixed_parts = ((mixed_ref, mixed_hbm), (mixed_rest_ref, mixed_rest_hbm), (recip_ref, recip_hbm))
+
+    def store_mixed(r, k):
+        source, target = mixed_parts[k]
+        return pltpu.make_async_copy(source, target.at[r], out_sem.at[2 + k])
+
+    def wait_stores(r):
+        store_one(r).wait()
+        store_qkv(r).wait()
+        for k in range(3):
+            store_mixed(r, k).wait()
+
     @pl.when(row > 0)
     def _():
-        store_one(row - 1).wait()
-        store_qkv(row - 1).wait()
+        wait_stores(row - 1)
 
     stream = tokens_ref[0].astype(f32)
     hat, _ = norm_parts(stream)
@@ -297,10 +308,12 @@
         recips = jnp.where(lanes == 2 * p, own, recips)
         recips = jnp.where(lanes == 2 * p + 1, recip, recips)
         low = mixed.astype(bf16)
-        mixed_ref[0, :, p * LANES : (p + 1) * LANES] = low
-        mixed_rest_ref[0, :, p * LANES : (p + 1) * LANES] = (mixed - low.astype(f32)).astype(bf16)
-    recip_ref[0] = recips
-    branch = dot(mixed_ref[0], out_w_ref[...]) + as_row(out_bias_ref)
+        mixed_ref[:, p * LANES : (p + 1) * LANES] = low
+        mixed_rest_ref[:, p * LANES : (p + 1) * LANES] = (mixed - low.astype(f32)).astype(bf16)
+    recip_ref[...] = recips
+    for k in range(3):
+        store_mixed(row, k).start()
+    branch = dot(mixed_ref[...], out_w_ref[...]) + as_row(out_bias_ref)
     residual = tokens_ref[0].astype(f32) + branch
     residual_ref[0] = residual
     hat_two, _ = norm_parts(residual)
@@ -310,8 +323,7 @@
 
     @pl.when(row == pl.num_programs(0) - 1)
     def _():
-        store_one(row).wait()
-        store_qkv(row).wait()
+        wait_stores(row)
 
     stream = tokens_ref[0].astype(f32)
     sums_ref[0] = jnp.concatenate(
@@ -352,8 +364,7 @@
             whole(width), whole(width),
         ],
         out_specs=[
-            pl.BlockSpec(memory_space=pl.ANY), pl.BlockSpec(memory_space=pl.ANY),
-            block(width), block(width), block(LANES),
+            *[pl.BlockSpec(memory_space=pl.ANY)] * 5,
             block(width), block(width), pl.BlockSpec((1, 8, width), lambda r: (r, 0, 0)),
             pl.BlockSpec(memory_space=pl.ANY),
         ],
@@ -366,6 +377,9 @@
         scratch_shapes=[
             pltpu.VMEM((seq_len, width), bf16),
             pltpu.VMEM((seq_len, 3 * width), bf16),
+            pltpu.VMEM((seq_len, width), bf16),
+            pltpu.VMEM((seq_len, width), bf16),
+            pltpu.VMEM((seq_len, LANES), f32),
             pltpu.VMEM((pairs, tiles, 2, TILE, 2 * LANES), bf16),
             pltpu.VMEM((pairs, seq_len, 2 * LANES), bf16),
             pltpu.VMEM((HEADS, seq_len, LANES), bf16),
@@ -375,7 +389,7 @@
             pltpu.VMEM((SLOTS, pairs, 2 * TILE, TILE), bf16),
             pltpu.SMEM((2, tiles * tiles), jnp.int32),
             pltpu.SemaphoreType.DMA((SLOTS,)),
-            pltpu.SemaphoreType.DMA((2,)),
+            pltpu.SemaphoreType.DMA((5,)),
         ],
         cost_estimate=pl.CostEstimate(
             flops=20 * 10**9, bytes_accessed=20 * 10**6, transcendentals=10**7
@@ -388,47 +402,50 @@
     )
 
 
-def padded_phi(phi_ref, lanes):
+def half_lanes(slots):
+    return LANES // 2 if slots <= LANES // 2 else -(-slots // LANES) * LANES
+
+
+def padded_phi(phi_ref, half):
     slots, width = phi_ref.shape
     phi = phi_ref[...]
-    if lanes > slots:
-        phi = jnp.concatenate([phi, jnp.zeros((lanes - slots, width), bf16)], axis=0)
+    if half > slots:
+        phi = jnp.concatenate([phi, jnp.zeros((half - slots, width), bf16)], axis=0)
     return phi
 
 
 def route_kernel(
-    low_two_ref, cot_ref, ids_ref, slot_ref, phi_ref, dispatch_ref, combine_ref, sent_ref, slots_scr
+    low_two_ref, cot_ref, ids_ref, slot_ref, phi_ref, weights_ref, sent_ref, slots_scr
 ):
     row = pl.program_id(0)
     rows, slots = slot_ref.shape
-    lanes = dispatch_ref.shape[2]
+    lanes = weights_ref.shape[2]
+    half = lanes // 2
     dp, ep, per_device, width = sent_ref.shape
     own = slots // ep
     columns = image_columns(ids_ref[pl.ds(row, 1), :])
     if lanes > LANES:
         columns = jnp.concatenate([columns] * (lanes // LANES), axis=1)
-    slot_row = dot(
-        slot_ref[pl.ds(row, 1), :].astype(bf16), selector(slots, lanes, lambda r: r)
-    )
-    slot_row = jnp.where(
-        lax.broadcasted_iota(jnp.int32, (1, lanes), 1) < slots, slot_row, -1.0
-    )
+    both_halves = selector(slots, lanes, lambda r: r) + selector(slots, lanes, lambda r: r + half)
+    slot_row = dot(slot_ref[pl.ds(row, 1), :].astype(bf16), both_halves)
+    lane = lax.broadcasted_iota(jnp.int32, (1, lanes), 1)
+    left = lax.broadcasted_iota(jnp.int32, (columns.shape[0], lanes), 1) < half
+    slot_row = jnp.where(split(lane, half)[1] < slots, slot_row, -1.0)
     allowed = columns == slot_row
     low_two = low_two_ref[0]
-    logits = jnp.where(allowed, dot(low_two, padded_phi(phi_ref, lanes), NT), MASKED)
-
-    def select(axis):
-        top = jnp.max(logits, axis=axis, keepdims=True)
-        weights = jnp.where(allowed, jnp.exp(logits - top), 0.0)
-        total = jnp.sum(weights, axis=axis, keepdims=True)
-        return weights / jnp.where(total == 0.0, 1.0, total)
-
-    dispatch = select(0)
-    combine = select(1)
-    dispatch_ref[0] = dispatch
-    combine_ref[0] = combine
-    slots_scr[row, 0] = dot(dispatch.astype(bf16), low_two, TN)[:slots].astype(bf16)
-    slots_scr[row, 1] = dot(combine.astype(bf16), cot_ref[0], TN)[:slots].astype(bf16)
+    phi = padded_phi(phi_ref, half)
+    logits = dot(low_two, jnp.concatenate([phi, phi], axis=0), NT)
+    logits = jnp.where(allowed, logits, MASKED)
+    slot_top = jnp.max(jnp.where(left, MASKED, logits), axis=1, keepdims=True)
+    top = jnp.where(left, jnp.max(logits, axis=0, keepdims=True), slot_top)
+    weights = jnp.where(allowed, jnp.exp(logits - top), 0.0)
+    slot_total = jnp.sum(jnp.where(left, 0.0, weights), axis=1, keepdims=True)
+    total = jnp.where(left, jnp.sum(weights, axis=0, keepdims=True), slot_total)
+    weights = weights / jnp.where(total == 0.0, 1.0, total)
+    weights_ref[0] = weights
+    low = weights.astype(bf16)
+    slots_scr[row, 0] = dot(low, low_two, TN)[:slots].astype(bf16)
+    slots_scr[row, 1] = dot(low, cot_ref[0], TN)[half : half + slots].astype(bf16)
 
     @pl.when(row == rows - 1)
     def _():
@@ -449,7 +466,7 @@
 def route(low_two, cotangent, image_ids, slot_image, phi, dp, ep):
     rows, seq_len, width = low_two.shape
     slots = slot_image.shape[1]
-    lanes = -(-slots // LANES) * LANES
+    lanes = 2 * half_lanes(slots)
     per_device = rows * 2 * slots // ep
     block = lambda n: per_row(seq_len, n)
     return pl.pallas_call(
@@ -459,9 +476,8 @@
             block(width), block(width), whole(rows, seq_len), whole(rows, slots),
             whole(slots, width),
         ],
-        out_specs=[block(lanes), block(lanes), whole(dp, ep, per_device, width)],
+        out_specs=[block(lanes), whole(dp, ep, per_device, width)],
         out_shape=[
-            jax.ShapeDtypeStruct((rows, seq_len, lanes), f32),
             jax.ShapeDtypeStruct((rows, seq_len, lanes), f32),
             jax.ShapeDtypeStruct((dp, ep, per_device, width), bf16),
         ],
@@ -569,12 +585,13 @@
 
 
 def back_kernel(
-    core_ref, residual_ref, low_two_ref, dispatch_ref, combine_ref, cot_ref, back_ref, sums_ref,
+    core_ref, residual_ref, low_two_ref, weights_ref, cot_ref, back_ref, sums_ref,
     ids_ref, gain2_ref, phi_ref, out_w_ref, mixed_hbm, mixed_rest_hbm, qkv_hbm, recip_hbm,
     low_one_hbm, probs_ref,
-    output_hbm, resid_grad_hbm, qkv_grad_ref, mine_ref, other_ref,
+    output_hbm, resid_grad_hbm, qkv_grad_hbm, mine_ref, other_ref,
     mixed_ref, mixed_rest_ref, qkv_ref, recip_ref, low_one_ref, output_ref, resid_grad_ref,
-    logit_scr, branch_scr, q_scr, o_scr, v_scr, dq_scr, dk_scr, dv_scr, grad_scr, p_scr, ds_scr,
+    qkv_grad_ref,
+    branch_scr, q_scr, o_scr, v_scr, dq_scr, dk_scr, dv_scr, grad_scr, p_scr, ds_scr,
     phi_grad_scr, rows_scr, list_scr, sem, in_sem, out_sem,
 ):
     row = pl.program_id(0)
@@ -583,7 +600,8 @@
     scale = (width // HEADS) ** -0.5
     lanes_all = lane_ids(seq_len)
     slots = phi_ref.shape[0]
-    slot_lanes = dispatch_ref.shape[2]
+    slot_lanes = weights_ref.shape[2]
+    half = slot_lanes // 2
 
     @pl.when(row == 0)
     def _():
@@ -612,6 +630,7 @@
     low_one_in = brought(4, low_one_hbm, low_one_ref)
     output_out = taken(0, output_ref, output_hbm)
     resid_out = taken(1, resid_grad_ref, resid_grad_hbm)
+    qkv_grad_out = taken(2, qkv_grad_ref, qkv_grad_hbm)
     for copy in (mixed_in, rest_in, recip_in, qkv_in):
         copy.start()
     for n in range(SLOTS):
@@ -625,33 +644,34 @@
         held += back_ref[d].astype(f32)
     held = held.reshape(ep * per_device, width).astype(bf16)
 
-    def of_kind(kind):
-        def wanted(slot):
+    def of_kind(kind, first):
+        def wanted(lane):
+            slot = lane - first
             device, mine = split(slot, own)
             place = device * per_device + (row * 2 + kind) * own + mine
-            return jnp.where(slot < slots, place, -1)
+            return jnp.where(jnp.logical_and(slot >= 0, slot < slots), place, -1)
 
         return dot(selector(slot_lanes, ep * per_device, wanted), held).astype(bf16)
 
-    expert_out = of_kind(0)
-    slot_grad = of_kind(1)
-    phi = padded_phi(phi_ref, slot_lanes)
-    combine, dispatch = combine_ref[0], dispatch_ref[0]
+    expert_out = of_kind(0, half)
+    slot_grad = of_kind(1, 0)
+    weights = weights_ref[0]
+    left_slots = lax.broadcasted_iota(jnp.int32, weights.shape, 1) < half
     cot = cot_ref[0]
     low_two = low_two_ref[0]
-    moe_out = dot(combine.astype(bf16), expert_out)
+    moe_out = dot(weights.astype(bf16), expert_out)
     output_ref[...] = (residual_ref[0] + moe_out).astype(bf16)
     output_out.start()
     moe_sq = jnp.sum(moe_out * moe_out, axis=0, keepdims=True)
-    combine_grad = dot(cot, expert_out, NT)
-    dispatch_grad = dot(low_two, slot_grad, NT)
-    logit_grad = combine * (
-        combine_grad - jnp.sum(combine * combine_grad, axis=1, keepdims=True)
-    ) + dispatch * (dispatch_grad - jnp.sum(dispatch * dispatch_grad, axis=0, keepdims=True))
-    logit_scr[...] = logit_grad.astype(bf16)
-    phi_grad_scr[...] += dot(logit_scr[...], low_two, TN)
-
-    grad = dot(dispatch.astype(bf16), slot_grad) + dot(logit_scr[...], phi)
+    weight_grad = dot(cot, expert_out, NT) + dot(low_two, slot_grad, NT)
+    weighted = weights * weight_grad
+    slot_sum = jnp.sum(jnp.where(left_slots, 0.0, weighted), axis=1, keepdims=True)
+    patch_sum = jnp.sum(weighted, axis=0, keepdims=True)
+    logit_grad = weights * (weight_grad - jnp.where(left_slots, patch_sum, slot_sum))
+    logit_grad += pltpu.roll(logit_grad, half, 1)
+    blend = jnp.where(left_slots, weights, logit_grad).astype(bf16)
+    phi_grad_scr[...] += dot(blend, low_two, TN)
+    grad = dot(blend, jnp.concatenate([slot_grad[:half], padded_phi(phi_ref, half)], axis=0))
     hat, recip = norm_parts(residual_ref[0])
     resid = cot.astype(f32) + norm_back(grad, hat, recip, as_row(gain2_ref))
     gain_sum = jnp.sum(grad * hat, axis=0, keepdims=True)
@@ -665,22 +685,17 @@
     mixed_grad = dot(branch_scr[...], out_w_ref[...], NT).astype(bf16).astype(f32)
     picker = head_picker(width)
     recip_in.wait()
-    recips = recip_ref[...]
-    recips_top = recips.astype(bf16)
-    recips_low = (recips - recips_top.astype(f32)).astype(bf16)
-    mixed_grad *= dot(recips_top, picker, NT) + dot(recips_low, picker, NT)
+    twice = jnp.concatenate([picker, picker], axis=1)
+    mixed_grad *= dot(low_terms(recip_ref[...]), twice, NT)
     mixed_grad = mixed_grad.astype(bf16).astype(f32)
     rest_in.wait()
     product = (mixed_ref[...].astype(f32) + mixed_rest_ref[...].astype(f32)) * mixed_grad
-    product_top = product.astype(bf16)
-    row_dots = dot(product_top, picker) + dot(
-        (product - product_top.astype(f32)).astype(bf16), picker
-    )
+    row_dots = dot(low_terms(product), head_picker(width, 2))
 
     qkv_in.wait()
     left = lanes_all < LANES // 2
-    marks_o = -three_parts(row_dots, lanes_all)
-    ones = jnp.where(lanes_all < 24, 1.0, 0.0).astype(bf16)
+    marks_o = -two_parts(row_dots, lanes_all)
+    ones = jnp.where(lanes_all < 16, 1.0, 0.0).astype(bf16)
     for p in range(pairs):
         cut = slice(p * LANES, (p + 1) * LANES)
         scaled = qkv_ref[:, cut].astype(f32) * scale
@@ -734,28 +749,30 @@
     for p in range(pairs):
         for block, (source, factor) in enumerate(((dq_scr, scale), (dk_scr, 1.0), (dv_scr, 1.0))):
             start = block * width + p * LANES
-            qkv_grad_ref[0, :, start : start + LANES] = (source[p] * factor).astype(bf16)
+            qkv_grad_ref[:, start : start + LANES] = (source[p] * factor).astype(bf16)
+    qkv_grad_out.start()
     low_one_in.wait()
-    grad_scr[:, : 3 * width] += dot(low_one_ref[...], qkv_grad_ref[0], TN)
-    query_sum = jnp.sum(qkv_grad_ref[0, :, :width].astype(f32), axis=0, keepdims=True)
-    value_sum = jnp.sum(qkv_grad_ref[0, :, 2 * width :].astype(f32), axis=0, keepdims=True)
+    grad_scr[:, : 3 * width] += dot(low_one_ref[...], qkv_grad_ref[...], TN)
+    query_sum = jnp.sum(qkv_grad_ref[:, :width].astype(f32), axis=0, keepdims=True)
+    value_sum = jnp.sum(qkv_grad_ref[:, 2 * width :].astype(f32), axis=0, keepdims=True)
     rows_scr[...] += jnp.concatenate(
         [query_sum, value_sum, bias_sum, gain_sum, shift_sum, moe_sq, sums_ref[0, 0:2, :]], axis=0
     )
 
     output_out.wait()
     resid_out.wait()
+    qkv_grad_out.wait()
 
     @pl.when(row == pl.num_programs(0) - 1)
     def _():
+        small = jnp.concatenate(
+            [phi_grad_scr[slot_lanes // 2 : slot_lanes // 2 + slots, b * LANES : (b + 1) * LANES] for b in range(pairs)]
+            + [rows_scr[:, b * LANES : (b + 1) * LANES] for b in range(pairs)],
+            axis=0,
+        )
         half, share, _ = mine_ref.shape
         main = share - PIECE
         extras = extra_rows(slots, width, 2 * half)
-        small = jnp.concatenate(
-            [phi_grad_scr[:slots, b * LANES : (b + 1) * LANES] for b in range(pairs)]
-            + [rows_scr[:, b * LANES : (b + 1) * LANES] for b in range(pairs)],
-            axis=0,
-        )
         filled = small.shape[0]
         padded = 2 * half * extras
         if padded > filled:
@@ -801,11 +818,11 @@
 
 
 def back(
-    core, residual, low_two, dispatch, combine, cotangent, returned, sums, image_ids, gain2, phi,
-    out_weight, mixed, mixed_rest, qkv, recips, low_one, probs,
+    core, residual, low_two, weights, cotangent, returned, sums, image_ids, gain2, phi, out_weight,
+    mixed, mixed_rest, qkv, recips, low_one, probs,
 ):
     rows, seq_len, width = residual.shape
-    lanes = dispatch.shape[2]
+    lanes = weights.shape[2]
     pairs, tiles = width // LANES, seq_len // TILE
     devices = returned.shape[0] * returned.shape[1]
     share = share_rows(width, devices)
@@ -815,13 +832,14 @@
         grid=(rows,),
         in_specs=[
             pl.BlockSpec(memory_space=pltpu.SMEM),
-            block(width), block(width), block(lanes), block(lanes), block(width),
+            block(width), block(width), block(lanes), block(width),
             whole(*returned.shape), pl.BlockSpec((1, 8, width), lambda r: (r, 0, 0)),
             whole(rows, seq_len), whole(width), whole(*phi.shape), whole(width, width),
         ]
         + [pl.BlockSpec(memory_space=pl.ANY)] * 6,
         out_specs=[
-            pl.BlockSpec(memory_space=pl.ANY), pl.BlockSpec(memory_space=pl.ANY), block(3 * width), whole(devices // 2, share, LANES),
+            pl.BlockSpec(memory_space=pl.ANY), pl.BlockSpec(memory_space=pl.ANY),
+            pl.BlockSpec(memory_space=pl.ANY), whole(devices // 2, share, LANES),
             whole(devices // 2, share, LANES),
         ],
         out_shape=[
@@ -839,7 +857,7 @@
             pltpu.VMEM((seq_len, width), bf16),
             pltpu.VMEM((seq_len, width), bf16),
             pltpu.VMEM((seq_len, width), f32),
-            pltpu.VMEM((seq_len, lanes), bf16),
+            pltpu.VMEM((seq_len, 3 * width), bf16),
             pltpu.VMEM((seq_len, width), bf16),
             pltpu.VMEM((pairs, tiles, 2, TILE, LANES), bf16),
             pltpu.VMEM((pairs, tiles, 2, TILE, 2 * LANES), bf16),
@@ -855,16 +873,16 @@
             pltpu.SMEM((2, tiles * tiles), jnp.int32),
             pltpu.SemaphoreType.DMA((SLOTS,)),
             pltpu.SemaphoreType.DMA((5,)),
-            pltpu.SemaphoreType.DMA((2,)),
+            pltpu.SemaphoreType.DMA((3,)),
         ],
         cost_estimate=pl.CostEstimate(
             flops=60 * 10**9, bytes_accessed=20 * 10**6, transcendentals=10**7
         ),
-        compiler_params=params(50),
+        compiler_params=params(52),
         name="back",
     )(
-        core, residual, low_two, dispatch, combine, cotangent, returned, sums, image_ids, gain2, phi,
-        out_weight, mixed, mixed_rest, qkv, recips, low_one, probs,
+        core, residual, low_two, weights, cotangent, returned, sums, image_ids, gain2, phi, out_weight,
+        mixed, mixed_rest, qkv, recips, low_one, probs,
     )
 
 
@@ -1061,7 +1079,7 @@
         tokens, image_ids, ln1_gain, ln1_bias, query_bias, value_bias, qkv_weight, out_weight,
         out_bias, ln2_gain, ln2_bias,
     )
-    dispatch, combine, sent = route(low_two, cotangent, image_ids, slot_image, phi, dp, ep)
+    slot_weights, sent = route(low_two, cotangent, image_ids, slot_image, phi, dp, ep)
     per_device = sent.shape[2]
     arrived = exchange(sent.reshape(devices, per_device, width), ("y", "core", "expert"))
     parts, rows, hidden, pre_grad = experts(
@@ -1073,7 +1091,7 @@
     )
 
     output, resid_grad, qkv_grad, mine, other = back(
-        core.reshape(1), residual, low_two, dispatch, combine, cotangent,
+        core.reshape(1), residual, low_two, slot_weights, cotangent,
         returned.reshape(dp, ep, per_device, width), sums, image_ids, ln2_gain, phi, out_weight, mixed,
         mixed_rest, qkv, recips, low_one, probs,
     )

time: 171 us -> 169 us (0.988)
  starting transfers between devices: 24.4 us -> 26.4 us
    all_to_all x4, starting transfers between devices: 22.3 us -> 26.3 us  [exchange(): return lax.all_to_all(values, over, split_axis=0, concat_axis=0, tiled=True)]
    ppermute x1, starting transfers between devices: 2.07 us -> 0.07 us  [local(): met = lax.ppermute(other, 'core', swap)]
    unnamed x32 -> x28, local copies, waits for them, and re-layouts: 5.5 us -> 4.27 us
where the time goes in v5:
time: 169 us; the launch traced here: 170 us
  Pallas kernels  86.1 us (51%)
  waiting for transfers between devices  27.9 us (17%)
  starting transfers between devices  26.4 us (16%)
  blocking collectives  21.9 us (13%)
  local copies, waits for them, and re-layouts  6.17 us (4%)
    pallas_call x1, Pallas kernels, back(): pl.pallas_call(back_kernel, grid=(rows,), in_specs=[pl.BlockSpec(memory_s...  42.1 us
    pallas_call x1, Pallas kernels, attend(): pl.pallas_call(attend_kernel, grid=(rows,), in_specs=[block(width), whole...  26.8 us
    all_to_all x4, starting transfers between devices, exchange(): return lax.all_to_all(values, over, split_axis=0, concat_axis=0, tiled=True)  26.3 us
    all_to_all x4, waiting for transfers between devices, exchange(): return lax.all_to_all(values, over, split_axis=0, concat_axis=0, tiled=True)  23.8 us
    all_to_all x1, blocking collectives, exchange(): return lax.all_to_all(values, over, split_axis=0, concat_axis=0, tiled=True)  21.9 us
    pallas_call x1, Pallas kernels, input_back(): pl.pallas_call(input_kernel, grid=(rows,), in_specs=[block(width), block(...  5.09 us
    pallas_call x1, Pallas kernels, route(): pl.pallas_call(route_kernel, grid=(rows,), in_specs=[block(width), block(...  4.99 us
    unnamed x28, local copies, waits for them, and re-layouts  4.27 us
  transfers between devices with their start and end apart: 6, of which 5 were waited for; matrix products, arithmetic and copies ran while one was open for 0% of the time, Pallas kernels for 20%

profile of v5, /device:TPU:0, one launch (start us, length us, event | category | flops | bytes accessed | tf_op | source)
XLA Modules:
  0.0 169.5 jit_solution(1106179394978406760)
XLA Ops:
  0.7 1.3 broadcast_in_dim.2
  1.9 7.3 %all-to-all-start = ((bf16[8,2,384]{2,1,0:T(2,128)(2,1)}), bf16[8,2,384]{2,1,0:T(2,128)(2,1)S(1)}, u32[]{:S(2)}, u32[]{:S(2)}) async-start(bf16[8,2,384]{2,1,0:T(2,128)(2,1)} %broadcast_in_dim.2), calls=%async_computation | async-start | bytes 24576 | tf_op jit(solution)/shard_map/all_to_all | solution.py:1073
  9.2 26.8 %attend.1 = (bf16[2,1024,384]{2,1,0:T(8,128)(2,1)}, bf16[2,1024,1152]{2,1,0:T(8,128)(2,1)}, bf16[2,1024,384]{2,1,0:T(8,128)(2,1)}, bf16[2,1024,384]{2,1,0:T(8,12...) custom-call(bf16[2,1024,384]{2,1,0:T(8,128)(2,1)} %tokens_ref.3, ...), custom_call_target="tpu_custom_call" | custom-call | flops 20000000000 | bytes 20000000 | tf_op jit(solution)/shard_map/attend/pallas_call | solution.py:358
  36.1 0.0 all-to-all-done
  36.1 0.6 reshape.48.phi_ref
  36.7 5.0 %route.1 = (f32[2,1024,128]{2,1,0:T(8,128)}, bf16[4,8,8,384]{3,2,1,0:T(8,128)(2,1)}) custom-call(bf16[2,1024,384]{2,1,0:T(8,128)(2,1)} %get-tuple-element.60.low_two_ref, bf16[2,1024,384]{2,1,0:T(8,128)(2,1)} %cot_ref.3, s32[2,1024]{1,0:T(2,128)} %ids_ref.5, s32[2,16]{1,0:T(2,128)} %slot_ref.1, bf16[16,384]{1,0:T(8,128)(2,1)} %reshape.48.phi_ref), custom_call_target="tpu_custom_call" | custom-call | tf_op jit(solution)/shard_map/route/pallas_call | solution.py:472
  41.7 0.0 copy-start.3
  41.7 0.0 copy-start.7
  41.7 0.0 copy-start.8
  41.7 0.0 copy-start.12
  41.7 8.4 %all-to-all-start.1 = ((bf16[32,8,384]{2,1,0:T(8,128)(2,1)}), bf16[32,8,384]{2,1,0:T(8,128)(2,1)S(1)}, u32[]{:S(2)}, u32[]{:S(2)}) async-start(bf16[32,8,384]{2,1,0:T(8,128)(2,1)} %bitcast.7), calls=%async_computation.1 | async-start | bytes 393216 | tf_op jit(solution)/shard_map/all_to_all | solution.py:1073
  50.2 8.5 %all-to-all-done.1.arrived_ref = bf16[32,8,384]{2,1,0:T(8,128)(2,1)S(1)} async-done(((bf16[32,8,384]{2,1,0:T(8,128)(2,1)}), bf16[32,8,384]{2,1,0:T(8,128)(2,1)S(1)}, u32[]{:S(2)}, u32[]{:S(2)}) %all-to-all-start.1) | async-done | bytes 196640 | tf_op jit(solution)/shard_map/all_to_all | solution.py:1073
  58.7 1.9 %experts.1 = (bf16[32,8,384]{2,1,0:T(8,128)(2,1)}, bf16[2,2,64,384]{3,2,1,0:T(8,128)(2,1)S(1)}, bf16[2,64,384]{2,1,0:T(8,128)(2,1)S(1)}, bf16[2,64,384]{2,1,0:T(8,128)(2,1)S(1)}) custom-call(bf16[32,8,384]{2,1,0:T(8,128)(2,1)S(1)} %all-to-all-done.1.arrived_ref, bf16[2,384,384]{2,1,0:T(8,128)(2,1)S(1)} %copy-done, bf16[2,384]{1,0:T(2,128)(2,1)S(1)} %copy-done.4, ...), custom_call_target="tpu_custom_call" | custom-call | tf_op jit(solution)/shard_map/experts/pallas_call | solution.py:558
  60.6 3.0 %all-to-all-start.2 = ((bf16[32,8,384]{2,1,0:T(8,128)(2,1)}), bf16[32,8,384]{2,1,0:T(8,128)(2,1)S(1)}, u32[]{:S(2)}, u32[]{:S(2)}) async-start(bf16[32,8,384]{2,1,0:T(8,128)(2,1)} %get-tuple-element.63), calls=%async_computation.2 | async-start | bytes 393216 | tf_op jit(solution)/shard_map/all_to_all | solution.py:1073
  63.6 1.8 %expert_grads.1 = (f32[2,384,384]{2,1,0:T(8,128)}, f32[2,384]{1,0:T(2,128)}, f32[2,384,384]{2,1,0:T(8,128)}, f32[2,384]{1,0:T(2,128)}) custom-call(bf16[2,2,64,384]{3,2,1,0:T(8,128)(2,1)S(1)} %get-tuple-element.64.rows_ref, bf16[2,64,384]{2,1,0:T(8,128)(2,1)S(1)} %get-tuple-element.65.hidden_ref, bf16[2,64,384]{2,1,0:T(8,128)(2,1)S(1)} %get-tuple-element.66.pre_grad_ref), custom_call_target="tpu_custom_call" | custom-call | flops 75497472 | bytes 4000000 | tf_op jit(solution)/shard_map/expert_grads/pallas_call | solution.py:574
  65.5 6.7 %all-to-all-done.2 = bf16[32,8,384]{2,1,0:T(8,128)(2,1)S(1)} async-done(((bf16[32,8,384]{2,1,0:T(8,128)(2,1)}), bf16[32,8,384]{2,1,0:T(8,128)(2,1)S(1)}, u32[]{:S(2)}, u32[]{:S(2)}) %all-to-all-start.2) | async-done | bytes 196640 | tf_op jit(solution)/shard_map/all_to_all | solution.py:1073
  72.2 0.0 copy-done.3
  72.2 42.1 %back.1 = (bf16[2,1024,384]{2,1,0:T(8,128)(2,1)}, f32[2,1024,384]{2,1,0:T(8,128)}, bf16[2,1024,1152]{2,1,0:T(8,128)(2,1)}, bf16[16,160,128]{2,1,0:T(8,128)(2,1)S(1)}, bf16[16,160,128]{2,1,0:T(8,128)(2,1)S(1)}) custom-call(s32[1]{0:T(128)} %bitcast.core_ref, f32[2,1024,384]{2,1,0:T(8,128)} %get-tuple-element.59.residual_ref, ...), custom_call_target="tpu_custom_call" | custom-call | flops 60000002048 | bytes 20000000 | tf_op jit(solution)/shard_map/back/pallas_call | solution.py:830
  114.3 0.1 collective-permute-start
  114.4 2.1 %collective-permute-done.two_ref = bf16[16,160,128]{2,1,0:T(8,128)(2,1)S(1)} collective-permute-done((bf16[16,160,128]{2,1,0:T(8,128)(2,1)S(1)}, bf16[16,160,128]{2,1,0:T(8,128)(2,1)S(1)}, u32[]{:S(2)}, u32[]{:S(2)}) %collective-permute-start) | collective-permute-done | bytes 655392 | tf_op jit(solution)/shard_map/ppermute | solution.py:1099
  116.5 1.0 add.3
  117.5 7.6 %all-to-all-start.3 = ((bf16[16,160,128]{2,1,0:T(8,128)(2,1)}), bf16[16,160,128]{2,1,0:T(8,128)(2,1)S(1)}, u32[]{:S(2)}, u32[]{:S(2)}) async-start(bf16[16,160,128]{2,1,0:T(8,128)(2,1)} %add.3), calls=%async_computation.3 | async-start | bytes 1310720 | tf_op jit(solution)/shard_map/all_to_all | solution.py:1073
  125.1 2.3 %copy-done.10 = bf16[2,1024,1152]{2,1,0:T(8,128)(2,1)S(1)} copy-done((bf16[2,1024,1152]{2,1,0:T(8,128)(2,1)S(1)}, bf16[2,1024,1152]{2,1,0:T(8,128)(2,1)}, u32[]{:S(2)}) %copy-start.10) | copy-done | bytes 4718616
  127.4 1.9 %copy-done.11 = f32[2,1024,384]{2,1,0:T(8,128)S(1)} copy-done((f32[2,1024,384]{2,1,0:T(8,128)S(1)}, f32[2,1024,384]{2,1,0:T(8,128)}, u32[]{:S(2)}) %copy-start.11) | copy-done | bytes 3145752
  129.3 5.1 %input_back.1 = (bf16[2,1024,384]{2,1,0:T(8,128)(2,1)}, f32[8,384]{1,0:T(8,128)S(1)}) custom-call(bf16[2,1024,384]{2,1,0:T(8,128)(2,1)S(1)} %copy-done.5, bf16[2,1024,1152]{2,1,0:T(8,128)(2,1)S(1)} %copy-done.10, f32[2,1024,384]{2,1,0:T(8,128)S(1)} %copy-done.11, f32[384]{0:T(512)S(1)} %copy-done.9, bf16[384,1152]{1,0:T(8,128)(2,1)S(1)} %copy-done.6), custom_call_target="tpu_custom_call" | custom-call | flops 6000000000 | bytes 10000000 | tf_op jit(solution)/shard_map/input_back/pallas_call | solution.py:913
  134.4 8.6 %all-to-all-done.3.collected_ref = bf16[16,160,128]{2,1,0:T(8,128)(2,1)S(1)} async-done(((bf16[16,160,128]{2,1,0:T(8,128)(2,1)}), bf16[16,160,128]{2,1,0:T(8,128)(2,1)S(1)}, u32[]{:S(2)}, u32[]{:S(2)}) %all-to-all-start.3) | async-done | bytes 655392 | tf_op jit(solution)/shard_map/all_to_all | solution.py:1073
  143.0 0.1 fold.1
  143.1 21.9 %all_to_all.25.refs_1_ = bf16[16,160,128]{2,1,0:T(8,128)(2,1)S(1)} all-to-all(bf16[16,160,128]{2,1,0:T(8,128)(2,1)S(1)} %fold.1), channel_id=1, replica_groups=mesh['y'=2,'core'=2,'expert'=8] {'y','expert'}, dimensions={0} | all-to-all | bytes 1310720 | tf_op jit(solution)/shard_map/all_to_all | solution.py:1073
  165.0 0.0 collective-permute-start.1
  165.0 0.1 pad_add_fusion.refs_0_
  165.1 2.0 %collective-permute-done.1.refs_2_ = bf16[16,160,128]{2,1,0:T(8,128)(2,1)S(1)} collective-permute-done((bf16[16,160,128]{2,1,0:T(8,128)(2,1)S(1)}, bf16[16,160,128]{2,1,0:T(8,128)(2,1)S(1)}, u32[]{:S(2)}, u32[]{:S(2)}) %collective-permute-start.1) | collective-permute-done | bytes 655392 | tf_op jit(solution)/shard_map/ppermute | solution.py:1103
  167.1 2.2 %finish.1 = (f32[384,1152]{1,0:T(8,128)}, f32[384,384]{1,0:T(8,128)}, f32[384]{0:T(512)}, f32[384]{0:T(512)}, f32[384]{0:T(512)}, /*index=5*/f32[384]{0:T(512)},...) custom-call(s32[2]{0:T(128)S(1)} %pad_add_fusion.refs_0_, ...), custom_call_target="tpu_custom_call" | custom-call | tf_op jit(solution)/shard_map/finish/pallas_call | solution.py:1042
  (22 shorter events, 0.0 us)
Async XLA Ops:
  1.9 34.1 %all-to-all-start = ((bf16[8,2,384]{2,1,0:T(2,128)(2,1)}), bf16[8,2,384]{2,1,0:T(2,128)(2,1)S(1)}, u32[]{:S(2)}, u32[]{:S(2)}) async-start(bf16[8,2,384]{2,1,0:T(2,128)(2,1)} %broadcast_in_dim.2), calls=%async_computation | async-start | bytes 24576 | tf_op jit(solution)/shard_map/all_to_all | solution.py:1073
  36.7 13.5 %copy-start.13 = (f32[2,384]{1,0:T(2,128)S(1)}, f32[2,384]{1,0:T(2,128)}, u32[]{:S(2)}) copy-start(f32[2,384]{1,0:T(2,128)} %param.34) | copy-start | bytes 9220
  36.7 22.0 %copy-start = (bf16[2,384,384]{2,1,0:T(8,128)(2,1)S(1)}, bf16[2,384,384]{2,1,0:T(8,128)(2,1)}, u32[]{:S(2)}) copy-start(bf16[2,384,384]{2,1,0:T(8,128)(2,1)} %up_ref.1) | copy-start | bytes 1769476
  36.7 22.0 %copy-start.1 = (bf16[2,384,384]{2,1,0:T(8,128)(2,1)S(1)}, bf16[2,384,384]{2,1,0:T(8,128)(2,1)}, u32[]{:S(2)}) copy-start(bf16[2,384,384]{2,1,0:T(8,128)(2,1)} %down_ref.1) | copy-start | bytes 1769476
  36.7 22.0 %copy-start.4 = (bf16[2,384]{1,0:T(2,128)(2,1)S(1)}, bf16[2,384]{1,0:T(2,128)(2,1)}, u32[]{:S(2)}) copy-start(bf16[2,384]{1,0:T(2,128)(2,1)} %up_bias_ref.1) | copy-start | bytes 4612
  41.7 30.5 %copy-start.2 = (bf16[16,384]{1,0:T(8,128)(2,1)S(1)}, bf16[16,384]{1,0:T(8,128)(2,1)}, u32[]{:S(2)}) copy-start(bf16[16,384]{1,0:T(8,128)(2,1)} %reshape.48.phi_ref) | copy-start | bytes 36868
  41.7 30.5 %copy-start.3 = (s32[2,1024]{1,0:T(2,128)S(1)}, s32[2,1024]{1,0:T(2,128)}, u32[]{:S(2)}) copy-start(s32[2,1024]{1,0:T(2,128)} %ids_ref.5) | copy-start | bytes 24580
  41.7 30.5 %copy-start.7 = (bf16[384,384]{1,0:T(8,128)(2,1)S(1)}, bf16[384,384]{1,0:T(8,128)(2,1)}, u32[]{:S(2)}) copy-start(bf16[384,384]{1,0:T(8,128)(2,1)} %out_w_ref.3) | copy-start | bytes 884740
  41.7 30.5 %copy-start.8 = (f32[384]{0:T(512)S(1)}, f32[384]{0:T(512)}, u32[]{:S(2)}) copy-start(f32[384]{0:T(512)} %gain2_ref.3) | copy-start | bytes 4612
  41.7 30.5 %copy-start.12 = (f32[2,8,384]{2,1,0:T(8,128)S(1)}, f32[2,8,384]{2,1,0:T(8,128)}, u32[]{:S(2)}) copy-start(f32[2,8,384]{2,1,0:T(8,128)} %get-tuple-element.72.sums_ref) | copy-start | bytes 73732
  41.7 17.0 %all-to-all-start.1 = ((bf16[32,8,384]{2,1,0:T(8,128)(2,1)}), bf16[32,8,384]{2,1,0:T(8,128)(2,1)S(1)}, u32[]{:S(2)}, u32[]{:S(2)}) async-start(bf16[32,8,384]{2,1,0:T(8,128)(2,1)} %bitcast.7), calls=%async_computation.1 | async-start | bytes 393216 | tf_op jit(solution)/shard_map/all_to_all | solution.py:1073
  60.6 11.6 %all-to-all-start.2 = ((bf16[32,8,384]{2,1,0:T(8,128)(2,1)}), bf16[32,8,384]{2,1,0:T(8,128)(2,1)S(1)}, u32[]{:S(2)}, u32[]{:S(2)}) async-start(bf16[32,8,384]{2,1,0:T(8,128)(2,1)} %get-tuple-element.63), calls=%async_computation.2 | async-start | bytes 393216 | tf_op jit(solution)/shard_map/all_to_all | solution.py:1073
  114.3 2.2 %collective-permute-start = (bf16[16,160,128]{2,1,0:T(8,128)(2,1)S(1)}, bf16[16,160,128]{2,1,0:T(8,128)(2,1)S(1)}, u32[]{:S(2)}, u32[]{:S(2)}) collective-permute-start(bf16[16,160,128]{2,1,0:T(8,128)(2,1)S(1)} %get-tuple-element.84), channel_id=1, source_target_pairs={{0,8},{8,0},{1,9},{9,1},{2,10},{10,2},{3,11},{11,3},{4,12},{12,4},... | collective-permute-start | bytes 1966088 | tf_op jit(solution)/shard_map/ppermute | solution.py:1099
  116.5 8.6 %copy-start.5 = (bf16[2,1024,384]{2,1,0:T(8,128)(2,1)S(1)}, bf16[2,1024,384]{2,1,0:T(8,128)(2,1)}, u32[]{:S(2)}) copy-start(bf16[2,1024,384]{2,1,0:T(8,128)(2,1)} %tokens_ref.3) | copy-start | bytes 4718596
  116.5 8.6 %copy-start.6 = (bf16[384,1152]{1,0:T(8,128)(2,1)S(1)}, bf16[384,1152]{1,0:T(8,128)(2,1)}, u32[]{:S(2)}) copy-start(bf16[384,1152]{1,0:T(8,128)(2,1)} %qkv_w_ref.3) | copy-start | bytes 2654212
  116.5 8.6 %copy-start.9 = (f32[384]{0:T(512)S(1)}, f32[384]{0:T(512)}, u32[]{:S(2)}) copy-start(f32[384]{0:T(512)} %gain1_ref.3) | copy-start | bytes 4612
  117.5 25.6 %all-to-all-start.3 = ((bf16[16,160,128]{2,1,0:T(8,128)(2,1)}), bf16[16,160,128]{2,1,0:T(8,128)(2,1)S(1)}, u32[]{:S(2)}, u32[]{:S(2)}) async-start(bf16[16,160,128]{2,1,0:T(8,128)(2,1)} %add.3), calls=%async_computation.3 | async-start | bytes 1310720 | tf_op jit(solution)/shard_map/all_to_all | solution.py:1073
  125.1 2.3 %copy-start.10 = (bf16[2,1024,1152]{2,1,0:T(8,128)(2,1)S(1)}, bf16[2,1024,1152]{2,1,0:T(8,128)(2,1)}, u32[]{:S(2)}) copy-start(bf16[2,1024,1152]{2,1,0:T(8,128)(2,1)} %get-tuple-element.80.qkv_grad_ref) | copy-start | bytes 14155780
  127.4 1.9 %copy-start.11 = (f32[2,1024,384]{2,1,0:T(8,128)S(1)}, f32[2,1024,384]{2,1,0:T(8,128)}, u32[]{:S(2)}) copy-start(f32[2,1024,384]{2,1,0:T(8,128)} %get-tuple-element.81.resid_grad_ref) | copy-start | bytes 9437188
  165.0 2.1 %collective-permute-start.1 = (bf16[16,160,128]{2,1,0:T(8,128)(2,1)S(1)}, bf16[16,160,128]{2,1,0:T(8,128)(2,1)S(1)}, u32[]{:S(2)}, u32[]{:S(2)}) collective-permute-start(bf16[16,160,128]{2,1,0:T(8,128)(2,1)S(1)} %all_to_all.25.refs_1_), channel_id=1, source_target_pairs={{0,8},{8,0},{1,9},{9,1},{2,10},{10,2},{3,11},{11,3},{4,12},{12,4},... | collective-permute-start | bytes 1966088 | tf_op jit(solution)/shard_map/ppermute | solution.py:1103

commit v6 on v5

--- a/solution.py
+++ b/solution.py
@@ -15,6 +15,8 @@
 SAFE = 30.0
 GROUP = 2
 SLOTS = 2 * GROUP
+BACK_GROUP = 3
+BACK_SLOTS = 2 * BACK_GROUP
 PIECE = 16
 
 bf16 = jnp.bfloat16
@@ -76,18 +78,18 @@
     return total
 
 
-def over_tiles(total, work):
+def over_tiles(total, group, work):
     def together(g, carry):
-        work([g * GROUP + k for k in range(GROUP)])
+        work([g * group + k for k in range(group)])
         return carry
 
     def alone(n, carry):
         work([n])
         return carry
 
-    whole_groups = lax.div(total, GROUP)
+    whole_groups = lax.div(total, group)
     lax.fori_loop(0, whole_groups, together, 0)
-    lax.fori_loop(whole_groups * GROUP, total, alone, 0)
+    lax.fori_loop(whole_groups * group, total, alone, 0)
 
 
 def head_picker(width, copies=1):
@@ -261,7 +263,7 @@
 
     @pl.when(small)
     def _():
-        over_tiles(total_tiles, lambda numbers: weigh(numbers, lambda n, p: jnp.exp(scores(n, p))))
+        over_tiles(total_tiles, GROUP, lambda numbers: weigh(numbers, lambda n, p: jnp.exp(scores(n, p))))
 
     @pl.when(jnp.logical_not(small))
     def _():
@@ -584,13 +586,32 @@
     )(rows, hidden, pre_grad)
 
 
+def from_experts(back_ref, row, slots, lanes):
+    dp, ep, per_device, width = back_ref.shape
+    own = slots // ep
+    held = back_ref[0].astype(f32)
+    for d in range(1, dp):
+        held += back_ref[d].astype(f32)
+    held = held.reshape(ep * per_device, width).astype(bf16)
+
+    def of_kind(kind, first):
+        def wanted(lane):
+            slot = lane - first
+            device, mine = split(slot, own)
+            place = device * per_device + (row * 2 + kind) * own + mine
+            return jnp.where(jnp.logical_and(slot >= 0, slot < slots), place, -1)
+
+        return dot(selector(lanes, ep * per_device, wanted), held).astype(bf16)
+
+    return of_kind
+
+
 def back_kernel(
     core_ref, residual_ref, low_two_ref, weights_ref, cot_ref, back_ref, sums_ref,
     ids_ref, gain2_ref, phi_ref, out_w_ref, mixed_hbm, mixed_rest_hbm, qkv_hbm, recip_hbm,
     low_one_hbm, probs_ref,
-    output_hbm, resid_grad_hbm, qkv_grad_hbm, mine_ref, other_ref,
-    mixed_ref, mixed_rest_ref, qkv_ref, recip_ref, low_one_ref, output_ref, resid_grad_ref,
-    qkv_grad_ref,
+    resid_grad_hbm, qkv_grad_hbm, mine_ref, other_ref,
+    mixed_ref, mixed_rest_ref, qkv_ref, recip_ref, low_one_ref, resid_grad_ref, qkv_grad_ref,
     branch_scr, q_scr, o_scr, v_scr, dq_scr, dk_scr, dv_scr, grad_scr, p_scr, ds_scr,
     phi_grad_scr, rows_scr, list_scr, sem, in_sem, out_sem,
 ):
@@ -614,7 +635,7 @@
     total_tiles = key_tiles(starts, seq_len, list_scr)
 
     def fetch(n):
-        slot = lax.rem(n, SLOTS)
+        slot = lax.rem(n, BACK_SLOTS)
         return pltpu.make_async_copy(probs_ref.at[row, n], p_scr.at[slot], sem.at[slot])
 
     def brought(k, source, target):
@@ -628,41 +649,26 @@
     recip_in = brought(2, recip_hbm, recip_ref)
     qkv_in = brought(3, qkv_hbm, qkv_ref)
     low_one_in = brought(4, low_one_hbm, low_one_ref)
-    output_out = taken(0, output_ref, output_hbm)
     resid_out = taken(1, resid_grad_ref, resid_grad_hbm)
     qkv_grad_out = taken(2, qkv_grad_ref, qkv_grad_hbm)
     for copy in (mixed_in, rest_in, recip_in, qkv_in):
         copy.start()
-    for n in range(SLOTS):
-        fetch(n).start()
+    for n in range(BACK_SLOTS):
+
+        @pl.when(n < total_tiles)
+        def _(n=n):
+            fetch(n).start()
+
     low_one_in.start()
 
-    dp, ep, per_device, _ = back_ref.shape
-    own = slots // ep
-    held = back_ref[0].astype(f32)
-    for d in range(1, dp):
-        held += back_ref[d].astype(f32)
-    held = held.reshape(ep * per_device, width).astype(bf16)
-
-    def of_kind(kind, first):
-        def wanted(lane):
-            slot = lane - first
-            device, mine = split(slot, own)
-            place = device * per_device + (row * 2 + kind) * own + mine
-            return jnp.where(jnp.logical_and(slot >= 0, slot < slots), place, -1)
-
-        return dot(selector(slot_lanes, ep * per_device, wanted), held).astype(bf16)
-
-    expert_out = of_kind(0, half)
-    slot_grad = of_kind(1, 0)
+    returned = from_experts(back_ref, row, slots, slot_lanes)
+
+    expert_out = returned(0, half)
+    slot_grad = returned(1, 0)
     weights = weights_ref[0]
     left_slots = lax.broadcasted_iota(jnp.int32, weights.shape, 1) < half
     cot = cot_ref[0]
     low_two = low_two_ref[0]
-    moe_out = dot(weights.astype(bf16), expert_out)
-    output_ref[...] = (residual_ref[0] + moe_out).astype(bf16)
-    output_out.start()
-    moe_sq = jnp.sum(moe_out * moe_out, axis=0, keepdims=True)
     weight_grad = dot(cot, expert_out, NT) + dot(low_two, slot_grad, NT)
     weighted = weights * weight_grad
     slot_sum = jnp.sum(jnp.where(left_slots, 0.0, weighted), axis=1, keepdims=True)
@@ -724,7 +730,7 @@
             i = list_scr[0, n]
             at = pl.ds(pl.multiple_of(i * TILE, TILE), TILE)
             keys = pl.ds(pl.multiple_of(list_scr[1, n], LANES), TILE)
-            places.append((i, at, keys, lax.rem(n, SLOTS)))
+            places.append((i, at, keys, lax.rem(n, BACK_SLOTS)))
         for k, (i, at, keys, slot) in enumerate(places):
             for p in range(pairs):
                 o2 = o_scr[p, i].reshape(2 * TILE, 2 * LANES)
@@ -741,11 +747,11 @@
                 dv_scr[p, keys, :] += dot(p_scr[slot, p], o2, TN)
         for n in numbers:
 
-            @pl.when(n + SLOTS < total_tiles)
+            @pl.when(n + BACK_SLOTS < total_tiles)
             def _(n=n):
-                fetch(n + SLOTS).start()
-
-    over_tiles(total_tiles, gradients)
+                fetch(n + BACK_SLOTS).start()
+
+    over_tiles(total_tiles, BACK_GROUP, gradients)
     for p in range(pairs):
         for block, (source, factor) in enumerate(((dq_scr, scale), (dk_scr, 1.0), (dv_scr, 1.0))):
             start = block * width + p * LANES
@@ -756,10 +762,13 @@
     query_sum = jnp.sum(qkv_grad_ref[:, :width].astype(f32), axis=0, keepdims=True)
     value_sum = jnp.sum(qkv_grad_ref[:, 2 * width :].astype(f32), axis=0, keepdims=True)
     rows_scr[...] += jnp.concatenate(
-        [query_sum, value_sum, bias_sum, gain_sum, shift_sum, moe_sq, sums_ref[0, 0:2, :]], axis=0
-    )
-
-    output_out.wait()
+        [
+            query_sum, value_sum, bias_sum, gain_sum, shift_sum, jnp.zeros((1, width), f32),
+            sums_ref[0, 0:2, :],
+        ],
+        axis=0,
+    )
+
     resid_out.wait()
     qkv_grad_out.wait()
 
@@ -838,12 +847,11 @@
         ]
         + [pl.BlockSpec(memory_space=pl.ANY)] * 6,
         out_specs=[
-            pl.BlockSpec(memory_space=pl.ANY), pl.BlockSpec(memory_space=pl.ANY),
+            pl.BlockSpec(memory_space=pl.ANY),
             pl.BlockSpec(memory_space=pl.ANY), whole(devices // 2, share, LANES),
             whole(devices // 2, share, LANES),
         ],
         out_shape=[
-            jax.ShapeDtypeStruct((rows, seq_len, width), bf16),
             jax.ShapeDtypeStruct((rows, seq_len, width), f32),
             jax.ShapeDtypeStruct((rows, seq_len, 3 * width), bf16),
             jax.ShapeDtypeStruct((devices // 2, share, LANES), bf16),
@@ -854,7 +862,6 @@
             pltpu.VMEM((seq_len, width), bf16),
             pltpu.VMEM((seq_len, 3 * width), bf16),
             pltpu.VMEM((seq_len, LANES), f32),
-            pltpu.VMEM((seq_len, width), bf16),
             pltpu.VMEM((seq_len, width), bf16),
             pltpu.VMEM((seq_len, width), f32),
             pltpu.VMEM((seq_len, 3 * width), bf16),
@@ -866,12 +873,12 @@
             pltpu.VMEM((pairs, seq_len, LANES), f32),
             pltpu.VMEM((pairs, seq_len, LANES), f32),
             pltpu.VMEM((width, 4 * width), f32),
-            pltpu.VMEM((SLOTS, pairs, 2 * TILE, TILE), bf16),
-            pltpu.VMEM((GROUP, pairs, 2 * TILE, TILE), bf16),
+            pltpu.VMEM((BACK_SLOTS, pairs, 2 * TILE, TILE), bf16),
+            pltpu.VMEM((BACK_GROUP, pairs, 2 * TILE, TILE), bf16),
             pltpu.VMEM((lanes, width), f32),
             pltpu.VMEM((8, width), f32),
             pltpu.SMEM((2, tiles * tiles), jnp.int32),
-            pltpu.SemaphoreType.DMA((SLOTS,)),
+            pltpu.SemaphoreType.DMA((BACK_SLOTS,)),
             pltpu.SemaphoreType.DMA((5,)),
             pltpu.SemaphoreType.DMA((3,)),
         ],
@@ -886,7 +893,11 @@
     )
 
 
-def input_kernel(tokens_ref, qkv_grad_ref, resid_grad_ref, gain1_ref, qkv_w_ref, out_ref, rows_ref):
+def input_kernel(
+    tokens_ref, qkv_grad_ref, resid_grad_ref, gain1_ref, qkv_w_ref, residual_ref, weights_ref,
+    back_ref, out_ref, output_ref, rows_ref,
+    *, slots,
+):
     width = tokens_ref.shape[2]
 
     @pl.when(pl.program_id(0) == 0)
@@ -897,27 +908,36 @@
     hat, recip = norm_parts(tokens_ref[0].astype(f32))
     through = norm_back(grad, hat, recip, as_row(gain1_ref))
     out_ref[0] = (resid_grad_ref[0] + through).astype(bf16)
+    lanes = weights_ref.shape[2]
+    expert_out = from_experts(back_ref, pl.program_id(0), slots, lanes)(0, lanes // 2)
+    moe_out = dot(weights_ref[0].astype(bf16), expert_out)
+    output_ref[0] = (residual_ref[0] + moe_out).astype(bf16)
     rows_ref[...] += jnp.concatenate(
         [
             jnp.sum(grad * hat, axis=0, keepdims=True),
             jnp.sum(grad, axis=0, keepdims=True),
-            jnp.zeros((6, width), f32),
+            jnp.sum(moe_out * moe_out, axis=0, keepdims=True),
+            jnp.zeros((5, width), f32),
         ],
         axis=0,
     )
 
 
-def input_back(tokens, qkv_grad, resid_grad, gain1, qkv_weight):
+def input_back(
+    tokens, qkv_grad, resid_grad, gain1, qkv_weight, residual, weights, returned, slots
+):
     rows, seq_len, width = tokens.shape
     block = lambda n: per_row(seq_len, n)
     return pl.pallas_call(
-        input_kernel,
+        lambda *refs: input_kernel(*refs, slots=slots),
         grid=(rows,),
         in_specs=[
             block(width), block(3 * width), block(width), whole(width), whole(width, 3 * width),
-        ],
-        out_specs=[block(width), whole(8, width)],
+            block(width), block(weights.shape[2]), whole(*returned.shape),
+        ],
+        out_specs=[block(width), block(width), whole(8, width)],
         out_shape=[
+            jax.ShapeDtypeStruct((rows, seq_len, width), bf16),
             jax.ShapeDtypeStruct((rows, seq_len, width), bf16),
             jax.ShapeDtypeStruct((8, width), f32),
         ],
@@ -926,7 +946,7 @@
         ),
         compiler_params=params(40),
         name="input_back",
-    )(tokens, qkv_grad, resid_grad, gain1, qkv_weight)
+    )(tokens, qkv_grad, resid_grad, gain1, qkv_weight, residual, weights, returned)
 
 
 def add_kernel(one_ref, two_ref, sum_ref):
@@ -949,8 +969,8 @@
     total = collected_ref[0].astype(f32)
     for d in range(1, half):
         total += collected_ref[d].astype(f32)
-    ln1 = [ln1_ref[0:2, b * LANES : (b + 1) * LANES] for b in range(width // LANES)]
-    count = 2 * (width // LANES)
+    ln1 = [ln1_ref[0:3, b * LANES : (b + 1) * LANES] for b in range(width // LANES)]
+    count = 3 * (width // LANES)
     keep = PIECE - count
     tail = jnp.concatenate([total[main : main + keep]] + ln1, axis=0)
     low = jnp.concatenate([total[:main], tail], axis=0).astype(bf16)
@@ -1001,10 +1021,10 @@
 
     small = small_scr[...]
     ln1 = jnp.sum(small, axis=0)
-    keep = PIECE - 2 * pairs
+    keep = PIECE - 3 * pairs
     ln1 = [
-        jnp.concatenate([ln1[keep + 2 * b + k : keep + 2 * b + k + 1] for b in range(pairs)], axis=1)
-        for k in range(2)
+        jnp.concatenate([ln1[keep + 3 * b + k : keep + 3 * b + k + 1] for b in range(pairs)], axis=1)
+        for k in range(3)
     ]
     ln1_gain_ref[...] = ln1[0].reshape(width)
     ln1_bias_ref[...] = ln1[1].reshape(width)
@@ -1021,7 +1041,7 @@
     out_bias_ref[...] = vector(2).reshape(width)
     gain2_ref[...] = vector(3).reshape(width)
     shift2_ref[...] = vector(4).reshape(width)
-    squares = [jnp.sum(vector(k), axis=1, keepdims=True) for k in (6, 7, 5)]
+    squares = [jnp.sum(row, axis=1, keepdims=True) for row in (vector(6), vector(7), ln1[2])]
     rms_ref[...] = jnp.sqrt(jnp.concatenate(squares, axis=1) * (1.0 / count)).reshape(3)
     own = phi_ref.shape[0]
     ep = slots // own
@@ -1090,15 +1110,18 @@
         (returned, tuple(expert_grads(rows, hidden, pre_grad)))
     )
 
-    output, resid_grad, qkv_grad, mine, other = back(
+    returned = returned.reshape(dp, ep, per_device, width)
+    resid_grad, qkv_grad, mine, other = back(
         core.reshape(1), residual, low_two, slot_weights, cotangent,
-        returned.reshape(dp, ep, per_device, width), sums, image_ids, ln2_gain, phi, out_weight, mixed,
+        returned, sums, image_ids, ln2_gain, phi, out_weight, mixed,
         mixed_rest, qkv, recips, low_one, probs,
     )
 
     met = lax.ppermute(other, "core", swap)
     collected = exchange(add(mine, met), across)
-    input_grad, ln1_rows = input_back(tokens, qkv_grad, resid_grad, ln1_gain, qkv_weight)
+    input_grad, output, ln1_rows = input_back(
+        tokens, qkv_grad, resid_grad, ln1_gain, qkv_weight, residual, slot_weights, returned, slots
+    )
     shares = exchange(fold(collected, ln1_rows), across)
     others = lax.ppermute(shares, "core", swap)
     (

time: 169 us -> 169 us (level); the launches traced: 170 us -> 167 us
  Pallas kernels: 86.1 us -> 90.8 us
  starting transfers between devices: 26.4 us -> 22.3 us
  waiting for transfers between devices: 27.9 us -> 24.5 us
    all_to_all x4, starting transfers between devices: 26.3 us -> 22.1 us  [exchange(): return lax.all_to_all(values, over, split_axis=0, concat_axis=0, tiled=True)]
    all_to_all x4, waiting for transfers between devices: 23.8 us -> 20.6 us  [exchange(): return lax.all_to_all(values, over, split_axis=0, concat_axis=0, tiled=True)]
    pallas_call x1, Pallas kernels: 5.09 us -> 7.65 us  [input_back(): pl.pallas_call(lambda *refs: input_kernel(*refs, slots=slots), grid=(rows...]
    unnamed x28 -> x30, local copies, waits for them, and re-layouts: 4.27 us -> 4.99 us
  transfers between devices with their start and end apart: 6 -> 6, of which waited for: 5 -> 5; matrix products, arithmetic and copies ran while one was open for 0% -> 0% of each run, Pallas kernels for 20% -> 22%
where the time goes in v6:
time: 169 us; the launch traced here: 167 us
  Pallas kernels  90.8 us (54%)
  waiting for transfers between devices  24.5 us (14%)
  starting transfers between devices  22.3 us (13%)
  blocking collectives  21.9 us (13%)
  local copies, waits for them, and re-layouts  6.89 us (4%)
    pallas_call x1, Pallas kernels, back(): pl.pallas_call(back_kernel, grid=(rows,), in_specs=[pl.BlockSpec(memory_s...  43 us
    pallas_call x1, Pallas kernels, attend(): pl.pallas_call(attend_kernel, grid=(rows,), in_specs=[block(width), whole...  28.1 us
    all_to_all x4, starting transfers between devices, exchange(): return lax.all_to_all(values, over, split_axis=0, concat_axis=0, tiled=True)  22.1 us
    all_to_all x1, blocking collectives, exchange(): return lax.all_to_all(values, over, split_axis=0, concat_axis=0, tiled=True)  21.9 us
    all_to_all x4, waiting for transfers between devices, exchange(): return lax.all_to_all(values, over, split_axis=0, concat_axis=0, tiled=True)  20.6 us
    pallas_call x1, Pallas kernels, input_back(): pl.pallas_call(lambda *refs: input_kernel(*refs, slots=slots), grid=(rows...  7.65 us
    pallas_call x1, Pallas kernels, route(): pl.pallas_call(route_kernel, grid=(rows,), in_specs=[block(width), block(...  5 us
    unnamed x30, local copies, waits for them, and re-layouts  4.99 us
  transfers between devices with their start and end apart: 6, of which 5 were waited for; matrix products, arithmetic and copies ran while one was open for 0% of the time, Pallas kernels for 22%

profile of v6, /device:TPU:0, one launch (start us, length us, event | category | flops | bytes accessed | tf_op | source)
XLA Modules:
  0.0 167.5 jit_solution(8062138402212581112)
XLA Ops:
  0.7 1.3 broadcast_in_dim.2
  1.9 7.3 %all-to-all-start = ((bf16[8,2,384]{2,1,0:T(2,128)(2,1)}), bf16[8,2,384]{2,1,0:T(2,128)(2,1)S(1)}, u32[]{:S(2)}, u32[]{:S(2)}) async-start(bf16[8,2,384]{2,1,0:T(2,128)(2,1)} %broadcast_in_dim.2), calls=%async_computation | async-start | bytes 24576 | tf_op jit(solution)/shard_map/all_to_all | solution.py:1093
  9.2 28.1 %attend.1 = (bf16[2,1024,384]{2,1,0:T(8,128)(2,1)}, bf16[2,1024,1152]{2,1,0:T(8,128)(2,1)}, bf16[2,1024,384]{2,1,0:T(8,128)(2,1)}, bf16[2,1024,384]{2,1,0:T(8,12...) custom-call(bf16[2,1024,384]{2,1,0:T(8,128)(2,1)} %refs_0_.1, ...), custom_call_target="tpu_custom_call" | custom-call | flops 20000000000 | bytes 20000000 | tf_op jit(solution)/shard_map/attend/pallas_call | solution.py:360
  37.3 0.0 all-to-all-done
  37.3 0.6 reshape.48.phi_ref
  37.9 5.0 %route.1 = (f32[2,1024,128]{2,1,0:T(8,128)}, bf16[4,8,8,384]{3,2,1,0:T(8,128)(2,1)}) custom-call(bf16[2,1024,384]{2,1,0:T(8,128)(2,1)} %get-tuple-element.60.low_two_ref, bf16[2,1024,384]{2,1,0:T(8,128)(2,1)} %cot_ref.3, s32[2,1024]{1,0:T(2,128)} %ids_ref.5, s32[2,16]{1,0:T(2,128)} %slot_ref.1, bf16[16,384]{1,0:T(8,128)(2,1)} %reshape.48.phi_ref), custom_call_target="tpu_custom_call" | custom-call | tf_op jit(solution)/shard_map/route/pallas_call | solution.py:474
  42.9 0.0 copy-start.3
  42.9 0.0 copy-start.8
  42.9 0.0 copy-start.9
  42.9 6.1 %all-to-all-start.1 = ((bf16[32,8,384]{2,1,0:T(8,128)(2,1)}), bf16[32,8,384]{2,1,0:T(8,128)(2,1)S(1)}, u32[]{:S(2)}, u32[]{:S(2)}) async-start(bf16[32,8,384]{2,1,0:T(8,128)(2,1)} %bitcast.8), calls=%async_computation.1 | async-start | bytes 393216 | tf_op jit(solution)/shard_map/all_to_all | solution.py:1093
  49.0 8.5 %all-to-all-done.1.arrived_ref = bf16[32,8,384]{2,1,0:T(8,128)(2,1)S(1)} async-done(((bf16[32,8,384]{2,1,0:T(8,128)(2,1)}), bf16[32,8,384]{2,1,0:T(8,128)(2,1)S(1)}, u32[]{:S(2)}, u32[]{:S(2)}) %all-to-all-start.1) | async-done | bytes 196640 | tf_op jit(solution)/shard_map/all_to_all | solution.py:1093
  57.6 1.9 %experts.1 = (bf16[32,8,384]{2,1,0:T(8,128)(2,1)}, bf16[2,2,64,384]{3,2,1,0:T(8,128)(2,1)S(1)}, bf16[2,64,384]{2,1,0:T(8,128)(2,1)S(1)}, bf16[2,64,384]{2,1,0:T(8,128)(2,1)S(1)}) custom-call(bf16[32,8,384]{2,1,0:T(8,128)(2,1)S(1)} %all-to-all-done.1.arrived_ref, bf16[2,384,384]{2,1,0:T(8,128)(2,1)S(1)} %copy-done, bf16[2,384]{1,0:T(2,128)(2,1)S(1)} %copy-done.4, ...), custom_call_target="tpu_custom_call" | custom-call | tf_op jit(solution)/shard_map/experts/pallas_call | solution.py:560
  59.4 3.0 %all-to-all-start.2 = ((bf16[32,8,384]{2,1,0:T(8,128)(2,1)}), bf16[32,8,384]{2,1,0:T(8,128)(2,1)S(1)}, u32[]{:S(2)}, u32[]{:S(2)}) async-start(bf16[32,8,384]{2,1,0:T(8,128)(2,1)} %get-tuple-element.63), calls=%async_computation.2 | async-start | bytes 393216 | tf_op jit(solution)/shard_map/all_to_all | solution.py:1093
  62.5 1.8 %expert_grads.1 = (f32[2,384,384]{2,1,0:T(8,128)}, f32[2,384]{1,0:T(2,128)}, f32[2,384,384]{2,1,0:T(8,128)}, f32[2,384]{1,0:T(2,128)}) custom-call(bf16[2,2,64,384]{3,2,1,0:T(8,128)(2,1)S(1)} %get-tuple-element.64.rows_ref, bf16[2,64,384]{2,1,0:T(8,128)(2,1)S(1)} %get-tuple-element.65.hidden_ref, bf16[2,64,384]{2,1,0:T(8,128)(2,1)S(1)} %get-tuple-element.66.pre_grad_ref), custom_call_target="tpu_custom_call" | custom-call | flops 75497472 | bytes 4000000 | tf_op jit(solution)/shard_map/expert_grads/pallas_call | solution.py:576
  64.3 6.7 %all-to-all-done.2 = bf16[32,8,384]{2,1,0:T(8,128)(2,1)S(1)} async-done(((bf16[32,8,384]{2,1,0:T(8,128)(2,1)}), bf16[32,8,384]{2,1,0:T(8,128)(2,1)S(1)}, u32[]{:S(2)}, u32[]{:S(2)}) %all-to-all-start.2) | async-done | bytes 196640 | tf_op jit(solution)/shard_map/all_to_all | solution.py:1093
  71.1 43.0 %back.1 = (f32[2,1024,384]{2,1,0:T(8,128)}, bf16[2,1024,1152]{2,1,0:T(8,128)(2,1)}, bf16[16,160,128]{2,1,0:T(8,128)(2,1)S(1)}, bf16[16,160,128]{2,1,0:T(8,128)(2,1)S(1)}) custom-call(s32[1]{0:T(128)} %bitcast.core_ref, f32[2,1024,384]{2,1,0:T(8,128)} %get-tuple-element.59.residual_ref.refs_5_, bf16[2,1024,384]{2,1,0:T(8,128)(2,1)} %get-tuple-element.60.low_two_ref, ...), custom_call_target="tpu_custom_call" | custom-call | flops 60000002048 | bytes 20000000 | tf_op jit(solution)/shard_map/back/pallas_call | solution.py:839
  114.1 0.2 collective-permute-start
  114.3 2.0 %collective-permute-done.two_ref = bf16[16,160,128]{2,1,0:T(8,128)(2,1)S(1)} collective-permute-done((bf16[16,160,128]{2,1,0:T(8,128)(2,1)S(1)}, bf16[16,160,128]{2,1,0:T(8,128)(2,1)S(1)}, u32[]{:S(2)}, u32[]{:S(2)}) %collective-permute-start) | collective-permute-done | bytes 655392 | tf_op jit(solution)/shard_map/ppermute | solution.py:1120
  116.2 1.0 add.3
  117.2 5.7 %all-to-all-start.3 = ((bf16[16,160,128]{2,1,0:T(8,128)(2,1)}), bf16[16,160,128]{2,1,0:T(8,128)(2,1)S(1)}, u32[]{:S(2)}, u32[]{:S(2)}) async-start(bf16[16,160,128]{2,1,0:T(8,128)(2,1)} %add.3), calls=%async_computation.3 | async-start | bytes 1310720 | tf_op jit(solution)/shard_map/all_to_all | solution.py:1093
  123.0 0.0 copy-start.7
  123.0 1.2 copy-done.7
  124.2 1.9 %copy-done.11 = f32[2,1024,384]{2,1,0:T(8,128)S(1)} copy-done((f32[2,1024,384]{2,1,0:T(8,128)S(1)}, f32[2,1024,384]{2,1,0:T(8,128)}, u32[]{:S(2)}) %copy-start.11) | copy-done | bytes 3145752
  126.1 1.9 %copy-done.12 = f32[2,1024,384]{2,1,0:T(8,128)S(1)} copy-done((f32[2,1024,384]{2,1,0:T(8,128)S(1)}, f32[2,1024,384]{2,1,0:T(8,128)}, u32[]{:S(2)}) %copy-start.12) | copy-done | bytes 3145752
  128.0 7.6 %input_back.1 = (bf16[2,1024,384]{2,1,0:T(8,128)(2,1)}, bf16[2,1024,384]{2,1,0:T(8,128)(2,1)}, f32[8,384]{1,0:T(8,128)S(1)}) custom-call(bf16[2,1024,384]{2,1,0:T(8,128)(2,1)S(1)} %copy-done.5, bf16[2,1024,1152]{2,1,0:T(8,128)(2,1)} %get-tuple-element.79.refs_1_, f32[2,1024,384]{2,1,0:T(8,128)S(1)} %copy-done.12, f32[384]{0:T(512)S(1)} %copy-done.10, ...), custom_call_target="tpu_custom_call" | custom-call | flops 6000000000 | bytes 10000000 | tf_op jit(solution)/shard_map/input_back/pallas_call | solution.py:931
  135.6 5.3 %all-to-all-done.3.collected_ref = bf16[16,160,128]{2,1,0:T(8,128)(2,1)S(1)} async-done(((bf16[16,160,128]{2,1,0:T(8,128)(2,1)}), bf16[16,160,128]{2,1,0:T(8,128)(2,1)S(1)}, u32[]{:S(2)}, u32[]{:S(2)}) %all-to-all-start.3) | async-done | bytes 655392 | tf_op jit(solution)/shard_map/all_to_all | solution.py:1093
  140.9 0.1 fold.1
  141.0 21.9 %all_to_all.25.refs_1_ = bf16[16,160,128]{2,1,0:T(8,128)(2,1)S(1)} all-to-all(bf16[16,160,128]{2,1,0:T(8,128)(2,1)S(1)} %fold.1), channel_id=1, replica_groups=mesh['y'=2,'core'=2,'expert'=8] {'y','expert'}, dimensions={0} | all-to-all | bytes 1310720 | tf_op jit(solution)/shard_map/all_to_all | solution.py:1093
  162.9 0.0 collective-permute-start.1
  162.9 0.1 pad_add_fusion.refs_0_
  163.0 2.0 %collective-permute-done.1.refs_2_ = bf16[16,160,128]{2,1,0:T(8,128)(2,1)S(1)} collective-permute-done((bf16[16,160,128]{2,1,0:T(8,128)(2,1)S(1)}, bf16[16,160,128]{2,1,0:T(8,128)(2,1)S(1)}, u32[]{:S(2)}, u32[]{:S(2)}) %collective-permute-start.1) | collective-permute-done | bytes 655392 | tf_op jit(solution)/shard_map/ppermute | solution.py:1126
  165.0 2.3 %finish.1 = (f32[384,1152]{1,0:T(8,128)}, f32[384,384]{1,0:T(8,128)}, f32[384]{0:T(512)}, f32[384]{0:T(512)}, f32[384]{0:T(512)}, /*index=5*/f32[384]{0:T(512)},...) custom-call(s32[2]{0:T(128)S(1)} %pad_add_fusion.refs_0_, ...), custom_call_target="tpu_custom_call" | custom-call | tf_op jit(solution)/shard_map/finish/pallas_call | solution.py:1062
  (24 shorter events, 0.0 us)
Async XLA Ops:
  1.9 35.3 %all-to-all-start = ((bf16[8,2,384]{2,1,0:T(2,128)(2,1)}), bf16[8,2,384]{2,1,0:T(2,128)(2,1)S(1)}, u32[]{:S(2)}, u32[]{:S(2)}) async-start(bf16[8,2,384]{2,1,0:T(2,128)(2,1)} %broadcast_in_dim.2), calls=%async_computation | async-start | bytes 24576 | tf_op jit(solution)/shard_map/all_to_all | solution.py:1093
  37.9 11.1 %copy-start.14 = (f32[2,384]{1,0:T(2,128)S(1)}, f32[2,384]{1,0:T(2,128)}, u32[]{:S(2)}) copy-start(f32[2,384]{1,0:T(2,128)} %param.34) | copy-start | bytes 9220
  37.9 19.7 %copy-start = (bf16[2,384,384]{2,1,0:T(8,128)(2,1)S(1)}, bf16[2,384,384]{2,1,0:T(8,128)(2,1)}, u32[]{:S(2)}) copy-start(bf16[2,384,384]{2,1,0:T(8,128)(2,1)} %up_ref.1) | copy-start | bytes 1769476
  37.9 19.7 %copy-start.1 = (bf16[2,384,384]{2,1,0:T(8,128)(2,1)S(1)}, bf16[2,384,384]{2,1,0:T(8,128)(2,1)}, u32[]{:S(2)}) copy-start(bf16[2,384,384]{2,1,0:T(8,128)(2,1)} %down_ref.1) | copy-start | bytes 1769476
  37.9 19.7 %copy-start.4 = (bf16[2,384]{1,0:T(2,128)(2,1)S(1)}, bf16[2,384]{1,0:T(2,128)(2,1)}, u32[]{:S(2)}) copy-start(bf16[2,384]{1,0:T(2,128)(2,1)} %up_bias_ref.1) | copy-start | bytes 4612
  42.9 28.1 %copy-start.2 = (bf16[16,384]{1,0:T(8,128)(2,1)S(1)}, bf16[16,384]{1,0:T(8,128)(2,1)}, u32[]{:S(2)}) copy-start(bf16[16,384]{1,0:T(8,128)(2,1)} %reshape.48.phi_ref) | copy-start | bytes 36868
  42.9 28.1 %copy-start.3 = (s32[2,1024]{1,0:T(2,128)S(1)}, s32[2,1024]{1,0:T(2,128)}, u32[]{:S(2)}) copy-start(s32[2,1024]{1,0:T(2,128)} %ids_ref.5) | copy-start | bytes 24580
  42.9 28.1 %copy-start.8 = (bf16[384,384]{1,0:T(8,128)(2,1)S(1)}, bf16[384,384]{1,0:T(8,128)(2,1)}, u32[]{:S(2)}) copy-start(bf16[384,384]{1,0:T(8,128)(2,1)} %out_w_ref.3) | copy-start | bytes 884740
  42.9 28.1 %copy-start.9 = (f32[384]{0:T(512)S(1)}, f32[384]{0:T(512)}, u32[]{:S(2)}) copy-start(f32[384]{0:T(512)} %gain2_ref.3) | copy-start | bytes 4612
  42.9 28.1 %copy-start.13 = (f32[2,8,384]{2,1,0:T(8,128)S(1)}, f32[2,8,384]{2,1,0:T(8,128)}, u32[]{:S(2)}) copy-start(f32[2,8,384]{2,1,0:T(8,128)} %get-tuple-element.72.sums_ref) | copy-start | bytes 73732
  42.9 14.6 %all-to-all-start.1 = ((bf16[32,8,384]{2,1,0:T(8,128)(2,1)}), bf16[32,8,384]{2,1,0:T(8,128)(2,1)S(1)}, u32[]{:S(2)}, u32[]{:S(2)}) async-start(bf16[32,8,384]{2,1,0:T(8,128)(2,1)} %bitcast.8), calls=%async_computation.1 | async-start | bytes 393216 | tf_op jit(solution)/shard_map/all_to_all | solution.py:1093
  59.4 11.6 %all-to-all-start.2 = ((bf16[32,8,384]{2,1,0:T(8,128)(2,1)}), bf16[32,8,384]{2,1,0:T(8,128)(2,1)S(1)}, u32[]{:S(2)}, u32[]{:S(2)}) async-start(bf16[32,8,384]{2,1,0:T(8,128)(2,1)} %get-tuple-element.63), calls=%async_computation.2 | async-start | bytes 393216 | tf_op jit(solution)/shard_map/all_to_all | solution.py:1093
  114.1 2.2 %collective-permute-start = (bf16[16,160,128]{2,1,0:T(8,128)(2,1)S(1)}, bf16[16,160,128]{2,1,0:T(8,128)(2,1)S(1)}, u32[]{:S(2)}, u32[]{:S(2)}) collective-permute-start(bf16[16,160,128]{2,1,0:T(8,128)(2,1)S(1)} %get-tuple-element.84), channel_id=1, source_target_pairs={{0,8},{8,0},{1,9},{9,1},{2,10},{10,2},{3,11},{11,3},{4,12},{12,4},... | collective-permute-start | bytes 1966088 | tf_op jit(solution)/shard_map/ppermute | solution.py:1120
  116.2 6.8 %copy-start.5 = (bf16[2,1024,384]{2,1,0:T(8,128)(2,1)S(1)}, bf16[2,1024,384]{2,1,0:T(8,128)(2,1)}, u32[]{:S(2)}) copy-start(bf16[2,1024,384]{2,1,0:T(8,128)(2,1)} %refs_0_.1) | copy-start | bytes 4718596
  116.2 6.8 %copy-start.6 = (f32[2,1024,128]{2,1,0:T(8,128)S(1)}, f32[2,1024,128]{2,1,0:T(8,128)}, u32[]{:S(2)}) copy-start(f32[2,1024,128]{2,1,0:T(8,128)} %get-tuple-element.61.weights_ref.refs_6_) | copy-start | bytes 3145732
  116.2 6.8 %copy-start.10 = (f32[384]{0:T(512)S(1)}, f32[384]{0:T(512)}, u32[]{:S(2)}) copy-start(f32[384]{0:T(512)} %refs_3_.1) | copy-start | bytes 4612
  117.2 23.7 %all-to-all-start.3 = ((bf16[16,160,128]{2,1,0:T(8,128)(2,1)}), bf16[16,160,128]{2,1,0:T(8,128)(2,1)S(1)}, u32[]{:S(2)}, u32[]{:S(2)}) async-start(bf16[16,160,128]{2,1,0:T(8,128)(2,1)} %add.3), calls=%async_computation.3 | async-start | bytes 1310720 | tf_op jit(solution)/shard_map/all_to_all | solution.py:1093
  123.0 1.2 copy-start.7
  124.2 1.9 %copy-start.11 = (f32[2,1024,384]{2,1,0:T(8,128)S(1)}, f32[2,1024,384]{2,1,0:T(8,128)}, u32[]{:S(2)}) copy-start(f32[2,1024,384]{2,1,0:T(8,128)} %get-tuple-element.59.residual_ref.refs_5_) | copy-start | bytes 9437188
  126.1 1.9 %copy-start.12 = (f32[2,1024,384]{2,1,0:T(8,128)S(1)}, f32[2,1024,384]{2,1,0:T(8,128)}, u32[]{:S(2)}) copy-start(f32[2,1024,384]{2,1,0:T(8,128)} %get-tuple-element.80.refs_2_) | copy-start | bytes 9437188
  162.9 2.1 %collective-permute-start.1 = (bf16[16,160,128]{2,1,0:T(8,128)(2,1)S(1)}, bf16[16,160,128]{2,1,0:T(8,128)(2,1)S(1)}, u32[]{:S(2)}, u32[]{:S(2)}) collective-permute-start(bf16[16,160,128]{2,1,0:T(8,128)(2,1)S(1)} %all_to_all.25.refs_1_), channel_id=1, source_target_pairs={{0,8},{8,0},{1,9},{9,1},{2,10},{10,2},{3,11},{11,3},{4,12},{12,4},... | collective-permute-start | bytes 1966088 | tf_op jit(solution)/shard_map/ppermute | solution.py:1126

commit v7 on v6

--- a/solution.py
+++ b/solution.py
@@ -224,12 +224,12 @@
     acc_scr[...] = jnp.zeros_like(acc_scr)
 
     picker = head_picker(width)
-
-    def longest(low):
-        wide = low.astype(f32)
-        return jnp.max(dot((wide * wide).astype(bf16), picker), axis=0, keepdims=True)
-
-    bound = jnp.max(longest(query) * longest(key)) * (scale * scale)
+    other_lanes = pltpu.roll(picker.astype(f32), 8, 1).astype(bf16)
+    q_wide, k_wide = query.astype(f32), key.astype(f32)
+    squares = jnp.concatenate([q_wide * q_wide, k_wide * k_wide], axis=1).astype(bf16)
+    most = jnp.max(dot(squares, jnp.concatenate([picker, other_lanes], axis=0)), axis=0, keepdims=True)
+    most = jnp.broadcast_to(most, (8, LANES))
+    bound = jnp.max(most * pltpu.roll(most, 8, 1)) * (scale * scale)
     small = bound <= SAFE * SAFE
 
     def leave(n):

time: 169 us -> 169 us (level)
  transfers between devices with their start and end apart: 6 -> 6, of which waited for: 5 -> 5; matrix products, arithmetic and copies ran while one was open for 0% -> 0% of each run, Pallas kernels for 22% -> 23%
where the time goes in v7:
time: 169 us; the launch traced here: 167 us
  Pallas kernels  90.9 us (54%)
  waiting for transfers between devices  24.8 us (15%)
  blocking collectives  22 us (13%)
  starting transfers between devices  21.2 us (13%)
  local copies, waits for them, and re-layouts  6.89 us (4%)
    pallas_call x1, Pallas kernels, back(): pl.pallas_call(back_kernel, grid=(rows,), in_specs=[pl.BlockSpec(memory_s...  43 us
    pallas_call x1, Pallas kernels, attend(): pl.pallas_call(attend_kernel, grid=(rows,), in_specs=[block(width), whole...  28.2 us
    all_to_all x1, blocking collectives, exchange(): return lax.all_to_all(values, over, split_axis=0, concat_axis=0, tiled=True)  22 us
    all_to_all x4, starting transfers between devices, exchange(): return lax.all_to_all(values, over, split_axis=0, concat_axis=0, tiled=True)  21 us
    all_to_all x4, waiting for transfers between devices, exchange(): return lax.all_to_all(values, over, split_axis=0, concat_axis=0, tiled=True)  20.8 us
    pallas_call x1, Pallas kernels, input_back(): pl.pallas_call(lambda *refs: input_kernel(*refs, slots=slots), grid=(rows...  7.65 us
    unnamed x30, local copies, waits for them, and re-layouts  4.99 us
    pallas_call x1, Pallas kernels, route(): pl.pallas_call(route_kernel, grid=(rows,), in_specs=[block(width), block(...  4.99 us
  transfers between devices with their start and end apart: 6, of which 5 were waited for; matrix products, arithmetic and copies ran while one was open for 0% of the time, Pallas kernels for 23%

profile of v7, /device:TPU:0, one launch (start us, length us, event | category | flops | bytes accessed | tf_op | source)
XLA Modules:
  0.0 166.8 jit_solution(5135563737037724912)
XLA Ops:
  0.7 1.3 broadcast_in_dim.2
  1.9 7.3 %all-to-all-start = ((bf16[8,2,384]{2,1,0:T(2,128)(2,1)}), bf16[8,2,384]{2,1,0:T(2,128)(2,1)S(1)}, u32[]{:S(2)}, u32[]{:S(2)}) async-start(bf16[8,2,384]{2,1,0:T(2,128)(2,1)} %broadcast_in_dim.2), calls=%async_computation | async-start | bytes 24576 | tf_op jit(solution)/shard_map/all_to_all | solution.py:1093
  9.2 28.2 %attend.1 = (bf16[2,1024,384]{2,1,0:T(8,128)(2,1)}, bf16[2,1024,1152]{2,1,0:T(8,128)(2,1)}, bf16[2,1024,384]{2,1,0:T(8,128)(2,1)}, bf16[2,1024,384]{2,1,0:T(8,12...) custom-call(bf16[2,1024,384]{2,1,0:T(8,128)(2,1)} %refs_0_.1, ...), custom_call_target="tpu_custom_call" | custom-call | flops 20000000000 | bytes 20000000 | tf_op jit(solution)/shard_map/attend/pallas_call | solution.py:360
  37.4 0.0 all-to-all-done
  37.4 0.6 reshape.48.phi_ref
  38.0 5.0 %route.1 = (f32[2,1024,128]{2,1,0:T(8,128)}, bf16[4,8,8,384]{3,2,1,0:T(8,128)(2,1)}) custom-call(bf16[2,1024,384]{2,1,0:T(8,128)(2,1)} %get-tuple-element.60.low_two_ref, bf16[2,1024,384]{2,1,0:T(8,128)(2,1)} %cot_ref.3, s32[2,1024]{1,0:T(2,128)} %ids_ref.5, s32[2,16]{1,0:T(2,128)} %slot_ref.1, bf16[16,384]{1,0:T(8,128)(2,1)} %reshape.48.phi_ref), custom_call_target="tpu_custom_call" | custom-call | tf_op jit(solution)/shard_map/route/pallas_call | solution.py:474
  43.0 0.0 copy-start.3
  43.1 0.0 copy-start.8
  43.1 0.0 copy-start.9
  43.1 5.5 %all-to-all-start.1 = ((bf16[32,8,384]{2,1,0:T(8,128)(2,1)}), bf16[32,8,384]{2,1,0:T(8,128)(2,1)S(1)}, u32[]{:S(2)}, u32[]{:S(2)}) async-start(bf16[32,8,384]{2,1,0:T(8,128)(2,1)} %bitcast.8), calls=%async_computation.1 | async-start | bytes 393216 | tf_op jit(solution)/shard_map/all_to_all | solution.py:1093
  48.6 8.5 %all-to-all-done.1.arrived_ref = bf16[32,8,384]{2,1,0:T(8,128)(2,1)S(1)} async-done(((bf16[32,8,384]{2,1,0:T(8,128)(2,1)}), bf16[32,8,384]{2,1,0:T(8,128)(2,1)S(1)}, u32[]{:S(2)}, u32[]{:S(2)}) %all-to-all-start.1) | async-done | bytes 196640 | tf_op jit(solution)/shard_map/all_to_all | solution.py:1093
  57.2 1.9 %experts.1 = (bf16[32,8,384]{2,1,0:T(8,128)(2,1)}, bf16[2,2,64,384]{3,2,1,0:T(8,128)(2,1)S(1)}, bf16[2,64,384]{2,1,0:T(8,128)(2,1)S(1)}, bf16[2,64,384]{2,1,0:T(8,128)(2,1)S(1)}) custom-call(bf16[32,8,384]{2,1,0:T(8,128)(2,1)S(1)} %all-to-all-done.1.arrived_ref, bf16[2,384,384]{2,1,0:T(8,128)(2,1)S(1)} %copy-done, bf16[2,384]{1,0:T(2,128)(2,1)S(1)} %copy-done.4, ...), custom_call_target="tpu_custom_call" | custom-call | tf_op jit(solution)/shard_map/experts/pallas_call | solution.py:560
  59.0 3.0 %all-to-all-start.2 = ((bf16[32,8,384]{2,1,0:T(8,128)(2,1)}), bf16[32,8,384]{2,1,0:T(8,128)(2,1)S(1)}, u32[]{:S(2)}, u32[]{:S(2)}) async-start(bf16[32,8,384]{2,1,0:T(8,128)(2,1)} %get-tuple-element.63), calls=%async_computation.2 | async-start | bytes 393216 | tf_op jit(solution)/shard_map/all_to_all | solution.py:1093
  62.1 1.8 %expert_grads.1 = (f32[2,384,384]{2,1,0:T(8,128)}, f32[2,384]{1,0:T(2,128)}, f32[2,384,384]{2,1,0:T(8,128)}, f32[2,384]{1,0:T(2,128)}) custom-call(bf16[2,2,64,384]{3,2,1,0:T(8,128)(2,1)S(1)} %get-tuple-element.64.rows_ref, bf16[2,64,384]{2,1,0:T(8,128)(2,1)S(1)} %get-tuple-element.65.hidden_ref, bf16[2,64,384]{2,1,0:T(8,128)(2,1)S(1)} %get-tuple-element.66.pre_grad_ref), custom_call_target="tpu_custom_call" | custom-call | flops 75497472 | bytes 4000000 | tf_op jit(solution)/shard_map/expert_grads/pallas_call | solution.py:576
  63.9 6.7 %all-to-all-done.2 = bf16[32,8,384]{2,1,0:T(8,128)(2,1)S(1)} async-done(((bf16[32,8,384]{2,1,0:T(8,128)(2,1)}), bf16[32,8,384]{2,1,0:T(8,128)(2,1)S(1)}, u32[]{:S(2)}, u32[]{:S(2)}) %all-to-all-start.2) | async-done | bytes 196640 | tf_op jit(solution)/shard_map/all_to_all | solution.py:1093
  70.6 43.0 %back.1 = (f32[2,1024,384]{2,1,0:T(8,128)}, bf16[2,1024,1152]{2,1,0:T(8,128)(2,1)}, bf16[16,160,128]{2,1,0:T(8,128)(2,1)S(1)}, bf16[16,160,128]{2,1,0:T(8,128)(2,1)S(1)}) custom-call(s32[1]{0:T(128)} %bitcast.core_ref, f32[2,1024,384]{2,1,0:T(8,128)} %get-tuple-element.59.residual_ref.refs_5_, bf16[2,1024,384]{2,1,0:T(8,128)(2,1)} %get-tuple-element.60.low_two_ref, ...), custom_call_target="tpu_custom_call" | custom-call | flops 60000002048 | bytes 20000000 | tf_op jit(solution)/shard_map/back/pallas_call | solution.py:839
  113.7 0.2 collective-permute-start
  113.9 2.0 %collective-permute-done.two_ref = bf16[16,160,128]{2,1,0:T(8,128)(2,1)S(1)} collective-permute-done((bf16[16,160,128]{2,1,0:T(8,128)(2,1)S(1)}, bf16[16,160,128]{2,1,0:T(8,128)(2,1)S(1)}, u32[]{:S(2)}, u32[]{:S(2)}) %collective-permute-start) | collective-permute-done | bytes 655392 | tf_op jit(solution)/shard_map/ppermute | solution.py:1120
  115.8 1.0 add.3
  116.8 5.2 %all-to-all-start.3 = ((bf16[16,160,128]{2,1,0:T(8,128)(2,1)}), bf16[16,160,128]{2,1,0:T(8,128)(2,1)S(1)}, u32[]{:S(2)}, u32[]{:S(2)}) async-start(bf16[16,160,128]{2,1,0:T(8,128)(2,1)} %add.3), calls=%async_computation.3 | async-start | bytes 1310720 | tf_op jit(solution)/shard_map/all_to_all | solution.py:1093
  122.0 0.0 copy-start.7
  122.0 1.2 copy-done.7
  123.2 1.9 %copy-done.11 = f32[2,1024,384]{2,1,0:T(8,128)S(1)} copy-done((f32[2,1024,384]{2,1,0:T(8,128)S(1)}, f32[2,1024,384]{2,1,0:T(8,128)}, u32[]{:S(2)}) %copy-start.11) | copy-done | bytes 3145752
  125.1 1.9 %copy-done.12 = f32[2,1024,384]{2,1,0:T(8,128)S(1)} copy-done((f32[2,1024,384]{2,1,0:T(8,128)S(1)}, f32[2,1024,384]{2,1,0:T(8,128)}, u32[]{:S(2)}) %copy-start.12) | copy-done | bytes 3145752
  127.0 7.6 %input_back.1 = (bf16[2,1024,384]{2,1,0:T(8,128)(2,1)}, bf16[2,1024,384]{2,1,0:T(8,128)(2,1)}, f32[8,384]{1,0:T(8,128)S(1)}) custom-call(bf16[2,1024,384]{2,1,0:T(8,128)(2,1)S(1)} %copy-done.5, bf16[2,1024,1152]{2,1,0:T(8,128)(2,1)} %get-tuple-element.79.refs_1_, f32[2,1024,384]{2,1,0:T(8,128)S(1)} %copy-done.12, f32[384]{0:T(512)S(1)} %copy-done.10, ...), custom_call_target="tpu_custom_call" | custom-call | flops 6000000000 | bytes 10000000 | tf_op jit(solution)/shard_map/input_back/pallas_call | solution.py:931
  134.6 5.6 %all-to-all-done.3.collected_ref = bf16[16,160,128]{2,1,0:T(8,128)(2,1)S(1)} async-done(((bf16[16,160,128]{2,1,0:T(8,128)(2,1)}), bf16[16,160,128]{2,1,0:T(8,128)(2,1)S(1)}, u32[]{:S(2)}, u32[]{:S(2)}) %all-to-all-start.3) | async-done | bytes 655392 | tf_op jit(solution)/shard_map/all_to_all | solution.py:1093
  140.2 0.1 fold.1
  140.3 22.0 %all_to_all.25.refs_1_ = bf16[16,160,128]{2,1,0:T(8,128)(2,1)S(1)} all-to-all(bf16[16,160,128]{2,1,0:T(8,128)(2,1)S(1)} %fold.1), channel_id=1, replica_groups=mesh['y'=2,'core'=2,'expert'=8] {'y','expert'}, dimensions={0} | all-to-all | bytes 1310720 | tf_op jit(solution)/shard_map/all_to_all | solution.py:1093
  162.3 0.0 collective-permute-start.1
  162.3 0.1 pad_add_fusion.refs_0_
  162.4 2.0 %collective-permute-done.1.refs_2_ = bf16[16,160,128]{2,1,0:T(8,128)(2,1)S(1)} collective-permute-done((bf16[16,160,128]{2,1,0:T(8,128)(2,1)S(1)}, bf16[16,160,128]{2,1,0:T(8,128)(2,1)S(1)}, u32[]{:S(2)}, u32[]{:S(2)}) %collective-permute-start.1) | collective-permute-done | bytes 655392 | tf_op jit(solution)/shard_map/ppermute | solution.py:1126
  164.4 2.3 %finish.1 = (f32[384,1152]{1,0:T(8,128)}, f32[384,384]{1,0:T(8,128)}, f32[384]{0:T(512)}, f32[384]{0:T(512)}, f32[384]{0:T(512)}, /*index=5*/f32[384]{0:T(512)},...) custom-call(s32[2]{0:T(128)S(1)} %pad_add_fusion.refs_0_, ...), custom_call_target="tpu_custom_call" | custom-call | tf_op jit(solution)/shard_map/finish/pallas_call | solution.py:1062
  (24 shorter events, 0.0 us)
Async XLA Ops:
  1.9 35.5 %all-to-all-start = ((bf16[8,2,384]{2,1,0:T(2,128)(2,1)}), bf16[8,2,384]{2,1,0:T(2,128)(2,1)S(1)}, u32[]{:S(2)}, u32[]{:S(2)}) async-start(bf16[8,2,384]{2,1,0:T(2,128)(2,1)} %broadcast_in_dim.2), calls=%async_computation | async-start | bytes 24576 | tf_op jit(solution)/shard_map/all_to_all | solution.py:1093
  38.0 10.6 %copy-start.14 = (f32[2,384]{1,0:T(2,128)S(1)}, f32[2,384]{1,0:T(2,128)}, u32[]{:S(2)}) copy-start(f32[2,384]{1,0:T(2,128)} %param.34) | copy-start | bytes 9220
  38.0 19.1 %copy-start = (bf16[2,384,384]{2,1,0:T(8,128)(2,1)S(1)}, bf16[2,384,384]{2,1,0:T(8,128)(2,1)}, u32[]{:S(2)}) copy-start(bf16[2,384,384]{2,1,0:T(8,128)(2,1)} %up_ref.1) | copy-start | bytes 1769476
  38.0 19.1 %copy-start.1 = (bf16[2,384,384]{2,1,0:T(8,128)(2,1)S(1)}, bf16[2,384,384]{2,1,0:T(8,128)(2,1)}, u32[]{:S(2)}) copy-start(bf16[2,384,384]{2,1,0:T(8,128)(2,1)} %down_ref.1) | copy-start | bytes 1769476
  38.0 19.1 %copy-start.4 = (bf16[2,384]{1,0:T(2,128)(2,1)S(1)}, bf16[2,384]{1,0:T(2,128)(2,1)}, u32[]{:S(2)}) copy-start(bf16[2,384]{1,0:T(2,128)(2,1)} %up_bias_ref.1) | copy-start | bytes 4612
  43.0 27.6 %copy-start.2 = (bf16[16,384]{1,0:T(8,128)(2,1)S(1)}, bf16[16,384]{1,0:T(8,128)(2,1)}, u32[]{:S(2)}) copy-start(bf16[16,384]{1,0:T(8,128)(2,1)} %reshape.48.phi_ref) | copy-start | bytes 36868
  43.0 27.6 %copy-start.3 = (s32[2,1024]{1,0:T(2,128)S(1)}, s32[2,1024]{1,0:T(2,128)}, u32[]{:S(2)}) copy-start(s32[2,1024]{1,0:T(2,128)} %ids_ref.5) | copy-start | bytes 24580
  43.1 27.6 %copy-start.8 = (bf16[384,384]{1,0:T(8,128)(2,1)S(1)}, bf16[384,384]{1,0:T(8,128)(2,1)}, u32[]{:S(2)}) copy-start(bf16[384,384]{1,0:T(8,128)(2,1)} %out_w_ref.3) | copy-start | bytes 884740
  43.1 27.6 %copy-start.9 = (f32[384]{0:T(512)S(1)}, f32[384]{0:T(512)}, u32[]{:S(2)}) copy-start(f32[384]{0:T(512)} %gain2_ref.3) | copy-start | bytes 4612
  43.1 27.6 %copy-start.13 = (f32[2,8,384]{2,1,0:T(8,128)S(1)}, f32[2,8,384]{2,1,0:T(8,128)}, u32[]{:S(2)}) copy-start(f32[2,8,384]{2,1,0:T(8,128)} %get-tuple-element.72.sums_ref) | copy-start | bytes 73732
  43.1 14.1 %all-to-all-start.1 = ((bf16[32,8,384]{2,1,0:T(8,128)(2,1)}), bf16[32,8,384]{2,1,0:T(8,128)(2,1)S(1)}, u32[]{:S(2)}, u32[]{:S(2)}) async-start(bf16[32,8,384]{2,1,0:T(8,128)(2,1)} %bitcast.8), calls=%async_computation.1 | async-start | bytes 393216 | tf_op jit(solution)/shard_map/all_to_all | solution.py:1093
  59.0 11.6 %all-to-all-start.2 = ((bf16[32,8,384]{2,1,0:T(8,128)(2,1)}), bf16[32,8,384]{2,1,0:T(8,128)(2,1)S(1)}, u32[]{:S(2)}, u32[]{:S(2)}) async-start(bf16[32,8,384]{2,1,0:T(8,128)(2,1)} %get-tuple-element.63), calls=%async_computation.2 | async-start | bytes 393216 | tf_op jit(solution)/shard_map/all_to_all | solution.py:1093
  113.7 2.2 %collective-permute-start = (bf16[16,160,128]{2,1,0:T(8,128)(2,1)S(1)}, bf16[16,160,128]{2,1,0:T(8,128)(2,1)S(1)}, u32[]{:S(2)}, u32[]{:S(2)}) collective-permute-start(bf16[16,160,128]{2,1,0:T(8,128)(2,1)S(1)} %get-tuple-element.84), channel_id=1, source_target_pairs={{0,8},{8,0},{1,9},{9,1},{2,10},{10,2},{3,11},{11,3},{4,12},{12,4},... | collective-permute-start | bytes 1966088 | tf_op jit(solution)/shard_map/ppermute | solution.py:1120
  115.8 6.2 %copy-start.5 = (bf16[2,1024,384]{2,1,0:T(8,128)(2,1)S(1)}, bf16[2,1024,384]{2,1,0:T(8,128)(2,1)}, u32[]{:S(2)}) copy-start(bf16[2,1024,384]{2,1,0:T(8,128)(2,1)} %refs_0_.1) | copy-start | bytes 4718596
  115.8 6.2 %copy-start.6 = (f32[2,1024,128]{2,1,0:T(8,128)S(1)}, f32[2,1024,128]{2,1,0:T(8,128)}, u32[]{:S(2)}) copy-start(f32[2,1024,128]{2,1,0:T(8,128)} %get-tuple-element.61.weights_ref.refs_6_) | copy-start | bytes 3145732
  115.8 6.2 %copy-start.10 = (f32[384]{0:T(512)S(1)}, f32[384]{0:T(512)}, u32[]{:S(2)}) copy-start(f32[384]{0:T(512)} %refs_3_.1) | copy-start | bytes 4612
  116.8 23.3 %all-to-all-start.3 = ((bf16[16,160,128]{2,1,0:T(8,128)(2,1)}), bf16[16,160,128]{2,1,0:T(8,128)(2,1)S(1)}, u32[]{:S(2)}, u32[]{:S(2)}) async-start(bf16[16,160,128]{2,1,0:T(8,128)(2,1)} %add.3), calls=%async_computation.3 | async-start | bytes 1310720 | tf_op jit(solution)/shard_map/all_to_all | solution.py:1093
  122.0 1.2 copy-start.7
  123.2 1.9 %copy-start.11 = (f32[2,1024,384]{2,1,0:T(8,128)S(1)}, f32[2,1024,384]{2,1,0:T(8,128)}, u32[]{:S(2)}) copy-start(f32[2,1024,384]{2,1,0:T(8,128)} %get-tuple-element.59.residual_ref.refs_5_) | copy-start | bytes 9437188
  125.1 1.9 %copy-start.12 = (f32[2,1024,384]{2,1,0:T(8,128)S(1)}, f32[2,1024,384]{2,1,0:T(8,128)}, u32[]{:S(2)}) copy-start(f32[2,1024,384]{2,1,0:T(8,128)} %get-tuple-element.80.refs_2_) | copy-start | bytes 9437188
  162.3 2.1 %collective-permute-start.1 = (bf16[16,160,128]{2,1,0:T(8,128)(2,1)S(1)}, bf16[16,160,128]{2,1,0:T(8,128)(2,1)S(1)}, u32[]{:S(2)}, u32[]{:S(2)}) collective-permute-start(bf16[16,160,128]{2,1,0:T(8,128)(2,1)S(1)} %all_to_all.25.refs_1_), channel_id=1, source_target_pairs={{0,8},{8,0},{1,9},{9,1},{2,10},{10,2},{3,11},{11,3},{4,12},{12,4},... | collective-permute-start | bytes 1966088 | tf_op jit(solution)/shard_map/ppermute | solution.py:1126
